TPU v7x, 512 devices: a whole 4x8x8 slice. The times are simulated.
512 devices in a mesh: gx: 32 (over x_lo, z, core), gy: 16 (over y, x_hi).
Axes of the slice: x: 4 (x_hi: 2, x_lo: 2; x = x_hi * 2 + x_lo), y: 8, z: 8, core: 2. Of those that a mesh axis runs over, the one named last changes fastest.
Arguments:
- concentration: float32 [3, 512, 256, 128], P(None, 'gx', 'gy'), may hold values from 0.2 to 2
- potential: float32 [512, 256, 128], P('gx', 'gy'), may hold values from -3 to 3
- permittivity: float32 [512, 256, 128], P('gx', 'gy'), may hold values from 0.5 to 4
- records: float32 [65536, 4, 128], P(('gx', 'gy')), may hold values from -3 to 3
- colloid_count: int32 [512], P(('gx', 'gy')), may hold values from 64 to 128, as said below
- move_slots: int32 [512, 4, 16], P(('gx', 'gy')), may hold values from 0 to 127, as said below
- move_count: int32 [512, 4], P(('gx', 'gy')), may hold values from 8 to 16, as said below
- own_nodes: int32 [65536, 128], P(('gx', 'gy')), may hold values from 0 to 41471, as said below
- arrive_nodes: int32 [512, 4, 16, 128], P(('gx', 'gy')), may hold values from 0 to 41471, as said below
Outputs:
- concentration_next: float32 [3, 512, 256, 128], P(None, 'gx', 'gy')
- potential_next: float32 [512, 256, 128], P('gx', 'gy')
- body_force: float32 [3, 512, 256, 128], P(None, 'gx', 'gy')
Inputs may be any that keep to these rules, and one draw needn't show every extreme that they name: `colloid_count`: every brick has at least 64 live slots; some brick has all 128. `move_slots`: the slots of one brick named across all four directions are distinct and below that brick's colloid_count; entries at k >= move_count are ignored. `move_count`: in every direction some brick sends exactly 16. `own_nodes`: index ((x+1)(18) + (y+1)) * 128 + z of a cell of the brick extended by one cell on each side of its first two dimensions, x from -1 to 16 and y from -1 to 16. `arrive_nodes`: same form as own_nodes, for the receiving brick.
All inputs are finite; a program needn't handle non-finite values.
Results may differ from a plain program's by a relative error of at most 0.00002.
Values sent between devices are 32-bit elements; how exact they have to be, the bound alone decides.
No kernel may reach another device: no remote copies, remote signals or barrier semaphores. Data moves between devices by JAX's collectives and lax.ppermute only.
A program may use at most 128 MiB of HBM per device.

v0:
```python
import jax
import jax.numpy as jnp
from jax import lax
from jax.sharding import PartitionSpec as P

SWEEPS = 8


diffusion = (1.0, 0.7, 0.45)
valence = (1.0, -1.0, 2.0)
time_step = 0.05
screening = 0.05


def with_halo(cells, sides, width):
    for axis, dim in sides:
        count = lax.axis_size(axis)
        head = lax.slice_in_dim(cells, 0, width, axis=dim)
        tail = lax.slice_in_dim(cells, cells.shape[dim] - width, cells.shape[dim], axis=dim)
        cells = jnp.concatenate(
            [
                lax.ppermute(tail, axis, [(i, (i + 1) % count) for i in range(count)]),
                cells,
                lax.ppermute(head, axis, [((i + 1) % count, i) for i in range(count)]),
            ],
            axis=dim,
        )
    return cells


def passed_along(block, axis, distance):
    devices = range(lax.axis_size(axis))
    route = [((i - distance) % len(devices), i) for i in devices]
    return lax.ppermute(block, axis, route)


def species_table(numbers):
    return jnp.array(numbers, dtype=jnp.float32).reshape(3, 1, 1, 1)


def face_flux(upper, lower, upper_pot, lower_pot):
    return -species_table(diffusion) * (
        upper - lower + species_table(valence) * 0.5 * (upper + lower) * (upper_pot - lower_pot)
    )


def jacobi_sweep(phi_wide, eps_wide, density):
    centre_eps = eps_wide[1:-1, 1:-1]
    centre_phi = phi_wide[1:-1, 1:-1]
    x_up = 0.5 * (centre_eps + eps_wide[2:, 1:-1])
    x_down = 0.5 * (centre_eps + eps_wide[:-2, 1:-1])
    y_up = 0.5 * (centre_eps + eps_wide[1:-1, 2:])
    y_down = 0.5 * (centre_eps + eps_wide[1:-1, :-2])
    z_up = 0.5 * (centre_eps + jnp.roll(centre_eps, -1, 2))
    z_down = 0.5 * (centre_eps + jnp.roll(centre_eps, 1, 2))
    numer = (
        x_up * phi_wide[2:, 1:-1]
        + x_down * phi_wide[:-2, 1:-1]
        + y_up * phi_wide[1:-1, 2:]
        + y_down * phi_wide[1:-1, :-2]
        + z_up * jnp.roll(centre_phi, -1, 2)
        + z_down * jnp.roll(centre_phi, 1, 2)
        + density
    )
    denom = x_up + x_down + y_up + y_down + z_up + z_down + screening
    return numer / denom


def body(
    concentration,
    potential,
    permittivity,
    records,
    colloid_count,
    move_slots,
    move_count,
    own_nodes,
    arrive_nodes,
):
    brick_x, brick_y, depth = potential.shape
    channels = records.shape[1]
    nodes = records.shape[2]
    mover_slots = move_slots[0]
    mover_counts = move_count[0]
    movers = mover_slots.shape[1]
    slot_ids = jnp.arange(records.shape[0], dtype=jnp.int32)
    slot_valid = jnp.arange(movers, dtype=jnp.int32)[None, :] < mover_counts[:, None]
    leaving = jnp.any((mover_slots[..., None] == slot_ids) & slot_valid[..., None], axis=(0, 1))
    staying = (slot_ids < colloid_count[0]) & jnp.logical_not(leaving)
    kept_rows = jnp.where(staying[:, None, None], records, 0.0)
    picked_rows = records[mover_slots.reshape(-1)].reshape(4, movers, channels, nodes)
    outgoing = jnp.where(slot_valid[..., None, None], picked_rows, 0.0)
    fields = jnp.concatenate([concentration, potential[None], permittivity[None]], axis=0)
    widened = with_halo(fields, (("gx", 1), ("gy", 2)), 1)
    from_low_x = passed_along(outgoing[0], "gx", 1)
    from_high_x = passed_along(outgoing[1], "gx", -1)
    from_low_y = passed_along(outgoing[2], "gy", 1)
    from_high_y = passed_along(outgoing[3], "gy", -1)
    conc_wide = widened[:3]
    pot_wide = widened[3]
    conc_x = conc_wide[:, :, 1:-1]
    pot_x = pot_wide[:, 1:-1]
    flux_x = face_flux(conc_x[:, 1:], conc_x[:, :-1], pot_x[1:], pot_x[:-1])
    div_x = flux_x[:, 1:] - flux_x[:, :-1]
    conc_y = conc_wide[:, 1:-1]
    pot_y = pot_wide[1:-1]
    flux_y = face_flux(conc_y[:, :, 1:], conc_y[:, :, :-1], pot_y[:, 1:], pot_y[:, :-1])
    div_y = flux_y[:, :, 1:] - flux_y[:, :, :-1]
    flux_z = face_flux(
        jnp.roll(concentration, -1, 3), concentration, jnp.roll(potential, -1, 2), potential
    )
    div_z = flux_z - jnp.roll(flux_z, 1, 3)
    concentration_next = concentration - time_step * (div_x + div_y + div_z)
    arrived_rows = jnp.stack([from_low_x, from_high_x, from_low_y, from_high_y]).reshape(
        4 * movers, channels, nodes
    )
    all_rows = jnp.concatenate([kept_rows, arrived_rows], axis=0)
    all_cells = jnp.concatenate([own_nodes, arrive_nodes[0].reshape(4 * movers, nodes)], axis=0)
    spread_grid = jnp.zeros((channels, (brick_x + 2) * (brick_y + 2) * depth), jnp.float32)
    spread_grid = spread_grid.at[:, all_cells.reshape(-1)].add(
        jnp.moveaxis(all_rows, 1, 0).reshape(channels, -1)
    )
    spread_grid = spread_grid.reshape(channels, brick_x + 2, brick_y + 2, depth)
    rims_x = jnp.stack([spread_grid[:, 0], spread_grid[:, brick_x + 1]], axis=1)
    landed_x = with_halo(rims_x, (("gx", 1),), 1)
    inner_rows = spread_grid[:, 1 : brick_x + 1]
    inner_rows = inner_rows.at[:, 0].add(landed_x[:, 0]).at[:, brick_x - 1].add(landed_x[:, 3])
    rims_y = jnp.stack([inner_rows[:, :, 0], inner_rows[:, :, brick_y + 1]], axis=2)
    landed_y = with_halo(rims_y, (("gy", 2),), 1)
    core_grid = inner_rows[:, :, 1 : brick_y + 1]
    core_grid = (
        core_grid.at[:, :, 0].add(landed_y[:, :, 0]).at[:, :, brick_y - 1].add(landed_y[:, :, 3])
    )
    colloid_charge = core_grid[0]
    body_force = core_grid[1:]
    charge_density = jnp.sum(species_table(valence) * concentration_next, axis=0) + colloid_charge
    eps_wide = widened[4]
    potential_now = jacobi_sweep(pot_wide, eps_wide, charge_density)
    for sweep_index in range(SWEEPS - 1):
        phi_wide = with_halo(potential_now, (("gx", 0), ("gy", 1)), 1)
        potential_now = jacobi_sweep(phi_wide, eps_wide, charge_density)
    return (concentration_next, potential_now, body_force)


def solution(mesh):
    placed = (
        P(None, "gx", "gy", None),
        P("gx", "gy", None),
        P("gx", "gy", None),
        P(("gx", "gy"), None, None),
        P(("gx", "gy")),
        P(("gx", "gy"), None, None),
        P(("gx", "gy"), None),
        P(("gx", "gy"), None),
        P(("gx", "gy"), None, None, None),
    )
    return jax.shard_map(
        body,
        mesh=mesh,
        in_specs=placed,
        out_specs=(P(None, "gx", "gy", None), P("gx", "gy", None), P(None, "gx", "gy", None)),
        check_vma=False,
    )
```

profile of v0, /device:TPU:1, one launch (start us, length us, event | category | flops | bytes accessed | tf_op | source)
XLA Modules:
  0.0 401.7 jit_solution(18356931266563191222)
XLA Ops:
  3.9 5.4 %collective-permute-start.4 = (f32[16,4,128]{2,1,0:T(4,128)S(1)}, f32[16,4,128]{2,1,0:T(4,128)S(1)}, u32[]{:S(2)}, u32[]{:S(2)}) collective-permute-start(f32[16,4,128]{2,1,0:T(4,128)S(1)} %get-tuple-element.136), channel_id=1, source_target_pairs={{496,0},{0,16},{16,32},{32,48},{48,64},{64,80},{80,96},{96,112},{1... | collective-permute-start | bytes 98312 | tf_op jit(solution)/shard_map/ppermute | solution.py:34
  9.3 5.3 %collective-permute-start.5 = (f32[16,4,128]{2,1,0:T(4,128)S(1)}, f32[16,4,128]{2,1,0:T(4,128)S(1)}, u32[]{:S(2)}, u32[]{:S(2)}) collective-permute-start(f32[16,4,128]{2,1,0:T(4,128)S(1)} %get-tuple-element.139), channel_id=1, source_target_pairs={{16,0},{32,16},{48,32},{64,48},{80,64},{96,80},{112,96},{128,112},... | collective-permute-start | bytes 98312 | tf_op jit(solution)/shard_map/ppermute | solution.py:34
  14.6 1.9 collective-permute-start.6
  16.6 7.0 %collective-permute-start.7 = (f32[16,4,128]{2,1,0:T(4,128)S(1)}, f32[16,4,128]{2,1,0:T(4,128)S(1)}, u32[]{:S(2)}, u32[]{:S(2)}) collective-permute-start(f32[16,4,128]{2,1,0:T(4,128)S(1)} %get-tuple-element.137), channel_id=1, source_target_pairs={{1,0},{2,1},{3,2},{4,3},{5,4},{6,5},{7,6},{8,7},{9,8},{10,9},{11,1... | collective-permute-start | bytes 98312 | tf_op jit(solution)/shard_map/ppermute | solution.py:34
  25.0 6.5 %collective-permute-start = (f32[5,1,16,128]{3,2,1,0:T(8,128)}, f32[5,1,16,128]{3,2,1,0:T(8,128)S(1)}, u32[]{:S(2)}, u32[]{:S(2)}) collective-permute-start(f32[5,1,16,128]{3,2,1,0:T(8,128)} %get-tuple-element.71), channel_id=1, source_target_pairs={{16,0},{32,16},{48,32},{64,48},{80,64},{96,80},{112,96},{128,112},... | collective-permute-start | bytes 122888 | tf_op jit(solution)/shard_map/ppermute | solution.py:24
  42.8 7.0 %copy.28 = f32[24576,4]{1,0:T(8,128)} copy(f32[24576,4]{0,1:T(4,128)S(1)} %maximum_bitcast_fusion) | data formatting | bytes 786432 | tf_op jit(solution)/shard_map/reshape | solution.py:121
  49.8 139.4 %scatter_custom_fusion = f32[4,41472]{0,1:T(8,128)} fusion(s32[24576]{0:T(1024)S(1)} %bitcast.66, f32[24576,4]{1,0:T(8,128)} %copy.28, f32[]{:T(128)} %constant.121.clone.1), kind=kCustom, calls=%fused_computation.2 | custom fusion | flops 98304 | bytes 664064 | tf_op jit(solution)/shard_map/scatter-add | solution.py:120
  189.2 3.4 fusion.110
  192.6 12.8 %slice.830 = f32[4,16,18,128]{0,3,2,1:T(8,128)} slice(f32[4,18,18,128]{0,3,2,1:T(8,128)} %bitcast.47), slice={[0:4], [1:17], [0:18], [0:128]} | slice | bytes 1179648 | tf_op jit(solution)/shard_map/slice | solution.py:126
  205.3 2.4 copy.35
  210.2 11.8 %copy.33 = f32[4,16,18,128]{3,2,1,0:T(8,128)S(1)} copy(f32[4,16,18,128]{0,3,2,1:T(8,128)} %slice.830) | data formatting | bytes 1179648
  222.4 2.4 collective-permute-start.9
  225.0 2.2 collective-permute-start.2
  227.2 6.7 %collective-permute-start.3 = (f32[5,18,1,128]{3,2,1,0:T(1,128)S(1)}, f32[5,18,1,128]{3,2,1,0:T(1,128)S(1)}, u32[]{:S(2)}, u32[]{:S(2)}) collective-permute-start(f32[5,18,1,128]{3,2,1,0:T(1,128)S(1)} %get-tuple-element.69), channel_id=1, source_target_pairs={{1,0},{2,1},{3,2},{4,3},{5,4},{6,5},{7,6},{8,7},{9,8},{10,9},{11,1... | collective-permute-start | bytes 138248 | tf_op jit(solution)/shard_map/ppermute | solution.py:24
  237.6 7.0 %collective-permute-start.11 = (f32[4,16,1,128]{3,2,1,0:T(1,128)S(1)}, f32[4,16,1,128]{3,2,1,0:T(1,128)S(1)}, u32[]{:S(2)}, u32[]{:S(2)}) collective-permute-start(f32[4,16,1,128]{3,2,1,0:T(1,128)S(1)} %get-tuple-element.66), channel_id=1, source_target_pairs={{1,0},{2,1},{3,2},{4,3},{5,4},{6,5},{7,6},{8,7},{9,8},{10,9},{11,1... | collective-permute-start | bytes 98312 | tf_op jit(solution)/shard_map/ppermute | solution.py:24
  246.0 2.0 multiply_reduce_fusion
  254.2 6.9 %collective-permute-start.12 = (f32[1,16,128]{2,1,0:T(8,128)S(1)}, f32[1,16,128]{2,1,0:T(8,128)S(1)}, u32[]{:S(2)}, u32[]{:S(2)}) collective-permute-start(f32[1,16,128]{2,1,0:T(8,128)S(1)} %get-tuple-element.135), channel_id=1, source_target_pairs={{16,0},{32,16},{48,32},{64,48},{80,64},{96,80},{112,96},{128,112},... | collective-permute-start | bytes 24584 | tf_op jit(solution)/shard_map/ppermute | solution.py:24
  261.1 1.9 collective-permute-start.13
  264.2 3.7 collective-permute-start.14
  267.9 3.1 collective-permute-start.15
  272.9 3.1 collective-permute-done.15
  276.2 7.4 %collective-permute-start.16 = (f32[1,16,128]{2,1,0:T(8,128)S(1)}, f32[1,16,128]{2,1,0:T(8,128)S(1)}, u32[]{:S(2)}, u32[]{:S(2)}) collective-permute-start(f32[1,16,128]{2,1,0:T(8,128)S(1)} %get-tuple-element.129), channel_id=1, source_target_pairs={{16,0},{32,16},{48,32},{64,48},{80,64},{96,80},{112,96},{128,112},... | collective-permute-start | bytes 24584 | tf_op jit(solution)/shard_map/ppermute | solution.py:24
  283.5 1.9 collective-permute-start.17
  286.6 1.9 collective-permute-start.18
  288.5 4.9 %collective-permute-start.19 = (f32[18,1,128]{2,1,0:T(1,128)S(1)}, f32[18,1,128]{2,1,0:T(1,128)S(1)}, u32[]{:S(2)}, u32[]{:S(2)}) collective-permute-start(f32[18,1,128]{2,1,0:T(1,128)S(1)} %get-tuple-element.91), channel_id=1, source_target_pairs={{0,1},{1,2},{2,3},{3,4},{4,5},{5,6},{6,7},{7,8},{8,9},{9,10},{10,1... | collective-permute-start | bytes 27656 | tf_op jit(solution)/shard_map/ppermute | solution.py:22
  293.5 3.0 collective-permute-done.19
  296.7 7.3 %collective-permute-start.20 = (f32[1,16,128]{2,1,0:T(8,128)S(1)}, f32[1,16,128]{2,1,0:T(8,128)S(1)}, u32[]{:S(2)}, u32[]{:S(2)}) collective-permute-start(f32[1,16,128]{2,1,0:T(8,128)S(1)} %get-tuple-element.123), channel_id=1, source_target_pairs={{16,0},{32,16},{48,32},{64,48},{80,64},{96,80},{112,96},{128,112},... | collective-permute-start | bytes 24584 | tf_op jit(solution)/shard_map/ppermute | solution.py:24
  304.1 1.9 collective-permute-start.21
  307.2 1.9 collective-permute-start.22
  309.1 4.9 %collective-permute-start.23 = (f32[18,1,128]{2,1,0:T(1,128)S(1)}, f32[18,1,128]{2,1,0:T(1,128)S(1)}, u32[]{:S(2)}, u32[]{:S(2)}) collective-permute-start(f32[18,1,128]{2,1,0:T(1,128)S(1)} %get-tuple-element.89), channel_id=1, source_target_pairs={{0,1},{1,2},{2,3},{3,4},{4,5},{5,6},{6,7},{7,8},{8,9},{9,10},{10,1... | collective-permute-start | bytes 27656 | tf_op jit(solution)/shard_map/ppermute | solution.py:22
  314.1 3.0 collective-permute-done.23
  317.3 7.1 %collective-permute-start.24 = (f32[1,16,128]{2,1,0:T(8,128)S(1)}, f32[1,16,128]{2,1,0:T(8,128)S(1)}, u32[]{:S(2)}, u32[]{:S(2)}) collective-permute-start(f32[1,16,128]{2,1,0:T(8,128)S(1)} %get-tuple-element.117), channel_id=1, source_target_pairs={{16,0},{32,16},{48,32},{64,48},{80,64},{96,80},{112,96},{128,112},... | collective-permute-start | bytes 24584 | tf_op jit(solution)/shard_map/ppermute | solution.py:24
  324.4 1.9 collective-permute-start.25
  329.4 4.9 %collective-permute-start.27 = (f32[18,1,128]{2,1,0:T(1,128)S(1)}, f32[18,1,128]{2,1,0:T(1,128)S(1)}, u32[]{:S(2)}, u32[]{:S(2)}) collective-permute-start(f32[18,1,128]{2,1,0:T(1,128)S(1)} %get-tuple-element.87), channel_id=1, source_target_pairs={{0,1},{1,2},{2,3},{3,4},{4,5},{5,6},{6,7},{7,8},{8,9},{9,10},{10,1... | collective-permute-start | bytes 27656 | tf_op jit(solution)/shard_map/ppermute | solution.py:22
  334.4 3.0 collective-permute-done.27
  337.6 7.1 %collective-permute-start.28 = (f32[1,16,128]{2,1,0:T(8,128)S(1)}, f32[1,16,128]{2,1,0:T(8,128)S(1)}, u32[]{:S(2)}, u32[]{:S(2)}) collective-permute-start(f32[1,16,128]{2,1,0:T(8,128)S(1)} %get-tuple-element.111), channel_id=1, source_target_pairs={{16,0},{32,16},{48,32},{64,48},{80,64},{96,80},{112,96},{128,112},... | collective-permute-start | bytes 24584 | tf_op jit(solution)/shard_map/ppermute | solution.py:24
  347.8 1.9 collective-permute-start.30
  349.7 4.9 %collective-permute-start.31 = (f32[18,1,128]{2,1,0:T(1,128)S(1)}, f32[18,1,128]{2,1,0:T(1,128)S(1)}, u32[]{:S(2)}, u32[]{:S(2)}) collective-permute-start(f32[18,1,128]{2,1,0:T(1,128)S(1)} %get-tuple-element.85), channel_id=1, source_target_pairs={{0,1},{1,2},{2,3},{3,4},{4,5},{5,6},{6,7},{7,8},{8,9},{9,10},{10,1... | collective-permute-start | bytes 27656 | tf_op jit(solution)/shard_map/ppermute | solution.py:22
  354.7 3.0 collective-permute-done.31
  357.9 7.1 %collective-permute-start.32 = (f32[1,16,128]{2,1,0:T(8,128)S(1)}, f32[1,16,128]{2,1,0:T(8,128)S(1)}, u32[]{:S(2)}, u32[]{:S(2)}) collective-permute-start(f32[1,16,128]{2,1,0:T(8,128)S(1)} %get-tuple-element.105), channel_id=1, source_target_pairs={{16,0},{32,16},{48,32},{64,48},{80,64},{96,80},{112,96},{128,112},... | collective-permute-start | bytes 24584 | tf_op jit(solution)/shard_map/ppermute | solution.py:24
  365.0 1.9 collective-permute-start.33
  368.1 2.1 collective-permute-start.34
  370.2 4.7 %collective-permute-start.35 = (f32[18,1,128]{2,1,0:T(1,128)S(1)}, f32[18,1,128]{2,1,0:T(1,128)S(1)}, u32[]{:S(2)}, u32[]{:S(2)}) collective-permute-start(f32[18,1,128]{2,1,0:T(1,128)S(1)} %get-tuple-element.83), channel_id=1, source_target_pairs={{0,1},{1,2},{2,3},{3,4},{4,5},{5,6},{6,7},{7,8},{8,9},{9,10},{10,1... | collective-permute-start | bytes 27656 | tf_op jit(solution)/shard_map/ppermute | solution.py:22
  375.0 3.2 collective-permute-done.35
  378.4 7.4 %collective-permute-start.36 = (f32[1,16,128]{2,1,0:T(8,128)S(1)}, f32[1,16,128]{2,1,0:T(8,128)S(1)}, u32[]{:S(2)}, u32[]{:S(2)}) collective-permute-start(f32[1,16,128]{2,1,0:T(8,128)S(1)} %get-tuple-element.99), channel_id=1, source_target_pairs={{16,0},{32,16},{48,32},{64,48},{80,64},{96,80},{112,96},{128,112},... | collective-permute-start | bytes 24584 | tf_op jit(solution)/shard_map/ppermute | solution.py:24
  388.9 3.9 collective-permute-start.38
  392.8 2.9 collective-permute-start.39
  395.8 5.1 %collective-permute-done.39 = f32[18,1,128]{2,1,0:T(1,128)S(1)} collective-permute-done((f32[18,1,128]{2,1,0:T(1,128)S(1)}, f32[18,1,128]{2,1,0:T(1,128)S(1)}, u32[]{:S(2)}, u32[]{:S(2)}) %collective-permute-start.39) | collective-permute-done | bytes 9248 | tf_op jit(solution)/shard_map/ppermute | solution.py:22
  (125 shorter events, 47.4 us)
Async XLA Ops:
  3.9 36.8 %collective-permute-start.4 = (f32[16,4,128]{2,1,0:T(4,128)S(1)}, f32[16,4,128]{2,1,0:T(4,128)S(1)}, u32[]{:S(2)}, u32[]{:S(2)}) collective-permute-start(f32[16,4,128]{2,1,0:T(4,128)S(1)} %get-tuple-element.136), channel_id=1, source_target_pairs={{496,0},{0,16},{16,32},{32,48},{48,64},{64,80},{80,96},{96,112},{1... | collective-permute-start | bytes 98312 | tf_op jit(solution)/shard_map/ppermute | solution.py:34
  9.3 33.3 %collective-permute-start.5 = (f32[16,4,128]{2,1,0:T(4,128)S(1)}, f32[16,4,128]{2,1,0:T(4,128)S(1)}, u32[]{:S(2)}, u32[]{:S(2)}) collective-permute-start(f32[16,4,128]{2,1,0:T(4,128)S(1)} %get-tuple-element.139), channel_id=1, source_target_pairs={{16,0},{32,16},{48,32},{64,48},{80,64},{96,80},{112,96},{128,112},... | collective-permute-start | bytes 98312 | tf_op jit(solution)/shard_map/ppermute | solution.py:34
  14.6 28.0 %collective-permute-start.6 = (f32[16,4,128]{2,1,0:T(4,128)S(1)}, f32[16,4,128]{2,1,0:T(4,128)S(1)}, u32[]{:S(2)}, u32[]{:S(2)}) collective-permute-start(f32[16,4,128]{2,1,0:T(4,128)S(1)} %get-tuple-element.138), channel_id=1, source_target_pairs={{15,0},{0,1},{1,2},{2,3},{3,4},{4,5},{5,6},{6,7},{7,8},{8,9},{9,10... | collective-permute-start | bytes 98312 | tf_op jit(solution)/shard_map/ppermute | solution.py:34
  16.6 26.1 %collective-permute-start.7 = (f32[16,4,128]{2,1,0:T(4,128)S(1)}, f32[16,4,128]{2,1,0:T(4,128)S(1)}, u32[]{:S(2)}, u32[]{:S(2)}) collective-permute-start(f32[16,4,128]{2,1,0:T(4,128)S(1)} %get-tuple-element.137), channel_id=1, source_target_pairs={{1,0},{2,1},{3,2},{4,3},{5,4},{6,5},{7,6},{8,7},{9,8},{10,9},{11,1... | collective-permute-start | bytes 98312 | tf_op jit(solution)/shard_map/ppermute | solution.py:34
  25.0 199.9 %collective-permute-start = (f32[5,1,16,128]{3,2,1,0:T(8,128)}, f32[5,1,16,128]{3,2,1,0:T(8,128)S(1)}, u32[]{:S(2)}, u32[]{:S(2)}) collective-permute-start(f32[5,1,16,128]{3,2,1,0:T(8,128)} %get-tuple-element.71), channel_id=1, source_target_pairs={{16,0},{32,16},{48,32},{64,48},{80,64},{96,80},{112,96},{128,112},... | collective-permute-start | bytes 122888 | tf_op jit(solution)/shard_map/ppermute | solution.py:24
  40.7 184.2 %collective-permute-start.1 = (f32[5,1,16,128]{3,2,1,0:T(8,128)}, f32[5,1,16,128]{3,2,1,0:T(8,128)S(1)}, u32[]{:S(2)}, u32[]{:S(2)}) collective-permute-start(f32[5,1,16,128]{3,2,1,0:T(8,128)} %get-tuple-element.70), channel_id=1, source_target_pairs={{0,16},{16,32},{32,48},{48,64},{64,80},{80,96},{96,112},{112,128},... | collective-permute-start | bytes 122888 | tf_op jit(solution)/shard_map/ppermute | solution.py:22
  205.3 19.5 %copy-start = (f32[3,16,16,128]{3,2,1,0:T(8,128)S(1)}, f32[3,16,16,128]{3,2,1,0:T(8,128)}, u32[]{:S(2)}) copy-start(f32[3,16,16,128]{3,2,1,0:T(8,128)} %param.24) | copy-start | bytes 1179652
  205.3 19.5 %copy-start.1 = (f32[16,16,128]{2,1,0:T(8,128)S(1)}, f32[16,16,128]{2,1,0:T(8,128)}, u32[]{:S(2)}) copy-start(f32[16,16,128]{2,1,0:T(8,128)} %param.25) | copy-start | bytes 393220
  205.3 19.6 %copy-start.2 = (f32[16,16,128]{2,1,0:T(8,128)S(1)}, f32[16,16,128]{2,1,0:T(8,128)}, u32[]{:S(2)}) copy-start(f32[16,16,128]{2,1,0:T(8,128)} %param.26) | copy-start | bytes 393220
  207.8 26.1 %collective-permute-start.8 = (f32[4,1,18,128]{3,2,1,0:T(8,128)}, f32[4,1,18,128]{3,2,1,0:T(8,128)}, u32[]{:S(2)}, u32[]{:S(2)}) collective-permute-start(f32[4,1,18,128]{3,2,1,0:T(8,128)} %copy.35), channel_id=1, source_target_pairs={{0,16},{16,32},{32,48},{48,64},{64,80},{80,96},{96,112},{112,128},... | collective-permute-start | bytes 110600 | tf_op jit(solution)/shard_map/ppermute | solution.py:22
  210.2 35.4 %copy-start.3 = (f32[3]{0:T(128)S(1)}, f32[3]{0:T(128)}, u32[]{:S(2)}) copy-start(f32[3]{0:T(128)} %constant.138) | copy-start | bytes 40
  210.2 35.4 %copy-start.4 = (f32[3]{0:T(128)S(1)}, f32[3]{0:T(128)}, u32[]{:S(2)}) copy-start(f32[3]{0:T(128)} %constant.139) | copy-start | bytes 40
  222.4 12.3 %collective-permute-start.9 = (f32[4,1,18,128]{3,2,1,0:T(8,128)S(1)}, f32[4,1,18,128]{3,2,1,0:T(8,128)S(1)}, u32[]{:S(2)}, u32[]{:S(2)}) collective-permute-start(f32[4,1,18,128]{3,2,1,0:T(8,128)S(1)} %copy.36), channel_id=1, source_target_pairs={{16,0},{32,16},{48,32},{64,48},{80,64},{96,80},{112,96},{128,112},... | collective-permute-start | bytes 110600 | tf_op jit(solution)/shard_map/ppermute | solution.py:24
  225.0 19.6 %collective-permute-start.2 = (f32[5,18,1,128]{3,2,1,0:T(1,128)S(1)}, f32[5,18,1,128]{3,2,1,0:T(1,128)S(1)}, u32[]{:S(2)}, u32[]{:S(2)}) collective-permute-start(f32[5,18,1,128]{3,2,1,0:T(1,128)S(1)} %get-tuple-element.68), channel_id=1, source_target_pairs={{0,1},{1,2},{2,3},{3,4},{4,5},{5,6},{6,7},{7,8},{8,9},{9,10},{10,1... | collective-permute-start | bytes 138248 | tf_op jit(solution)/shard_map/ppermute | solution.py:22
  227.2 17.4 %collective-permute-start.3 = (f32[5,18,1,128]{3,2,1,0:T(1,128)S(1)}, f32[5,18,1,128]{3,2,1,0:T(1,128)S(1)}, u32[]{:S(2)}, u32[]{:S(2)}) collective-permute-start(f32[5,18,1,128]{3,2,1,0:T(1,128)S(1)} %get-tuple-element.69), channel_id=1, source_target_pairs={{1,0},{2,1},{3,2},{4,3},{5,4},{6,5},{7,6},{8,7},{9,8},{10,9},{11,1... | collective-permute-start | bytes 138248 | tf_op jit(solution)/shard_map/ppermute | solution.py:24
  235.7 12.5 %collective-permute-start.10 = (f32[4,16,1,128]{3,2,1,0:T(1,128)S(1)}, f32[4,16,1,128]{3,2,1,0:T(1,128)S(1)}, u32[]{:S(2)}, u32[]{:S(2)}) collective-permute-start(f32[4,16,1,128]{3,2,1,0:T(1,128)S(1)} %get-tuple-element.67), channel_id=1, source_target_pairs={{0,1},{1,2},{2,3},{3,4},{4,5},{5,6},{6,7},{7,8},{8,9},{9,10},{10,1... | collective-permute-start | bytes 98312 | tf_op jit(solution)/shard_map/ppermute | solution.py:22
  237.6 12.4 %collective-permute-start.11 = (f32[4,16,1,128]{3,2,1,0:T(1,128)S(1)}, f32[4,16,1,128]{3,2,1,0:T(1,128)S(1)}, u32[]{:S(2)}, u32[]{:S(2)}) collective-permute-start(f32[4,16,1,128]{3,2,1,0:T(1,128)S(1)} %get-tuple-element.66), channel_id=1, source_target_pairs={{1,0},{2,1},{3,2},{4,3},{5,4},{6,5},{7,6},{8,7},{9,8},{10,9},{11,1... | collective-permute-start | bytes 98312 | tf_op jit(solution)/shard_map/ppermute | solution.py:24
  254.2 8.9 %collective-permute-start.12 = (f32[1,16,128]{2,1,0:T(8,128)S(1)}, f32[1,16,128]{2,1,0:T(8,128)S(1)}, u32[]{:S(2)}, u32[]{:S(2)}) collective-permute-start(f32[1,16,128]{2,1,0:T(8,128)S(1)} %get-tuple-element.135), channel_id=1, source_target_pairs={{16,0},{32,16},{48,32},{64,48},{80,64},{96,80},{112,96},{128,112},... | collective-permute-start | bytes 24584 | tf_op jit(solution)/shard_map/ppermute | solution.py:24
  261.1 3.1 collective-permute-start.13
  264.2 8.7 %collective-permute-start.14 = (f32[18,1,128]{2,1,0:T(1,128)S(1)}, f32[18,1,128]{2,1,0:T(1,128)S(1)}, u32[]{:S(2)}, u32[]{:S(2)}) collective-permute-start(f32[18,1,128]{2,1,0:T(1,128)S(1)} %get-tuple-element.92), channel_id=1, source_target_pairs={{1,0},{2,1},{3,2},{4,3},{5,4},{6,5},{7,6},{8,7},{9,8},{10,9},{11,1... | collective-permute-start | bytes 27656 | tf_op jit(solution)/shard_map/ppermute | solution.py:24
  267.9 8.0 %collective-permute-start.15 = (f32[18,1,128]{2,1,0:T(1,128)S(1)}, f32[18,1,128]{2,1,0:T(1,128)S(1)}, u32[]{:S(2)}, u32[]{:S(2)}) collective-permute-start(f32[18,1,128]{2,1,0:T(1,128)S(1)} %get-tuple-element.93), channel_id=1, source_target_pairs={{0,1},{1,2},{2,3},{3,4},{4,5},{5,6},{6,7},{7,8},{8,9},{9,10},{10,1... | collective-permute-start | bytes 27656 | tf_op jit(solution)/shard_map/ppermute | solution.py:22
  276.2 9.4 %collective-permute-start.16 = (f32[1,16,128]{2,1,0:T(8,128)S(1)}, f32[1,16,128]{2,1,0:T(8,128)S(1)}, u32[]{:S(2)}, u32[]{:S(2)}) collective-permute-start(f32[1,16,128]{2,1,0:T(8,128)S(1)} %get-tuple-element.129), channel_id=1, source_target_pairs={{16,0},{32,16},{48,32},{64,48},{80,64},{96,80},{112,96},{128,112},... | collective-permute-start | bytes 24584 | tf_op jit(solution)/shard_map/ppermute | solution.py:24
  283.5 3.1 collective-permute-start.17
  286.6 6.9 %collective-permute-start.18 = (f32[18,1,128]{2,1,0:T(1,128)S(1)}, f32[18,1,128]{2,1,0:T(1,128)S(1)}, u32[]{:S(2)}, u32[]{:S(2)}) collective-permute-start(f32[18,1,128]{2,1,0:T(1,128)S(1)} %get-tuple-element.90), channel_id=1, source_target_pairs={{1,0},{2,1},{3,2},{4,3},{5,4},{6,5},{7,6},{8,7},{9,8},{10,9},{11,1... | collective-permute-start | bytes 27656 | tf_op jit(solution)/shard_map/ppermute | solution.py:24
  288.5 8.0 %collective-permute-start.19 = (f32[18,1,128]{2,1,0:T(1,128)S(1)}, f32[18,1,128]{2,1,0:T(1,128)S(1)}, u32[]{:S(2)}, u32[]{:S(2)}) collective-permute-start(f32[18,1,128]{2,1,0:T(1,128)S(1)} %get-tuple-element.91), channel_id=1, source_target_pairs={{0,1},{1,2},{2,3},{3,4},{4,5},{5,6},{6,7},{7,8},{8,9},{9,10},{10,1... | collective-permute-start | bytes 27656 | tf_op jit(solution)/shard_map/ppermute | solution.py:22
  296.7 9.4 %collective-permute-start.20 = (f32[1,16,128]{2,1,0:T(8,128)S(1)}, f32[1,16,128]{2,1,0:T(8,128)S(1)}, u32[]{:S(2)}, u32[]{:S(2)}) collective-permute-start(f32[1,16,128]{2,1,0:T(8,128)S(1)} %get-tuple-element.123), channel_id=1, source_target_pairs={{16,0},{32,16},{48,32},{64,48},{80,64},{96,80},{112,96},{128,112},... | collective-permute-start | bytes 24584 | tf_op jit(solution)/shard_map/ppermute | solution.py:24
  304.1 3.1 collective-permute-start.21
  307.2 6.9 %collective-permute-start.22 = (f32[18,1,128]{2,1,0:T(1,128)S(1)}, f32[18,1,128]{2,1,0:T(1,128)S(1)}, u32[]{:S(2)}, u32[]{:S(2)}) collective-permute-start(f32[18,1,128]{2,1,0:T(1,128)S(1)} %get-tuple-element.88), channel_id=1, source_target_pairs={{1,0},{2,1},{3,2},{4,3},{5,4},{6,5},{7,6},{8,7},{9,8},{10,9},{11,1... | collective-permute-start | bytes 27656 | tf_op jit(solution)/shard_map/ppermute | solution.py:24
  309.1 8.0 %collective-permute-start.23 = (f32[18,1,128]{2,1,0:T(1,128)S(1)}, f32[18,1,128]{2,1,0:T(1,128)S(1)}, u32[]{:S(2)}, u32[]{:S(2)}) collective-permute-start(f32[18,1,128]{2,1,0:T(1,128)S(1)} %get-tuple-element.89), channel_id=1, source_target_pairs={{0,1},{1,2},{2,3},{3,4},{4,5},{5,6},{6,7},{7,8},{8,9},{9,10},{10,1... | collective-permute-start | bytes 27656 | tf_op jit(solution)/shard_map/ppermute | solution.py:22
  317.3 9.1 %collective-permute-start.24 = (f32[1,16,128]{2,1,0:T(8,128)S(1)}, f32[1,16,128]{2,1,0:T(8,128)S(1)}, u32[]{:S(2)}, u32[]{:S(2)}) collective-permute-start(f32[1,16,128]{2,1,0:T(8,128)S(1)} %get-tuple-element.117), channel_id=1, source_target_pairs={{16,0},{32,16},{48,32},{64,48},{80,64},{96,80},{112,96},{128,112},... | collective-permute-start | bytes 24584 | tf_op jit(solution)/shard_map/ppermute | solution.py:24
  324.4 3.1 collective-permute-start.25
  327.5 6.9 %collective-permute-start.26 = (f32[18,1,128]{2,1,0:T(1,128)S(1)}, f32[18,1,128]{2,1,0:T(1,128)S(1)}, u32[]{:S(2)}, u32[]{:S(2)}) collective-permute-start(f32[18,1,128]{2,1,0:T(1,128)S(1)} %get-tuple-element.86), channel_id=1, source_target_pairs={{1,0},{2,1},{3,2},{4,3},{5,4},{6,5},{7,6},{8,7},{9,8},{10,9},{11,1... | collective-permute-start | bytes 27656 | tf_op jit(solution)/shard_map/ppermute | solution.py:24
  329.4 8.0 %collective-permute-start.27 = (f32[18,1,128]{2,1,0:T(1,128)S(1)}, f32[18,1,128]{2,1,0:T(1,128)S(1)}, u32[]{:S(2)}, u32[]{:S(2)}) collective-permute-start(f32[18,1,128]{2,1,0:T(1,128)S(1)} %get-tuple-element.87), channel_id=1, source_target_pairs={{0,1},{1,2},{2,3},{3,4},{4,5},{5,6},{6,7},{7,8},{8,9},{9,10},{10,1... | collective-permute-start | bytes 27656 | tf_op jit(solution)/shard_map/ppermute | solution.py:22
  337.6 9.1 %collective-permute-start.28 = (f32[1,16,128]{2,1,0:T(8,128)S(1)}, f32[1,16,128]{2,1,0:T(8,128)S(1)}, u32[]{:S(2)}, u32[]{:S(2)}) collective-permute-start(f32[1,16,128]{2,1,0:T(8,128)S(1)} %get-tuple-element.111), channel_id=1, source_target_pairs={{16,0},{32,16},{48,32},{64,48},{80,64},{96,80},{112,96},{128,112},... | collective-permute-start | bytes 24584 | tf_op jit(solution)/shard_map/ppermute | solution.py:24
  344.7 3.1 collective-permute-start.29
  347.8 6.9 %collective-permute-start.30 = (f32[18,1,128]{2,1,0:T(1,128)S(1)}, f32[18,1,128]{2,1,0:T(1,128)S(1)}, u32[]{:S(2)}, u32[]{:S(2)}) collective-permute-start(f32[18,1,128]{2,1,0:T(1,128)S(1)} %get-tuple-element.84), channel_id=1, source_target_pairs={{1,0},{2,1},{3,2},{4,3},{5,4},{6,5},{7,6},{8,7},{9,8},{10,9},{11,1... | collective-permute-start | bytes 27656 | tf_op jit(solution)/shard_map/ppermute | solution.py:24
  349.7 8.0 %collective-permute-start.31 = (f32[18,1,128]{2,1,0:T(1,128)S(1)}, f32[18,1,128]{2,1,0:T(1,128)S(1)}, u32[]{:S(2)}, u32[]{:S(2)}) collective-permute-start(f32[18,1,128]{2,1,0:T(1,128)S(1)} %get-tuple-element.85), channel_id=1, source_target_pairs={{0,1},{1,2},{2,3},{3,4},{4,5},{5,6},{6,7},{7,8},{8,9},{9,10},{10,1... | collective-permute-start | bytes 27656 | tf_op jit(solution)/shard_map/ppermute | solution.py:22
  357.9 9.1 %collective-permute-start.32 = (f32[1,16,128]{2,1,0:T(8,128)S(1)}, f32[1,16,128]{2,1,0:T(8,128)S(1)}, u32[]{:S(2)}, u32[]{:S(2)}) collective-permute-start(f32[1,16,128]{2,1,0:T(8,128)S(1)} %get-tuple-element.105), channel_id=1, source_target_pairs={{16,0},{32,16},{48,32},{64,48},{80,64},{96,80},{112,96},{128,112},... | collective-permute-start | bytes 24584 | tf_op jit(solution)/shard_map/ppermute | solution.py:24
  365.0 3.1 collective-permute-start.33
  368.1 6.9 %collective-permute-start.34 = (f32[18,1,128]{2,1,0:T(1,128)S(1)}, f32[18,1,128]{2,1,0:T(1,128)S(1)}, u32[]{:S(2)}, u32[]{:S(2)}) collective-permute-start(f32[18,1,128]{2,1,0:T(1,128)S(1)} %get-tuple-element.82), channel_id=1, source_target_pairs={{1,0},{2,1},{3,2},{4,3},{5,4},{6,5},{7,6},{8,7},{9,8},{10,9},{11,1... | collective-permute-start | bytes 27656 | tf_op jit(solution)/shard_map/ppermute | solution.py:24
  370.2 8.0 %collective-permute-start.35 = (f32[18,1,128]{2,1,0:T(1,128)S(1)}, f32[18,1,128]{2,1,0:T(1,128)S(1)}, u32[]{:S(2)}, u32[]{:S(2)}) collective-permute-start(f32[18,1,128]{2,1,0:T(1,128)S(1)} %get-tuple-element.83), channel_id=1, source_target_pairs={{0,1},{1,2},{2,3},{3,4},{4,5},{5,6},{6,7},{7,8},{8,9},{9,10},{10,1... | collective-permute-start | bytes 27656 | tf_op jit(solution)/shard_map/ppermute | solution.py:22
  378.4 9.4 %collective-permute-start.36 = (f32[1,16,128]{2,1,0:T(8,128)S(1)}, f32[1,16,128]{2,1,0:T(8,128)S(1)}, u32[]{:S(2)}, u32[]{:S(2)}) collective-permute-start(f32[1,16,128]{2,1,0:T(8,128)S(1)} %get-tuple-element.99), channel_id=1, source_target_pairs={{16,0},{32,16},{48,32},{64,48},{80,64},{96,80},{112,96},{128,112},... | collective-permute-start | bytes 24584 | tf_op jit(solution)/shard_map/ppermute | solution.py:24
  385.8 3.1 collective-permute-start.37
  388.9 6.9 %collective-permute-start.38 = (f32[18,1,128]{2,1,0:T(1,128)S(1)}, f32[18,1,128]{2,1,0:T(1,128)S(1)}, u32[]{:S(2)}, u32[]{:S(2)}) collective-permute-start(f32[18,1,128]{2,1,0:T(1,128)S(1)} %get-tuple-element.80), channel_id=1, source_target_pairs={{1,0},{2,1},{3,2},{4,3},{5,4},{6,5},{7,6},{8,7},{9,8},{10,9},{11,1... | collective-permute-start | bytes 27656 | tf_op jit(solution)/shard_map/ppermute | solution.py:24
  392.8 8.0 %collective-permute-start.39 = (f32[18,1,128]{2,1,0:T(1,128)S(1)}, f32[18,1,128]{2,1,0:T(1,128)S(1)}, u32[]{:S(2)}, u32[]{:S(2)}) collective-permute-start(f32[18,1,128]{2,1,0:T(1,128)S(1)} %get-tuple-element.81), channel_id=1, source_target_pairs={{0,1},{1,2},{2,3},{3,4},{4,5},{5,6},{6,7},{7,8},{8,9},{9,10},{10,1... | collective-permute-start | bytes 27656 | tf_op jit(solution)/shard_map/ppermute | solution.py:22
where the time goes:
time: 407 us; the launch traced here: 402 us
  starting transfers between devices  161 us (40%)
  other arithmetic  155 us (38%)
  local copies, waits for them, and re-layouts  52.3 us (13%)
  waiting for transfers between devices  30.8 us (8%)
    scatter-add x1, other arithmetic, body(): spread_grid.at[:, all_cells.reshape(-1)]  139 us
    ppermute x18, starting transfers between devices, with_halo(): lax.ppermute(head, axis, [((i + 1) % count, i) for i in range(count)])  90.2 us
    ppermute x18, starting transfers between devices, with_halo(): lax.ppermute(tail, axis, [(i, (i + 1) % count) for i in range(count)])  51.5 us
    ppermute x18, waiting for transfers between devices, with_halo(): lax.ppermute(tail, axis, [(i, (i + 1) % count) for i in range(count)])  30.7 us
    ppermute x4, starting transfers between devices, passed_along(): return lax.ppermute(block, axis, route)  19.6 us
    unnamed x14, local copies, waits for them, and re-layouts  15.2 us
    slice x1, local copies, waits for them, and re-layouts, body(): inner_rows = spread_grid[:, 1:brick_x + 1]  12.8 us
  transfers between devices with their start and end apart: 40, of which 14 were waited for; matrix products, arithmetic and copies ran while one was open for 49% of the time, Pallas kernels for 0%

commit v1 on v0

v1 whole, which is shorter than its diff:
```python
import jax
import jax.numpy as jnp
from jax import lax
from jax.experimental import pallas as pl
from jax.experimental.pallas import tpu as pltpu
from jax.sharding import PartitionSpec as P

SWEEPS = 8
DIFFUSION = (1.0, 0.7, 0.45)
VALENCE = (1.0, -1.0, 2.0)
TIME_STEP = 0.05
SCREENING = 0.05

F32 = jnp.float32
BF16 = jnp.bfloat16
BX, BY, NZ = 16, 16, 128
SLOTS, MOVERS, CHANNELS, NODES = 128, 16, 4, 128
W = 8
EXT = BX + 2 * W
WIDE = BX + 2
PAIRS = WIDE * WIDE // 2
ROWS = PAIRS * 2 * CHANNELS
GROUP = 8
KEPT = SLOTS - 4 * 8

T_REC, T_CONC, T_POT, T_EPS, T_A = 0, 8, 14, 30, 46
T_DY, T_FY, T_BY = 0, 18, 25
T_DX, T_FX, T_CX, T_BX = 0, 32, 38, 70

VMEM = pl.BlockSpec(memory_space=pltpu.VMEM)
SMEM = pl.BlockSpec(memory_space=pltpu.SMEM)


def parity(axis):
    return lax.rem(lax.axis_index(axis), 2)


def swap(block, axis, odd):
    count = lax.axis_size(axis)
    route = [(i, (((i - odd) % count ^ 1) + odd) % count) for i in range(count)]
    return lax.ppermute(block, axis, route)


def pack_kernel(conc, pot, eps, rec, slots, counts, *outs):
    for axis, odd, out in (("gx", 0, outs[0]), ("gx", 1, outs[1]), ("gy", 0, outs[2]), ("gy", 1, outs[3])):
        p = parity(axis)
        up = 1 - p if odd == 0 else p
        way = (1 if axis == "gx" else 3) - up
        number = counts[0, way]
        for k in range(MOVERS):
            row = rec[slots[0, way, k]]
            out[T_REC + k // 2, (k % 2) * 4 : (k % 2) * 4 + 4] = jnp.where(k < number, row, 0.0)
        if axis == "gx":
            out[T_CONC:T_POT] = conc[:, up * (BX - 1)].reshape(6, 8, NZ)
            out[T_POT:T_EPS] = pot[pl.ds(up * W, W)].reshape(16, 8, NZ)
            out[T_EPS:T_A] = eps[pl.ds(up * W, W)].reshape(16, 8, NZ)
        else:
            for s in range(3):
                face = jnp.where(up == 1, conc[s, :, BY - 1], conc[s, :, 0])
                out[T_CONC + 2 * s : T_CONC + 2 * s + 2] = face.reshape(2, 8, NZ)
            start = pl.multiple_of(up * W, W)
            out[T_POT:T_EPS] = pot[:, pl.ds(start, W)]
            out[T_EPS:T_A] = eps[:, pl.ds(start, W)]


def hot_group(rows_of, a_s, b_s):
    sub = lax.broadcasted_iota(jnp.int32, (16, NODES), 0)
    second = (sub >= 8).astype(F32)
    subf = sub.astype(F32)
    for g in range(GROUP):
        cell, value = rows_of(g)
        half = (cell >= PAIRS * NZ).astype(jnp.int32)
        high = ((cell - half * (PAIRS * NZ)) >> 7).astype(F32)
        low = ((cell & (NZ - 1)) + half * NZ).astype(F32)
        high = (jnp.broadcast_to(high, (16, NODES)) - second).astype(BF16)
        low = (jnp.broadcast_to(low, (16, NODES)) - subf).astype(BF16)
        lead = value.astype(BF16).astype(F32)
        rest = value - lead
        parts = jnp.concatenate([lead, rest, lead, rest], axis=0).astype(BF16)
        lanes = slice(g * NODES, (g + 1) * NODES)
        for m in range(ROWS // 16):
            a_s[m * 16 : (m + 1) * 16, lanes] = jnp.where(high == BF16(2 * m), parts, BF16(0))
        for m in range(16):
            b_s[m * 16 : (m + 1) * 16, lanes] = jnp.where(low == BF16(16 * m), BF16(1), BF16(0))
    sums = lax.dot_general(a_s[...], b_s[...], (((1,), (1,)), ((), ())), preferred_element_type=F32)
    return sums[:, :NZ], sums[:, NZ:]


def kept_kernel(rec, nodes, count, slots, counts, acc, a_s, b_s, gone, order):
    def clear(c, _):
        gone[c] = 0
        return 0

    lax.fori_loop(0, SLOTS, clear, 0, unroll=8)
    for way in range(4):
        number = counts[0, way]

        def mark(k, _, way=way):
            gone[slots[0, way, k]] = 1
            return 0

        lax.fori_loop(0, number, mark, 0)
    live = count[0]

    def gather(c, found):
        order[found] = c
        stays = jnp.logical_and(c < live, gone[c] == 0)
        return found + stays.astype(jnp.int32)

    found = lax.fori_loop(0, SLOTS, gather, 0, unroll=8)
    acc[...] = jnp.zeros_like(acc)

    def group(c, _):
        def rows_of(g):
            at = c * GROUP + g
            inside = at < found
            slot = jnp.where(inside, order[at], 0)
            return nodes[pl.ds(slot, 1), :], jnp.where(inside, rec[slot], 0.0)

        left, right = hot_group(rows_of, a_s, b_s)
        acc[0] += left
        acc[1] += right
        return 0

    lax.fori_loop(0, (found + GROUP - 1) // GROUP, group, 0)


def face_flux(s, upper, lower, step):
    return -DIFFUSION[s] * ((upper - lower) + (VALENCE[s] * 0.5) * (upper + lower) * step)


def arrive_kernel(acc_in, x0, x1, y0, y1, nodes, conc, pot, conc_next, dens, force, s0, s1, acc, a_s, b_s, rec, cells, wide):
    px, py = parity("gx"), parity("gy")
    for b, (buf, way) in enumerate(((x0, 1 - px), (x1, px), (y0, 3 - py), (y1, 2 + py))):
        for t in range(8):
            rec[b * 16 + 2 * t] = buf[T_REC + t, 0:4]
            rec[b * 16 + 2 * t + 1] = buf[T_REC + t, 4:8]
        cells[b * 16 : (b + 1) * 16] = nodes[0, way]

    def rows_at(c):
        def rows_of(g):
            at = c * GROUP + g
            return cells[pl.ds(at, 1), :], rec[at]

        return rows_of

    left, right = hot_group(rows_at(0), a_s, b_s)
    acc[0] = acc_in[0] + left
    acc[1] = acc_in[1] + right

    def group(c, _):
        left, right = hot_group(rows_at(c), a_s, b_s)
        acc[0] += left
        acc[1] += right
        return 0

    lax.fori_loop(1, 4 * MOVERS // GROUP, group, 0)

    x_low_first, y_low_first = px == 1, py == 1
    for f in range(4):
        first, last = (T_CONC + 2 * f, T_CONC + 2 * f + 2) if f < 3 else (T_POT, T_POT + 2)
        own = conc[f] if f < 3 else pot[...]
        wide[f, 1 : BX + 1, 8 : 8 + BY] = own
        if f < 3:
            xa, xb = x0[first:last], x1[first:last]
            wide[f, 0, 8 : 8 + BY] = jnp.where(x_low_first, xa, xb).reshape(BY, NZ)
            wide[f, BX + 1, 8 : 8 + BY] = jnp.where(x_low_first, xb, xa).reshape(BY, NZ)
            ya, yb = y0[first:last].reshape(BX, NZ), y1[first:last].reshape(BX, NZ)
            y_low, y_high = jnp.where(y_low_first, ya, yb), jnp.where(y_low_first, yb, ya)
        else:
            lows = jnp.where(x_low_first, x0[T_EPS - 2 : T_EPS], x1[T_EPS - 2 : T_EPS])
            highs = jnp.where(x_low_first, x1[T_POT : T_POT + 2], x0[T_POT : T_POT + 2])
            wide[f, 0, 8 : 8 + BY] = lows.reshape(BY, NZ)
            wide[f, BX + 1, 8 : 8 + BY] = highs.reshape(BY, NZ)
            y_low = jnp.where(y_low_first, y0[T_POT:T_EPS, 7], y1[T_POT:T_EPS, 7])
            y_high = jnp.where(y_low_first, y1[T_POT:T_EPS, 0], y0[T_POT:T_EPS, 0])
        wide[f, 1 : BX + 1, 7] = y_low
        wide[f, 1 : BX + 1, 8 + BY] = y_high

    dens[...] = jnp.zeros_like(dens)

    def spread(channel, ex, first, number):
        half, row = (0, ex) if ex < WIDE // 2 else (1, ex - WIDE // 2)
        base = (row * WIDE + first) * 8 + channel
        return acc[half, pl.ds(base, number, stride=8)] + acc[half, pl.ds(base + 4, number, stride=8)]

    for ex in range(WIDE):
        dens[ex, 7 : 7 + WIDE] = spread(0, ex, 0, WIDE)
        for a in range(3):
            force[a, ex] = spread(a + 1, ex, 1, BY)

    def plane(x, _):
        pc, pe, pw = wide[3, x + 1, 8:24], wide[3, x + 2, 8:24], wide[3, x, 8:24]
        pn, ps = wide[3, x + 1, 9:25], wide[3, x + 1, 7:23]
        pz = pltpu.roll(pc, NZ - 1, 1)
        dx, dw, dn, ds, dz = pe - pc, pc - pw, pn - pc, pc - ps, pz - pc
        total = dens[x + 1, 8:24]
        for s in range(3):
            c = wide[s, x + 1, 8:24]
            flux_x = face_flux(s, wide[s, x + 2, 8:24], c, dx)
            flux_w = face_flux(s, c, wide[s, x, 8:24], dw)
            flux_n = face_flux(s, wide[s, x + 1, 9:25], c, dn)
            flux_s = face_flux(s, c, wide[s, x + 1, 7:23], ds)
            flux_z = face_flux(s, pltpu.roll(c, NZ - 1, 1), c, dz)
            div = ((flux_x - flux_w) + (flux_n - flux_s)) + (flux_z - pltpu.roll(flux_z, 1, 1))
            later = c - TIME_STEP * div
            conc_next[s, x] = later
            total = total + VALENCE[s] * later
        dens[x + 1, 8:24] = total
        return 0

    lax.fori_loop(0, BX, plane, 0)

    for out, up in ((s0, 1 - py), (s1, py)):
        for ex in range(WIDE):
            out[T_DY + ex] = jnp.where(up == 1, dens[ex, 17:25], dens[ex, 7:15])
        for a in range(3):
            for ex in range(WIDE):
                r = a * WIDE + ex
                rim = jnp.where(up == 1, spread(a + 1, ex, WIDE - 1, 1), spread(a + 1, ex, 0, 1))
                out[T_FY + r // 8, r % 8 : r % 8 + 1] = rim
        out[T_FY + 6, 6:8] = jnp.zeros((2, NZ), F32)


def middle_kernel(dens, force, r0, r1, y0, y1, dext, fcore, s0, s1):
    px, py = parity("gx"), parity("gy")
    low_first = py == 1
    dext[...] = jnp.zeros_like(dext)
    for ex in range(WIDE):
        dext[ex + 7] = dens[ex]
        a, b = r0[T_DY + ex], r1[T_DY + ex]
        dext[ex + 7, 1:9] += jnp.where(low_first, a, b)
        dext[ex + 7, 23:31] += jnp.where(low_first, b, a)
    for c in range(3):
        for ex in range(WIDE):
            r = c * WIDE + ex
            a, b = r0[T_FY + r // 8, r % 8 : r % 8 + 1], r1[T_FY + r // 8, r % 8 : r % 8 + 1]
            fcore[c, ex] = force[c, ex]
            fcore[c, ex, 0:1] += jnp.where(low_first, a, b)
            fcore[c, ex, 15:16] += jnp.where(low_first, b, a)
    for out, up in ((s0, 1 - px), (s1, px)):
        out[T_DX:T_FX] = dext[pl.ds(7 + 10 * up, 8)].reshape(32, 8, NZ)
        out[T_FX:T_CX] = fcore[:, up * (WIDE - 1)].reshape(6, 8, NZ)
        for n, (buf, first) in enumerate(((y0, T_POT), (y1, T_POT), (y0, T_EPS), (y1, T_EPS))):
            out[T_CX + 8 * n : T_CX + 8 * n + 8] = buf[pl.ds(first + W * up, W)]


def sweep_kernel(dext, fcore, r0, r1, x0, x1, y0, y1, pot, eps, pot_next, force, phi_a, phi_b, ew, cx, cy, cz, cd, inv):
    px, py = parity("gx"), parity("gy")
    x_low_first, y_low_first = px == 1, py == 1

    force[...] = fcore[:, 1 : BX + 1]
    fa, fb = r0[T_FX:T_CX].reshape(3, BY, NZ), r1[T_FX:T_CX].reshape(3, BY, NZ)
    force[:, 0] += jnp.where(x_low_first, fa, fb)
    force[:, BX - 1] += jnp.where(x_low_first, fb, fa)

    cd[...] = dext[...]
    da, db = r0[T_DX:T_FX].reshape(8, EXT, NZ), r1[T_DX:T_FX].reshape(8, EXT, NZ)
    cd[1:9] += jnp.where(x_low_first, da, db)
    cd[23:31] += jnp.where(x_low_first, db, da)

    zero = jnp.zeros((EXT, 8, NZ), F32)
    for buf in (phi_a, phi_b, ew):
        buf[:, 0:8] = zero
        buf[:, 40:48] = zero
    for n, (buf, own, tile) in enumerate(((phi_a, pot, T_POT), (ew, eps, T_EPS))):
        buf[W : W + BX, 16:32] = own[...]
        a, b = x0[tile : tile + 16].reshape(W, BY, NZ), x1[tile : tile + 16].reshape(W, BY, NZ)
        buf[0:W, 16:32] = jnp.where(x_low_first, a, b)
        buf[W + BX : EXT, 16:32] = jnp.where(x_low_first, b, a)
        a, b = y0[tile : tile + 16], y1[tile : tile + 16]
        buf[W : W + BX, 8:16] = jnp.where(y_low_first, a, b)
        buf[W : W + BX, 32:40] = jnp.where(y_low_first, b, a)
        corner = T_CX + 16 * n
        for r, low in ((r0, x_low_first), (r1, jnp.logical_not(x_low_first))):
            a, b = r[corner : corner + 8], r[corner + 8 : corner + 16]
            first = jnp.where(low, 0, W + BX)
            buf[pl.ds(first, W), 8:16] = jnp.where(y_low_first, a, b)
            buf[pl.ds(first, W), 32:40] = jnp.where(y_low_first, b, a)

    def coefficients(x, _):
        e = ew[x, 8:40]
        up = e + ew[jnp.minimum(x + 1, EXT - 1), 8:40]
        cx[x] = up
        n = e + ew[x, 9:41]
        s = e + ew[x, 7:39]
        cy[x] = n
        z = e + pltpu.roll(e, NZ - 1, 1)
        cz[x] = z
        down = e + ew[jnp.maximum(x - 1, 0), 8:40]
        inv[x] = 1.0 / ((((up + down) + (n + s)) + (z + pltpu.roll(z, 1, 1))) + 2.0 * SCREENING)
        cd[x] = 2.0 * cd[x]
        return 0

    lax.fori_loop(0, EXT, coefficients, 0)

    for k in range(1, SWEEPS + 1):
        old, new = (phi_a, phi_b) if k % 2 == 1 else (phi_b, phi_a)
        lo, hi = (8, 40) if k < SWEEPS else (16, 32)

        def plane(x, _, old=old, new=new, lo=lo, hi=hi, k=k):
            f = slice(lo - 8, hi - 8)
            p = old[x, lo:hi]
            z = cz[x, f]
            c = cy[x, f]
            e_here = ew[x, lo:hi]
            total = cx[x, f] * old[x + 1, lo:hi] + cx[x - 1, f] * old[x - 1, lo:hi]
            total += c * old[x, lo + 1 : hi + 1] + (e_here + ew[x, lo - 1 : hi - 1]) * old[x, lo - 1 : hi - 1]
            total += z * pltpu.roll(p, NZ - 1, 1) + pltpu.roll(z * p, 1, 1)
            total = (total + cd[x, f]) * inv[x, f]
            if k < SWEEPS:
                new[x, lo:hi] = total
            else:
                pot_next[x - W] = total
            return 0

        lax.fori_loop(k, EXT - k, plane, 0, unroll=2)


def shape(*dims):
    return jax.ShapeDtypeStruct(dims, F32)


def call(kernel, name, ins, outs, scratch=(), flops=0):
    moved = 4 * sum(int(o.size) for o in outs)
    return pl.pallas_call(
        kernel,
        name=name,
        in_specs=ins,
        out_specs=[VMEM] * len(outs),
        out_shape=outs,
        scratch_shapes=scratch,
        compiler_params=pltpu.CompilerParams(vmem_limit_bytes=40 << 20),
        cost_estimate=pl.CostEstimate(flops=flops, bytes_accessed=moved, transcendentals=0),
    )


def body(conc, pot, eps, records, count, slots, counts, own_nodes, arrive_nodes):
    hot = [pltpu.VMEM((ROWS, GROUP * NODES), BF16), pltpu.VMEM((2 * NZ, GROUP * NODES), BF16)]
    sends = call(pack_kernel, "pack", [VMEM] * 4 + [SMEM] * 2, [shape(T_A, 8, NZ)] * 4)(
        conc, pot, eps, records, slots, counts
    )
    y0, y1 = swap(sends[2], "gy", 0), swap(sends[3], "gy", 1)
    x1, x0 = swap(sends[1], "gx", 1), swap(sends[0], "gx", 0)
    (acc,) = call(
        kept_kernel,
        "spread_kept",
        [VMEM] * 2 + [SMEM] * 3,
        [shape(2, ROWS, NZ)],
        hot + [pltpu.SMEM((SLOTS,), jnp.int32), pltpu.SMEM((SLOTS + GROUP,), jnp.int32)],
        flops=2 * ROWS * 2 * NZ * KEPT * NODES,
    )(records, own_nodes, count, slots, counts)
    conc_next, dens, force, b0, b1 = call(
        arrive_kernel,
        "spread_arrived",
        [VMEM] * 8,
        [shape(3, BX, BY, NZ), shape(WIDE, EXT, NZ), shape(3, WIDE, BY, NZ), shape(T_BY, 8, NZ), shape(T_BY, 8, NZ)],
        [pltpu.VMEM((2, ROWS, NZ), F32)]
        + hot
        + [
            pltpu.VMEM((4 * MOVERS, CHANNELS, NODES), F32),
            pltpu.VMEM((4 * MOVERS, NODES), jnp.int32),
            pltpu.VMEM((4, WIDE, 32, NZ), F32),
        ],
        flops=2 * ROWS * 2 * NZ * 4 * MOVERS * NODES,
    )(acc, x0, x1, y0, y1, arrive_nodes, conc, pot)
    c0, c1 = swap(b0, "gy", 0), swap(b1, "gy", 1)
    dext, fcore, e0, e1 = call(
        middle_kernel,
        "join_y",
        [VMEM] * 6,
        [shape(EXT, EXT, NZ), shape(3, WIDE, BY, NZ), shape(T_BX, 8, NZ), shape(T_BX, 8, NZ)],
    )(dens, force, c0, c1, y0, y1)
    g1, g0 = swap(e1, "gx", 1), swap(e0, "gx", 0)
    field = pltpu.VMEM((EXT, 48, NZ), F32)
    plain = pltpu.VMEM((EXT, EXT, NZ), F32)
    pot_next, body_force = call(
        sweep_kernel,
        "sweeps",
        [VMEM] * 10,
        [shape(BX, BY, NZ), shape(3, BX, BY, NZ)],
        [field, field, field, plain, plain, plain, plain, plain],
        flops=20 * SWEEPS * EXT * EXT * NZ,
    )(dext, fcore, g0, g1, x0, x1, y0, y1, pot, eps)
    return conc_next, pot_next, body_force


def solution(mesh):
    placed = (
        P(None, "gx", "gy", None),
        P("gx", "gy", None),
        P("gx", "gy", None),
        P(("gx", "gy"), None, None),
        P(("gx", "gy")),
        P(("gx", "gy"), None, None),
        P(("gx", "gy"), None),
        P(("gx", "gy"), None),
        P(("gx", "gy"), None, None, None),
    )
    return jax.shard_map(
        body,
        mesh=mesh,
        in_specs=placed,
        out_specs=(P(None, "gx", "gy", None), P("gx", "gy", None), P(None, "gx", "gy", None)),
        check_vma=False,
    )
```

time: 407 us -> 96.2 us (0.24)
  the two profiles are of different devices: /device:TPU:1 before, /device:TPU:24 now
where the time goes in v1:
time: 96.2 us; the launch traced here: 95.6 us
  starting transfers between devices  35.9 us (37%)
  Pallas kernels  35.8 us (37%)
  waiting for transfers between devices  15.2 us (16%)
  local copies, waits for them, and re-layouts  7.27 us (8%)
  between operations  1.45 us (2%)
    ppermute x8, starting transfers between devices, swap(): return lax.ppermute(block, axis, route)  35.9 us
    ppermute x8, waiting for transfers between devices, swap(): return lax.ppermute(block, axis, route)  15.2 us
    pallas_call x1, Pallas kernels, body(): call(sweep_kernel, 'sweeps', [VMEM] * 10, [shape(BX, BY, NZ), shape(3, BX...  14.3 us
    pallas_call x1, Pallas kernels, body(): call(arrive_kernel, 'spread_arrived', [VMEM] * 8, [shape(3, BX, BY, NZ),...  11.2 us
    pallas_call x1, Pallas kernels, body(): call(kept_kernel, 'spread_kept', [VMEM] * 2 + [SMEM] * 3, [shape(2, ROWS,...  9.4 us
    unnamed x26, local copies, waits for them, and re-layouts  7.27 us
  transfers between devices with their start and end apart: 8, of which 3 were waited for; matrix products, arithmetic and copies ran while one was open for 0% of the time, Pallas kernels for 10%

profile of v1, /device:TPU:24, one launch (start us, length us, event | category | flops | bytes accessed | tf_op | source)
XLA Modules:
  0.0 95.6 jit_solution(9903339276067392438)
XLA Ops:
  0.6 0.0 copy-start
  0.6 0.9 copy-done
  1.5 0.0 copy-start.2
  1.5 0.9 copy-done.2
  2.4 0.0 copy-start.4
  2.4 1.0 %copy-done.4 = f32[3,16,16,128]{3,2,1,0:T(8,128)S(1)} copy-done((f32[3,16,16,128]{3,2,1,0:T(8,128)S(1)}, f32[3,16,16,128]{3,2,1,0:T(8,128)}, u32[]{:S(2)}) %copy-start.4) | copy-done | bytes 393240
  3.4 0.0 copy-start.6
  3.4 0.9 copy-done.6
  4.4 0.0 copy-start.7
  4.4 0.7 copy-done.7
  5.1 0.0 copy-start.9
  5.1 0.7 copy-done.9
  5.7 0.7 pack.1
  6.5 1.9 %collective-permute-start = (f32[46,8,128]{2,1,0:T(8,128)S(1)}, f32[46,8,128]{2,1,0:T(8,128)S(1)}, u32[]{:S(2)}, u32[]{:S(2)}) collective-permute-start(f32[46,8,128]{2,1,0:T(8,128)S(1)} %get-tuple-element.18), channel_id=1, source_target_pairs={{0,16},{16,0},{32,48},{48,32},{64,80},{80,64},{96,112},{112,96},{1... | collective-permute-start | bytes 565256 | tf_op jit(solution)/shard_map/ppermute | solution.py:41
  8.4 12.0 %collective-permute-start.1 = (f32[46,8,128]{2,1,0:T(8,128)S(1)}, f32[46,8,128]{2,1,0:T(8,128)S(1)}, u32[]{:S(2)}, u32[]{:S(2)}) collective-permute-start(f32[46,8,128]{2,1,0:T(8,128)S(1)} %get-tuple-element.19), channel_id=1, source_target_pairs={{0,496},{16,32},{32,16},{48,64},{64,48},{80,96},{96,80},{112,128},... | collective-permute-start | bytes 565256 | tf_op jit(solution)/shard_map/ppermute | solution.py:41
  20.4 4.6 %collective-permute-start.2 = (f32[46,8,128]{2,1,0:T(8,128)S(1)}, f32[46,8,128]{2,1,0:T(8,128)S(1)}, u32[]{:S(2)}, u32[]{:S(2)}) collective-permute-start(f32[46,8,128]{2,1,0:T(8,128)S(1)} %get-tuple-element.20), channel_id=1, source_target_pairs={{0,1},{1,0},{2,3},{3,2},{4,5},{5,4},{6,7},{7,6},{8,9},{9,8},{10,11... | collective-permute-start | bytes 565256 | tf_op jit(solution)/shard_map/ppermute | solution.py:41
  25.0 2.6 %collective-permute-start.3 = (f32[46,8,128]{2,1,0:T(8,128)S(1)}, f32[46,8,128]{2,1,0:T(8,128)S(1)}, u32[]{:S(2)}, u32[]{:S(2)}) collective-permute-start(f32[46,8,128]{2,1,0:T(8,128)S(1)} %get-tuple-element.21), channel_id=1, source_target_pairs={{0,15},{1,2},{2,1},{3,4},{4,3},{5,6},{6,5},{7,8},{8,7},{9,10},{10,... | collective-permute-start | bytes 565256 | tf_op jit(solution)/shard_map/ppermute | solution.py:41
  28.3 0.0 copy-start.8
  28.3 0.7 copy-done.8
  29.0 0.0 copy-start.10
  29.0 0.7 copy-done.10
  29.6 0.0 copy-start.11
  29.6 0.8 copy-done.11
  30.5 0.0 copy-start.1
  30.5 0.0 copy-start.5
  30.5 0.0 copy-start.12
  30.5 9.4 %spread_kept.1.acc_in = f32[2,1296,128]{2,1,0:T(8,128)S(1)} custom-call(f32[128,4,128]{2,1,0:T(4,128)S(1)} %copy-done.6, s32[128,128]{1,0:T(8,128)S(1)} %copy-done.11, s32[1]{0:T(128)S(6)} %copy.12.count, s32[1,4,16]{2,1,0:T(4,128)S(1)} %copy-done.8, s32[1,4]{1,0:T(1,128)S(1)} %copy-done.10), custom_call_target="tpu_custom_call" | custom-call | flops 8153726976 | bytes 1327104 | tf_op jit(solution)/shard_map/spread_kept/pallas_call | solution.py:345
  39.9 0.0 collective-permute-done.x0
  39.9 0.0 collective-permute-done.1.x1
  39.9 0.0 collective-permute-done.2.y0
  39.9 0.0 collective-permute-done.3.y1
  39.9 0.0 copy-done.1
  39.9 0.0 copy-done.5
  39.9 0.0 copy-done.12
  39.9 11.2 %spread_arrived.1 = (f32[3,16,16,128]{3,2,1,0:T(8,128)}, f32[18,32,128]{2,1,0:T(8,128)S(1)}, f32[3,18,16,128]{3,2,1,0:T(8,128)S(1)}, f32[25,8,128]{2,1,0:T(8,128)S(1)}, f32[25,8,128]{2,1,0:T(8,128)S(1)}) custom-call(f32[2,1296,128]{2,1,0:T(8,128)S(1)} %spread_kept.1.acc_in, f32[46,8,128]{2,1,0:T(8,128)S(1)} %collective-permute-done.x0, ...), custom_call_target="tpu_custom_call" | custom-call | flops 5435817984 | bytes 1335296 | tf_op jit(solution)/shard_map/spread_arrived/pallas_call | solution.py:353
  51.1 0.0 copy-start.3
  51.1 9.0 %collective-permute-start.4 = (f32[25,8,128]{2,1,0:T(8,128)S(1)}, f32[25,8,128]{2,1,0:T(8,128)S(1)}, u32[]{:S(2)}, u32[]{:S(2)}) collective-permute-start(f32[25,8,128]{2,1,0:T(8,128)S(1)} %get-tuple-element.25), channel_id=1, source_target_pairs={{0,1},{1,0},{2,3},{3,2},{4,5},{5,4},{6,7},{7,6},{8,9},{9,8},{10,11... | collective-permute-start | bytes 307208 | tf_op jit(solution)/shard_map/ppermute | solution.py:41
  60.1 1.9 %collective-permute-start.5 = (f32[25,8,128]{2,1,0:T(8,128)S(1)}, f32[25,8,128]{2,1,0:T(8,128)S(1)}, u32[]{:S(2)}, u32[]{:S(2)}) collective-permute-start(f32[25,8,128]{2,1,0:T(8,128)S(1)} %get-tuple-element.26), channel_id=1, source_target_pairs={{0,15},{1,2},{2,1},{3,4},{4,3},{5,6},{6,5},{7,8},{8,7},{9,10},{10,... | collective-permute-start | bytes 307208 | tf_op jit(solution)/shard_map/ppermute | solution.py:41
  62.1 0.7 collective-permute-done.4.r0
  62.8 6.3 %collective-permute-done.5.r1 = f32[25,8,128]{2,1,0:T(8,128)S(1)} collective-permute-done((f32[25,8,128]{2,1,0:T(8,128)S(1)}, f32[25,8,128]{2,1,0:T(8,128)S(1)}, u32[]{:S(2)}, u32[]{:S(2)}) %collective-permute-start.5) | collective-permute-done | bytes 102432 | tf_op jit(solution)/shard_map/ppermute | solution.py:41
  69.1 0.2 join_y.1
  69.3 1.9 %collective-permute-start.6 = (f32[70,8,128]{2,1,0:T(8,128)S(1)}, f32[70,8,128]{2,1,0:T(8,128)S(1)}, u32[]{:S(2)}, u32[]{:S(2)}) collective-permute-start(f32[70,8,128]{2,1,0:T(8,128)S(1)} %get-tuple-element.29), channel_id=1, source_target_pairs={{0,16},{16,0},{32,48},{48,32},{64,80},{80,64},{96,112},{112,96},{1... | collective-permute-start | bytes 860168 | tf_op jit(solution)/shard_map/ppermute | solution.py:41
  71.2 1.9 %collective-permute-start.7 = (f32[70,8,128]{2,1,0:T(8,128)S(1)}, f32[70,8,128]{2,1,0:T(8,128)S(1)}, u32[]{:S(2)}, u32[]{:S(2)}) collective-permute-start(f32[70,8,128]{2,1,0:T(8,128)S(1)} %get-tuple-element.30), channel_id=1, source_target_pairs={{0,496},{16,32},{32,16},{48,64},{64,48},{80,96},{96,80},{112,128},... | collective-permute-start | bytes 860168 | tf_op jit(solution)/shard_map/ppermute | solution.py:41
  73.1 0.0 collective-permute-done.6.r0
  73.1 8.1 %collective-permute-done.7.r1 = f32[70,8,128]{2,1,0:T(8,128)S(1)} collective-permute-done((f32[70,8,128]{2,1,0:T(8,128)S(1)}, f32[70,8,128]{2,1,0:T(8,128)S(1)}, u32[]{:S(2)}, u32[]{:S(2)}) %collective-permute-start.7) | collective-permute-done | bytes 286752 | tf_op jit(solution)/shard_map/ppermute | solution.py:41
  81.3 0.0 copy-done.3
  81.3 14.3 %sweeps.1 = (f32[16,16,128]{2,1,0:T(8,128)}, f32[3,16,16,128]{3,2,1,0:T(8,128)}) custom-call(f32[32,32,128]{2,1,0:T(8,128)S(1)} %get-tuple-element.27.dext, f32[3,18,16,128]{3,2,1,0:T(8,128)S(1)} %get-tuple-element.28.fcore, f32[70,8,128]{2,1,0:T(8,128)S(1)} %collective-permute-done.6.r0, f32[70,8,128]{2,1,0:T(8,128)S(1)} %collective-permute-done.7.r1, ...), custom_call_target="tpu_custom_call" | custom-call | flops 20971520 | bytes 524288 | tf_op jit(solution)/shard_map/sweeps/pallas_call | solution.py:377
Async XLA Ops:
  0.6 0.9 copy-start
  1.5 0.9 copy-start.2
  2.4 1.0 %copy-start.4 = (f32[3,16,16,128]{3,2,1,0:T(8,128)S(1)}, f32[3,16,16,128]{3,2,1,0:T(8,128)}, u32[]{:S(2)}) copy-start(f32[3,16,16,128]{3,2,1,0:T(8,128)} %conc.3) | copy-start | bytes 1179652
  3.4 0.9 copy-start.6
  4.4 0.7 copy-start.7
  5.1 0.7 copy-start.9
  6.5 33.4 %collective-permute-start = (f32[46,8,128]{2,1,0:T(8,128)S(1)}, f32[46,8,128]{2,1,0:T(8,128)S(1)}, u32[]{:S(2)}, u32[]{:S(2)}) collective-permute-start(f32[46,8,128]{2,1,0:T(8,128)S(1)} %get-tuple-element.18), channel_id=1, source_target_pairs={{0,16},{16,0},{32,48},{48,32},{64,80},{80,64},{96,112},{112,96},{1... | collective-permute-start | bytes 565256 | tf_op jit(solution)/shard_map/ppermute | solution.py:41
  8.4 31.5 %collective-permute-start.1 = (f32[46,8,128]{2,1,0:T(8,128)S(1)}, f32[46,8,128]{2,1,0:T(8,128)S(1)}, u32[]{:S(2)}, u32[]{:S(2)}) collective-permute-start(f32[46,8,128]{2,1,0:T(8,128)S(1)} %get-tuple-element.19), channel_id=1, source_target_pairs={{0,496},{16,32},{32,16},{48,64},{64,48},{80,96},{96,80},{112,128},... | collective-permute-start | bytes 565256 | tf_op jit(solution)/shard_map/ppermute | solution.py:41
  20.4 19.5 %collective-permute-start.2 = (f32[46,8,128]{2,1,0:T(8,128)S(1)}, f32[46,8,128]{2,1,0:T(8,128)S(1)}, u32[]{:S(2)}, u32[]{:S(2)}) collective-permute-start(f32[46,8,128]{2,1,0:T(8,128)S(1)} %get-tuple-element.20), channel_id=1, source_target_pairs={{0,1},{1,0},{2,3},{3,2},{4,5},{5,4},{6,7},{7,6},{8,9},{9,8},{10,11... | collective-permute-start | bytes 565256 | tf_op jit(solution)/shard_map/ppermute | solution.py:41
  25.0 14.9 %collective-permute-start.3 = (f32[46,8,128]{2,1,0:T(8,128)S(1)}, f32[46,8,128]{2,1,0:T(8,128)S(1)}, u32[]{:S(2)}, u32[]{:S(2)}) collective-permute-start(f32[46,8,128]{2,1,0:T(8,128)S(1)} %get-tuple-element.21), channel_id=1, source_target_pairs={{0,15},{1,2},{2,1},{3,4},{4,3},{5,6},{6,5},{7,8},{8,7},{9,10},{10,... | collective-permute-start | bytes 565256 | tf_op jit(solution)/shard_map/ppermute | solution.py:41
  28.3 0.7 copy-start.8
  29.0 0.7 copy-start.10
  29.6 0.8 copy-start.11
  30.5 9.5 %copy-start.1 = (f32[16,16,128]{2,1,0:T(8,128)S(1)}, f32[16,16,128]{2,1,0:T(8,128)}, u32[]{:S(2)}) copy-start(f32[16,16,128]{2,1,0:T(8,128)} %pot.5) | copy-start | bytes 393220
  30.5 9.5 %copy-start.5 = (f32[3,16,16,128]{3,2,1,0:T(8,128)S(1)}, f32[3,16,16,128]{3,2,1,0:T(8,128)}, u32[]{:S(2)}) copy-start(f32[3,16,16,128]{3,2,1,0:T(8,128)} %conc.3) | copy-start | bytes 1179652
  30.5 9.5 %copy-start.12 = (s32[1,4,16,128]{3,2,1,0:T(8,128)S(1)}, s32[1,4,16,128]{3,2,1,0:T(8,128)}, u32[]{:S(2)}) copy-start(s32[1,4,16,128]{3,2,1,0:T(8,128)} %nodes.3) | copy-start | bytes 98308
  51.1 30.1 %copy-start.3 = (f32[16,16,128]{2,1,0:T(8,128)S(1)}, f32[16,16,128]{2,1,0:T(8,128)}, u32[]{:S(2)}) copy-start(f32[16,16,128]{2,1,0:T(8,128)} %eps.3) | copy-start | bytes 393220
  51.1 11.6 %collective-permute-start.4 = (f32[25,8,128]{2,1,0:T(8,128)S(1)}, f32[25,8,128]{2,1,0:T(8,128)S(1)}, u32[]{:S(2)}, u32[]{:S(2)}) collective-permute-start(f32[25,8,128]{2,1,0:T(8,128)S(1)} %get-tuple-element.25), channel_id=1, source_target_pairs={{0,1},{1,0},{2,3},{3,2},{4,5},{5,4},{6,7},{7,6},{8,9},{9,8},{10,11... | collective-permute-start | bytes 307208 | tf_op jit(solution)/shard_map/ppermute | solution.py:41
  60.1 9.0 %collective-permute-start.5 = (f32[25,8,128]{2,1,0:T(8,128)S(1)}, f32[25,8,128]{2,1,0:T(8,128)S(1)}, u32[]{:S(2)}, u32[]{:S(2)}) collective-permute-start(f32[25,8,128]{2,1,0:T(8,128)S(1)} %get-tuple-element.26), channel_id=1, source_target_pairs={{0,15},{1,2},{2,1},{3,4},{4,3},{5,6},{6,5},{7,8},{8,7},{9,10},{10,... | collective-permute-start | bytes 307208 | tf_op jit(solution)/shard_map/ppermute | solution.py:41
  69.3 3.9 %collective-permute-start.6 = (f32[70,8,128]{2,1,0:T(8,128)S(1)}, f32[70,8,128]{2,1,0:T(8,128)S(1)}, u32[]{:S(2)}, u32[]{:S(2)}) collective-permute-start(f32[70,8,128]{2,1,0:T(8,128)S(1)} %get-tuple-element.29), channel_id=1, source_target_pairs={{0,16},{16,0},{32,48},{48,32},{64,80},{80,64},{96,112},{112,96},{1... | collective-permute-start | bytes 860168 | tf_op jit(solution)/shard_map/ppermute | solution.py:41
  71.2 10.1 %collective-permute-start.7 = (f32[70,8,128]{2,1,0:T(8,128)S(1)}, f32[70,8,128]{2,1,0:T(8,128)S(1)}, u32[]{:S(2)}, u32[]{:S(2)}) collective-permute-start(f32[70,8,128]{2,1,0:T(8,128)S(1)} %get-tuple-element.30), channel_id=1, source_target_pairs={{0,496},{16,32},{32,16},{48,64},{64,48},{80,96},{96,80},{112,128},... | collective-permute-start | bytes 860168 | tf_op jit(solution)/shard_map/ppermute | solution.py:41

commit v2 on v1

v2 whole, which is shorter than its diff:
```python
import jax
import jax.numpy as jnp
from jax import lax
from jax.experimental import pallas as pl
from jax.experimental.pallas import tpu as pltpu
from jax.sharding import PartitionSpec as P

SWEEPS = 8
DIFFUSION = (1.0, 0.7, 0.45)
VALENCE = (1.0, -1.0, 2.0)
TIME_STEP = 0.05
SCREENING = 0.05

F32 = jnp.float32
BF16 = jnp.bfloat16
BX, BY, NZ = 16, 16, 128
SLOTS, MOVERS, CHANNELS, NODES = 128, 16, 4, 128
W = 8
EXT = BX + 2 * W
WIDE = BX + 2
PAIRS = WIDE * WIDE // 2
ROWS = PAIRS * 2 * CHANNELS
GROUP = 8
LATER = 24

Y_CONC, Y_POT, Y_EPS, Y_END = 8, 14, 30, 46
X_CONC, X_POT, X_EPS, X_END = 8, 14, 46, 78
DY_FORCE, DY_END = WIDE * W, WIDE * W + 56
DX_FORCE, DX_END = 32, 38

VMEM = pl.BlockSpec(memory_space=pltpu.VMEM)
SMEM = pl.BlockSpec(memory_space=pltpu.SMEM)
HBM = pl.BlockSpec(memory_space=pltpu.HBM)


def parity(axis):
    return lax.rem(lax.axis_index(axis), 2)


def swap(block, axis, odd):
    count = lax.axis_size(axis)
    route = [(i, (((i - odd) % count ^ 1) + odd) % count) for i in range(count)]
    return lax.ppermute(block, axis, route)


def hot_group(rows_of, a_s, b_s):
    sub = lax.broadcasted_iota(jnp.int32, (16, NODES), 0)
    second = (sub >= 8).astype(F32)
    subf = sub.astype(F32)
    for g in range(GROUP):
        cell, value = rows_of(g)
        half = (cell >= PAIRS * NZ).astype(jnp.int32)
        high = ((cell - half * (PAIRS * NZ)) >> 7).astype(F32)
        low = ((cell & (NZ - 1)) + half * NZ).astype(F32)
        high = (jnp.broadcast_to(high, (16, NODES)) - second).astype(BF16)
        low = (jnp.broadcast_to(low, (16, NODES)) - subf).astype(BF16)
        lead = value.astype(BF16).astype(F32)
        rest = value - lead
        parts = jnp.concatenate([lead, rest, lead, rest], axis=0).astype(BF16)
        lanes = slice(g * NODES, (g + 1) * NODES)
        for m in range(ROWS // 16):
            a_s[m * 16 : (m + 1) * 16, lanes] = jnp.where(high == BF16(2 * m), parts, BF16(0))
        for m in range(16):
            b_s[m * 16 : (m + 1) * 16, lanes] = jnp.where(low == BF16(16 * m), BF16(1), BF16(0))
    sums = lax.dot_general(a_s[...], b_s[...], (((1,), (1,)), ((), ())), preferred_element_type=F32)
    return sums[:, :NZ], sums[:, NZ:]


def spread_groups(groups, rows_of, acc_in, acc, a_s, b_s):
    left, right = hot_group(lambda g: rows_of(g), a_s, b_s)
    acc[0] = acc_in[0] + left
    acc[1] = acc_in[1] + right

    def group(c, _):
        left, right = hot_group(lambda g: rows_of(c * GROUP + g), a_s, b_s)
        acc[0] += left
        acc[1] += right
        return 0

    lax.fori_loop(1, groups, group, 0)


def first_kernel(
    conc_h, pot_h, eps_h, rec_h, nodes_h, count_h, slots_h, counts_h,
    conc, pot, eps, y0, y1, xr, kept_rec, kept_nodes, acc,
    rec, nodes, count, slots, counts, gone, order, a_s, b_s, sems,
):
    pairs = ((slots_h, slots), (counts_h, counts), (count_h, count), (rec_h, rec), (pot_h, pot), (eps_h, eps), (conc_h, conc), (nodes_h, nodes))
    copies = [pltpu.make_async_copy(a, b, sems.at[n]) for n, (a, b) in enumerate(pairs)]
    for copy in copies:
        copy.start()
    acc[...] = jnp.zeros_like(acc)

    def clear(c, _):
        gone[c] = 0
        return 0

    lax.fori_loop(0, SLOTS, clear, 0, unroll=16)
    for copy in copies[:3]:
        copy.wait()
    for way in range(4):

        def mark(k, _, way=way):
            gone[slots[0, way, k]] = 1
            return 0

        lax.fori_loop(0, counts[0, way], mark, 0)
    live = count[0]

    def gather(c, found):
        order[found] = c
        stays = jnp.logical_and(c < live, gone[c] == 0)
        return found + stays.astype(jnp.int32)

    found = lax.fori_loop(0, SLOTS, gather, 0, unroll=16)
    for copy in copies[3:]:
        copy.wait()

    for n, (axis, odd) in enumerate((("gy", 0), ("gy", 1), ("gx", 0), ("gx", 1))):
        p = parity(axis)
        up = 1 - p if odd == 0 else p
        way = (1 if axis == "gx" else 3) - up
        number = counts[0, way]
        out = (y0, y1, xr.at[0], xr.at[1])[n]
        for k in range(MOVERS):
            row = rec[slots[0, way, k]]
            out[k // 2, (k % 2) * 4 : (k % 2) * 4 + 4] = jnp.where(k < number, row, 0.0)
        if axis == "gx":
            out[X_CONC:X_POT] = conc[:, up * (BX - 1)].reshape(6, 8, NZ)
        else:
            for s in range(3):
                face = jnp.where(up == 1, conc[s, :, BY - 1], conc[s, :, 0])
                out[Y_CONC + 2 * s : Y_CONC + 2 * s + 2] = face.reshape(2, 8, NZ)
            start = pl.multiple_of(up * W, W)
            out[Y_POT:Y_EPS] = pot[:, pl.ds(start, W)]
            out[Y_EPS:Y_END] = eps[:, pl.ds(start, W)]

    def kept_row(at):
        inside = at < found
        slot = jnp.where(inside, order[at], 0)
        return nodes[pl.ds(slot, 1), :], jnp.where(inside, rec[slot], 0.0)

    for r in range(LATER):
        cell, value = kept_row(r)
        kept_nodes[r : r + 1] = cell
        kept_rec[r] = value

    def group(c, _):
        left, right = hot_group(lambda g: kept_row(c * GROUP + g), a_s, b_s)
        acc[0] += left
        acc[1] += right
        return 0

    lax.fori_loop(LATER // GROUP, (found + GROUP - 1) // GROUP, group, 0)


def kept_kernel(acc_in, rec, nodes, acc, a_s, b_s):
    spread_groups(LATER // GROUP, lambda r: (nodes[pl.ds(r, 1), :], rec[r]), acc_in, acc, a_s, b_s)


def pack_x_kernel(xr, pot, eps, y0, y1, s0, s1):
    px, py = parity("gx"), parity("gy")
    for n, (out, up) in enumerate(((s0, 1 - px), (s1, px))):
        out[0:X_POT] = xr[n]
        for first, own, tile in ((X_POT, pot, Y_POT), (X_EPS, eps, Y_EPS)):
            own = own[pl.ds(up * W, W)]
            a, b = y0[pl.ds(tile + up * W, W)], y1[pl.ds(tile + up * W, W)]
            low, high = jnp.where(py == 1, a, b), jnp.where(py == 1, b, a)
            for x in range(W):
                out[first + 4 * x] = low[x]
                out[first + 4 * x + 1] = own[x, 0:8]
                out[first + 4 * x + 2] = own[x, 8:16]
                out[first + 4 * x + 3] = high[x]


def collect(buf0, buf1, way0, way1, nodes, rec, cells):
    for b, (buf, way) in enumerate(((buf0, way0), (buf1, way1))):
        for t in range(8):
            rec[b * 16 + 2 * t] = buf[t, 0:4]
            rec[b * 16 + 2 * t + 1] = buf[t, 4:8]
        cells[b * 16 : (b + 1) * 16] = nodes[0, way]


def arrive_y_kernel(acc_in, y0, y1, nodes, acc, a_s, b_s, rec, cells):
    py = parity("gy")
    collect(y0, y1, 3 - py, 2 + py, nodes, rec, cells)
    spread_groups(2 * MOVERS // GROUP, lambda r: (cells[pl.ds(r, 1), :], rec[r]), acc_in, acc, a_s, b_s)


def face_flux(s, upper, lower, step):
    return -DIFFUSION[s] * ((upper - lower) + (VALENCE[s] * 0.5) * (upper + lower) * step)


def spread_rows(acc, channel, ex, first, number):
    half, row = divmod(ex, WIDE // 2)
    base = (row * WIDE + first) * 8 + channel
    return acc[half, pl.ds(base, number, stride=8)] + acc[half, pl.ds(base + 4, number, stride=8)]


def arrive_x_kernel(acc_in, x0, x1, y0, y1, nodes, conc, pot, conc_next, acc, dens, s0, s1, a_s, b_s, rec, cells, wide):
    px, py = parity("gx"), parity("gy")
    x_low_first, y_low_first = px == 1, py == 1
    collect(x0, x1, 1 - px, px, nodes, rec, cells)
    spread_groups(2 * MOVERS // GROUP, lambda r: (cells[pl.ds(r, 1), :], rec[r]), acc_in, acc, a_s, b_s)

    for f in range(4):
        wide[f, 1 : BX + 1, 8 : 8 + BY] = conc[f] if f < 3 else pot[...]
        if f < 3:
            xa, xb = (x[X_CONC + 2 * f : X_CONC + 2 * f + 2].reshape(BY, NZ) for x in (x0, x1))
            x_low, x_high = jnp.where(x_low_first, xa, xb), jnp.where(x_low_first, xb, xa)
            ya, yb = (y[Y_CONC + 2 * f : Y_CONC + 2 * f + 2].reshape(BX, NZ) for y in (y0, y1))
            y_low, y_high = jnp.where(y_low_first, ya, yb), jnp.where(y_low_first, yb, ya)
        else:
            last, first = X_POT + 4 * (W - 1) + 1, X_POT + 1
            x_low = jnp.where(x_low_first, x0[last : last + 2], x1[last : last + 2]).reshape(BY, NZ)
            x_high = jnp.where(x_low_first, x1[first : first + 2], x0[first : first + 2]).reshape(BY, NZ)
            y_low = jnp.where(y_low_first, y0[Y_POT:Y_EPS, 7], y1[Y_POT:Y_EPS, 7])
            y_high = jnp.where(y_low_first, y1[Y_POT:Y_EPS, 0], y0[Y_POT:Y_EPS, 0])
        wide[f, 0, 8 : 8 + BY] = x_low
        wide[f, BX + 1, 8 : 8 + BY] = x_high
        wide[f, 1 : BX + 1, 7] = y_low
        wide[f, 1 : BX + 1, 8 + BY] = y_high

    dens[...] = jnp.zeros_like(dens)
    for ex in range(WIDE):
        dens[ex, 7 : 7 + WIDE] = spread_rows(acc, 0, ex, 0, WIDE)

    for x in range(BX):
        pc, pe, pw = wide[3, x + 1, 8:24], wide[3, x + 2, 8:24], wide[3, x, 8:24]
        pn, ps = wide[3, x + 1, 9:25], wide[3, x + 1, 7:23]
        pz = pltpu.roll(pc, NZ - 1, 1)
        dx, dw, dn, ds, dz = pe - pc, pc - pw, pn - pc, pc - ps, pz - pc
        total = dens[x + 1, 8:24]
        for s in range(3):
            c = wide[s, x + 1, 8:24]
            flux_x = face_flux(s, wide[s, x + 2, 8:24], c, dx)
            flux_w = face_flux(s, c, wide[s, x, 8:24], dw)
            flux_n = face_flux(s, wide[s, x + 1, 9:25], c, dn)
            flux_s = face_flux(s, c, wide[s, x + 1, 7:23], ds)
            flux_z = face_flux(s, pltpu.roll(c, NZ - 1, 1), c, dz)
            div = ((flux_x - flux_w) + (flux_n - flux_s)) + (flux_z - pltpu.roll(flux_z, 1, 1))
            later = c - TIME_STEP * div
            conc_next[s, x] = later
            total = total + VALENCE[s] * later
        dens[x + 1, 8:24] = total

    for out, up in ((s0, 1 - py), (s1, py)):
        for ex in range(WIDE):
            out[ex * 8 : ex * 8 + 8] = jnp.where(up == 1, dens[ex, 17:25], dens[ex, 7:15])
        for a in range(3):
            for half in range(2):
                rims = []
                for ey in (0, WIDE - 1):
                    base = ey * 8 + a + 1
                    lead = acc[half, pl.ds(base, WIDE // 2, stride=WIDE * 8)]
                    rims.append(lead + acc[half, pl.ds(base + 4, WIDE // 2, stride=WIDE * 8)])
                r = DY_FORCE + a * WIDE + half * (WIDE // 2)
                out[r : r + WIDE // 2] = jnp.where(up == 1, rims[1], rims[0])
        out[DY_FORCE + 54 : DY_END] = jnp.zeros((2, NZ), F32)


def coefficient_kernel(acc, x0, x1, y0, y1, pot, eps, force, phi, xp, xm, yp, ym, zp, zm, inv, ew):
    px, py = parity("gx"), parity("gy")
    x_low_first, y_low_first = px == 1, py == 1
    for c in range(3):
        for ex in range(WIDE):
            force[c, ex] = spread_rows(acc, c + 1, ex, 1, BY)
    for buf, own, x_tile, y_tile in ((phi, pot, X_POT, Y_POT), (ew, eps, X_EPS, Y_EPS)):
        buf[W : W + BX, W : W + BY] = own[...]
        a, b = y0[y_tile : y_tile + BX], y1[y_tile : y_tile + BX]
        buf[W : W + BX, 0:W] = jnp.where(y_low_first, a, b)
        buf[W : W + BX, W + BY : EXT] = jnp.where(y_low_first, b, a)
        a, b = (x[x_tile : x_tile + 4 * W].reshape(W, EXT, NZ) for x in (x0, x1))
        buf[0:W] = jnp.where(x_low_first, a, b)
        buf[W + BX : EXT] = jnp.where(x_low_first, b, a)
    for x in range(1, EXT - 1):
        e = ew[x]
        up, down = e + ew[x + 1], e + ew[x - 1]
        north, south = e + pltpu.roll(e, EXT - 1, 0), e + pltpu.roll(e, 1, 0)
        over = e + pltpu.roll(e, NZ - 1, 1)
        under = pltpu.roll(over, 1, 1)
        scale = 1.0 / ((((up + down) + (north + south)) + (over + under)) + 2.0 * SCREENING)
        xp[x], xm[x] = up * scale, down * scale
        yp[x], ym[x] = north * scale, south * scale
        zp[x], zm[x] = over * scale, under * scale
        inv[x] = 2.0 * scale
    for buf in (xp, xm, yp, ym, zp, zm, inv):
        buf[0] = jnp.zeros((EXT, NZ), F32)
        buf[EXT - 1] = jnp.zeros((EXT, NZ), F32)


def join_y_kernel(dens, force, r0, r1, dext, fcore, s0, s1):
    px, py = parity("gx"), parity("gy")
    low_first = py == 1
    dext[0:7] = jnp.zeros((7, EXT, NZ), F32)
    dext[25:32] = jnp.zeros((7, EXT, NZ), F32)
    for ex in range(WIDE):
        dext[ex + 7] = dens[ex]
        a, b = r0[ex * 8 : ex * 8 + 8], r1[ex * 8 : ex * 8 + 8]
        dext[ex + 7, 1:9] += jnp.where(low_first, a, b)
        dext[ex + 7, 23:31] += jnp.where(low_first, b, a)
    fcore[...] = force[...]
    for c in range(3):
        r = DY_FORCE + c * WIDE
        a, b = r0[r : r + WIDE], r1[r : r + WIDE]
        fcore[c, :, 0] += jnp.where(low_first, a, b)
        fcore[c, :, BY - 1] += jnp.where(low_first, b, a)
    for out, up in ((s0, 1 - px), (s1, px)):
        out[0:DX_FORCE] = dext[pl.ds(7 + 10 * up, 8)].reshape(32, 8, NZ)
        out[DX_FORCE:DX_END] = fcore[:, up * (WIDE - 1)].reshape(6, 8, NZ)


def sweep_kernel(dext, fcore, r0, r1, phi, xp, xm, yp, ym, zp, zm, inv, pot_next, force, phi_a, phi_b, rhs):
    low_first = parity("gx") == 1
    force[...] = fcore[:, 1 : BX + 1]
    a, b = (r[DX_FORCE:DX_END].reshape(3, BY, NZ) for r in (r0, r1))
    force[:, 0] += jnp.where(low_first, a, b)
    force[:, BX - 1] += jnp.where(low_first, b, a)

    for x in range(1, EXT - 1):
        total = dext[x]
        if x < 9 or x > 22:
            t = 4 * (x - 1 if x < 9 else x - 23)
            a, b = (r[t : t + 4].reshape(EXT, NZ) for r in (r0, r1))
            total = total + (jnp.where(low_first, a, b) if x < 9 else jnp.where(low_first, b, a))
        rhs[x] = total * inv[x]

    for k in range(1, SWEEPS + 1):
        old = phi if k == 1 else (phi_a, phi_b)[k % 2]
        new = (phi_a, phi_b)[(k + 1) % 2]
        for x in range(k, EXT - k):
            if k < SWEEPS:
                f = slice(0, EXT)
                here = old[x]
                north, south = pltpu.roll(here, EXT - 1, 0), pltpu.roll(here, 1, 0)
            else:
                f = slice(W, W + BY)
                here = old[x, f]
                north, south = old[x, W + 1 : W + BY + 1], old[x, W - 1 : W + BY - 1]
            total = (xp[x, f] * old[x + 1, f] + xm[x, f] * old[x - 1, f]) + (yp[x, f] * north + ym[x, f] * south)
            total += (zp[x, f] * pltpu.roll(here, NZ - 1, 1) + zm[x, f] * pltpu.roll(here, 1, 1)) + rhs[x, f]
            if k < SWEEPS:
                new[x] = total
            else:
                pot_next[x - W] = total


def shape(*dims):
    return jax.ShapeDtypeStruct(dims, F32)


def call(kernel, name, ins, outs, scratch=(), flops=0):
    moved = 4 * sum(int(o.size) for o in outs)
    return pl.pallas_call(
        kernel,
        name=name,
        in_specs=ins,
        out_specs=[VMEM] * len(outs),
        out_shape=outs,
        scratch_shapes=scratch,
        compiler_params=pltpu.CompilerParams(vmem_limit_bytes=32 << 20),
        cost_estimate=pl.CostEstimate(flops=flops, bytes_accessed=moved, transcendentals=0),
    )


def body(conc, pot, eps, records, count, slots, counts, own_nodes, arrive_nodes):
    hot = [pltpu.VMEM((ROWS, GROUP * NODES), BF16), pltpu.VMEM((2 * NZ, GROUP * NODES), BF16)]
    some = [pltpu.VMEM((2 * MOVERS, CHANNELS, NODES), F32), pltpu.VMEM((2 * MOVERS, NODES), jnp.int32)]
    sums = shape(2, ROWS, NZ)
    row_flops = 2 * ROWS * 2 * NZ * NODES
    field = shape(EXT, EXT, NZ)
    core = shape(BX, BY, NZ)

    conc_v, pot_v, eps_v, a0, a1, xr, kept_rec, kept_nodes, acc = call(
        first_kernel,
        "first",
        [HBM] * 8,
        [
            shape(3, BX, BY, NZ), core, core, shape(Y_END, 8, NZ), shape(Y_END, 8, NZ), shape(2, X_POT, 8, NZ),
            shape(LATER, CHANNELS, NODES), jax.ShapeDtypeStruct((LATER, NODES), jnp.int32), sums,
        ],
        [
            pltpu.VMEM((SLOTS, CHANNELS, NODES), F32), pltpu.VMEM((SLOTS, NODES), jnp.int32), pltpu.SMEM((1,), jnp.int32),
            pltpu.SMEM((1, 4, MOVERS), jnp.int32), pltpu.SMEM((1, 4), jnp.int32), pltpu.SMEM((SLOTS,), jnp.int32),
            pltpu.SMEM((SLOTS + GROUP,), jnp.int32), *hot, pltpu.SemaphoreType.DMA((8,)),
        ],
        flops=row_flops * 32,
    )(conc, pot, eps, records, own_nodes, count, slots, counts)
    y0, y1 = swap(a0, "gy", 0), swap(a1, "gy", 1)
    (acc,) = call(kept_kernel, "spread_kept", [VMEM] * 3, [sums], hot, flops=row_flops * LATER)(acc, kept_rec, kept_nodes)
    b0, b1 = call(pack_x_kernel, "pack_x", [VMEM] * 5, [shape(X_END, 8, NZ)] * 2)(xr, pot_v, eps_v, y0, y1)
    x1, x0 = swap(b1, "gx", 1), swap(b0, "gx", 0)
    (acc,) = call(arrive_y_kernel, "spread_y", [VMEM] * 4, [sums], hot + some, flops=row_flops * 2 * MOVERS)(
        acc, y0, y1, arrive_nodes
    )
    conc_next, acc, dens, c0, c1 = call(
        arrive_x_kernel,
        "spread_x",
        [VMEM] * 8,
        [shape(3, BX, BY, NZ), sums, shape(WIDE, EXT, NZ), shape(DY_END, NZ), shape(DY_END, NZ)],
        hot + some + [pltpu.VMEM((4, WIDE, 32, NZ), F32)],
        flops=row_flops * 2 * MOVERS,
    )(acc, x0, x1, y0, y1, arrive_nodes, conc_v, pot_v)
    r0, r1 = swap(c0, "gy", 0), swap(c1, "gy", 1)
    force, phi, *weights = call(
        coefficient_kernel,
        "coefficients",
        [VMEM] * 7,
        [shape(3, WIDE, BY, NZ)] + [field] * 8,
        [pltpu.VMEM((EXT, EXT, NZ), F32)],
        flops=row_flops * 8,
    )(acc, x0, x1, y0, y1, pot_v, eps_v)
    dext, fcore, e0, e1 = call(
        join_y_kernel, "join_y", [VMEM] * 4, [field, shape(3, WIDE, BY, NZ), shape(DX_END, 8, NZ), shape(DX_END, 8, NZ)]
    )(dens, force, r0, r1)
    g1, g0 = swap(e1, "gx", 1), swap(e0, "gx", 0)
    pot_next, body_force = call(
        sweep_kernel,
        "sweeps",
        [VMEM] * 12,
        [core, shape(3, BX, BY, NZ)],
        [pltpu.VMEM((EXT, EXT, NZ), F32)] * 3,
        flops=20 * SWEEPS * EXT * EXT * NZ,
    )(dext, fcore, g0, g1, phi, *weights)
    return conc_next, pot_next, body_force


def solution(mesh):
    placed = (
        P(None, "gx", "gy", None),
        P("gx", "gy", None),
        P("gx", "gy", None),
        P(("gx", "gy"), None, None),
        P(("gx", "gy")),
        P(("gx", "gy"), None, None),
        P(("gx", "gy"), None),
        P(("gx", "gy"), None),
        P(("gx", "gy"), None, None, None),
    )
    return jax.shard_map(
        body,
        mesh=mesh,
        in_specs=placed,
        out_specs=(P(None, "gx", "gy", None), P("gx", "gy", None), P(None, "gx", "gy", None)),
        check_vma=False,
    )
```

time: 96.2 us -> 86.2 us (0.90)
  the two profiles are of different devices: /device:TPU:24 before, /device:TPU:1 now
where the time goes in v2:
time: 86.2 us; the launch traced here: 85.7 us
  starting transfers between devices  43.7 us (51%)
  Pallas kernels  22.1 us (26%)
  waiting for transfers between devices  12.5 us (15%)
  local copies, waits for them, and re-layouts  5.93 us (7%)
  between operations  1.45 us (2%)
    ppermute x8, starting transfers between devices, swap(): return lax.ppermute(block, axis, route)  43.7 us
    ppermute x8, waiting for transfers between devices, swap(): return lax.ppermute(block, axis, route)  12.5 us
    pallas_call x1, Pallas kernels, body(): call(arrive_x_kernel, 'spread_x', [VMEM] * 8, [shape(3, BX, BY, NZ), sums...  6.31 us
    unnamed x16, local copies, waits for them, and re-layouts  5.93 us
    pallas_call x1, Pallas kernels, body(): call(first_kernel, 'first', [HBM] * 8, [shape(3, BX, BY, NZ), core, core,...  4.77 us
    pallas_call x1, Pallas kernels, body(): call(arrive_y_kernel, 'spread_y', [VMEM] * 4, [sums], hot + some, flops=r...  3.9 us
    pallas_call x1, Pallas kernels, body(): call(kept_kernel, 'spread_kept', [VMEM] * 3, [sums], hot, flops=row_flops...  2.92 us
    pallas_call x1, Pallas kernels, body(): call(sweep_kernel, 'sweeps', [VMEM] * 12, [core, shape(3, BX, BY, NZ)], [...  2.57 us
  transfers between devices with their start and end apart: 8, of which 3 were waited for; matrix products, arithmetic and copies ran while one was open for 0% of the time, Pallas kernels for 10%

profile of v2, /device:TPU:1, one launch (start us, length us, event | category | flops | bytes accessed | tf_op | source)
XLA Modules:
  0.0 85.7 jit_solution(3079809641601331294)
XLA Ops:
  1.3 0.0 copy-start
  1.3 1.0 %copy-done = f32[3,16,16,128]{3,2,1,0:T(8,128)S(1)} copy-done((f32[3,16,16,128]{3,2,1,0:T(8,128)S(1)}, f32[3,16,16,128]{3,2,1,0:T(8,128)}, u32[]{:S(2)}) %copy-start) | copy-done | bytes 393240
  2.3 0.0 copy-start.1
  2.3 0.9 %copy-done.1 = f32[128,4,128]{2,1,0:T(4,128)S(1)} copy-done((f32[128,4,128]{2,1,0:T(4,128)S(1)}, f32[128,4,128]{2,1,0:T(4,128)}, u32[]{:S(2)}) %copy-start.1) | copy-done | bytes 262168
  3.2 0.0 copy-start.2
  3.2 0.9 %copy-done.2 = f32[16,16,128]{2,1,0:T(8,128)S(1)} copy-done((f32[16,16,128]{2,1,0:T(8,128)S(1)}, f32[16,16,128]{2,1,0:T(8,128)}, u32[]{:S(2)}) %copy-start.2) | copy-done | bytes 131096
  4.1 0.0 copy-start.3
  4.1 0.9 %copy-done.3 = f32[16,16,128]{2,1,0:T(8,128)S(1)} copy-done((f32[16,16,128]{2,1,0:T(8,128)S(1)}, f32[16,16,128]{2,1,0:T(8,128)}, u32[]{:S(2)}) %copy-start.3) | copy-done | bytes 131096
  5.0 0.0 copy-start.4
  5.0 0.8 copy-done.4
  5.9 0.0 copy-start.6
  5.9 0.7 copy-done.6
  6.6 0.0 copy-start.7
  6.6 0.7 copy-done.7
  7.2 4.8 %first.1 = (f32[3,16,16,128]{3,2,1,0:T(8,128)S(1)}, f32[16,16,128]{2,1,0:T(8,128)S(1)}, f32[16,16,128]{2,1,0:T(8,128)S(1)}, f32[46,8,128]{2,1,0:T(8,128)S(1)}, f...) custom-call(f32[3,16,16,128]{3,2,1,0:T(8,128)S(1)} %copy-done, ...), custom_call_target="tpu_custom_call" | custom-call | flops 2717908992 | bytes 2535424 | tf_op jit(solution)/shard_map/first/pallas_call | solution.py:374
  12.0 5.4 %collective-permute-start = (f32[46,8,128]{2,1,0:T(8,128)S(1)}, f32[46,8,128]{2,1,0:T(8,128)S(1)}, u32[]{:S(2)}, u32[]{:S(2)}) collective-permute-start(f32[46,8,128]{2,1,0:T(8,128)S(1)} %get-tuple-element.37), channel_id=1, source_target_pairs={{0,1},{1,0},{2,3},{3,2},{4,5},{5,4},{6,7},{7,6},{8,9},{9,8},{10,11... | collective-permute-start | bytes 565256 | tf_op jit(solution)/shard_map/ppermute | solution.py:43
  17.4 4.8 %collective-permute-start.1 = (f32[46,8,128]{2,1,0:T(8,128)S(1)}, f32[46,8,128]{2,1,0:T(8,128)S(1)}, u32[]{:S(2)}, u32[]{:S(2)}) collective-permute-start(f32[46,8,128]{2,1,0:T(8,128)S(1)} %get-tuple-element.38), channel_id=1, source_target_pairs={{0,15},{1,2},{2,1},{3,4},{4,3},{5,6},{6,5},{7,8},{8,7},{9,10},{10,... | collective-permute-start | bytes 565256 | tf_op jit(solution)/shard_map/ppermute | solution.py:43
  22.3 0.0 collective-permute-done.y0
  22.3 5.1 %collective-permute-done.1.y1 = f32[46,8,128]{2,1,0:T(8,128)S(1)} collective-permute-done((f32[46,8,128]{2,1,0:T(8,128)S(1)}, f32[46,8,128]{2,1,0:T(8,128)S(1)}, u32[]{:S(2)}, u32[]{:S(2)}) %collective-permute-start.1) | collective-permute-done | bytes 188448 | tf_op jit(solution)/shard_map/ppermute | solution.py:43
  27.4 8.4 %collective-permute-start.2 = (f32[78,8,128]{2,1,0:T(8,128)S(1)}, f32[78,8,128]{2,1,0:T(8,128)S(1)}, u32[]{:S(2)}, u32[]{:S(2)}) collective-permute-start(f32[78,8,128]{2,1,0:T(8,128)S(1)} %get-tuple-element.42), channel_id=1, source_target_pairs={{0,16},{16,0},{32,48},{48,32},{64,80},{80,64},{96,112},{112,96},{1... | collective-permute-start | bytes 958472 | tf_op jit(solution)/shard_map/ppermute | solution.py:43
  35.8 1.9 %collective-permute-start.3 = (f32[78,8,128]{2,1,0:T(8,128)S(1)}, f32[78,8,128]{2,1,0:T(8,128)S(1)}, u32[]{:S(2)}, u32[]{:S(2)}) collective-permute-start(f32[78,8,128]{2,1,0:T(8,128)S(1)} %get-tuple-element.43), channel_id=1, source_target_pairs={{0,496},{16,32},{32,16},{48,64},{64,48},{80,96},{96,80},{112,128},... | collective-permute-start | bytes 958472 | tf_op jit(solution)/shard_map/ppermute | solution.py:43
  37.8 0.0 copy-start.5
  37.8 2.9 %spread_kept.1.acc_in = f32[2,1296,128]{2,1,0:T(8,128)S(1)} custom-call(f32[2,1296,128]{2,1,0:T(8,128)S(1)} %get-tuple-element.34.acc_in, f32[24,4,128]{2,1,0:T(4,128)S(1)} %get-tuple-element.35.rec, s32[24,128]{1,0:T(8,128)S(1)} %get-tuple-element.36.nodes), custom_call_target="tpu_custom_call" | custom-call | flops 2038431744 | bytes 1327104 | tf_op jit(solution)/shard_map/spread_kept/pallas_call | solution.py:390
  40.7 0.0 copy-done.5
  40.7 3.9 %spread_y.1.acc_in = f32[2,1296,128]{2,1,0:T(8,128)S(1)} custom-call(f32[2,1296,128]{2,1,0:T(8,128)S(1)} %spread_kept.1.acc_in, f32[46,8,128]{2,1,0:T(8,128)S(1)} %collective-permute-done.y0, f32[46,8,128]{2,1,0:T(8,128)S(1)} %collective-permute-done.1.y1, s32[1,4,16,128]{3,2,1,0:T(8,128)S(1)} %copy-done.5), custom_call_target="tpu_custom_call" | custom-call | flops 2717908992 | bytes 1327104 | tf_op jit(solution)/shard_map/spread_y/pallas_call | solution.py:393
  44.6 0.0 collective-permute-done.2.x0
  44.6 0.0 collective-permute-done.3.x1
  44.7 6.3 %spread_x.1 = (f32[3,16,16,128]{3,2,1,0:T(8,128)}, f32[2,1296,128]{2,1,0:T(8,128)S(1)}, f32[18,32,128]{2,1,0:T(8,128)S(1)}, f32[200,128]{1,0:T(8,128)S(1)}, f32[200,128]{1,0:T(8,128)S(1)}) custom-call(f32[2,1296,128]{2,1,0:T(8,128)S(1)} %spread_y.1.acc_in, f32[78,8,128]{2,1,0:T(8,128)S(1)} %collective-permute-done.2.x0, ...), custom_call_target="tpu_custom_call" | custom-call | flops 2717908992 | bytes 2220032 | tf_op jit(solution)/shard_map/spread_x/pallas_call | solution.py:396
  51.0 3.9 %collective-permute-start.4 = (f32[200,128]{1,0:T(8,128)S(1)}, f32[200,128]{1,0:T(8,128)S(1)}, u32[]{:S(2)}, u32[]{:S(2)}) collective-permute-start(f32[200,128]{1,0:T(8,128)S(1)} %get-tuple-element.49), channel_id=1, source_target_pairs={{0,1},{1,0},{2,3},{3,2},{4,5},{5,4},{6,7},{7,6},{8,9},{9,8},{10,11... | collective-permute-start | bytes 307208 | tf_op jit(solution)/shard_map/ppermute | solution.py:43
  54.9 5.1 %collective-permute-start.5 = (f32[200,128]{1,0:T(8,128)S(1)}, f32[200,128]{1,0:T(8,128)S(1)}, u32[]{:S(2)}, u32[]{:S(2)}) collective-permute-start(f32[200,128]{1,0:T(8,128)S(1)} %get-tuple-element.50), channel_id=1, source_target_pairs={{0,15},{1,2},{2,1},{3,4},{4,3},{5,6},{6,5},{7,8},{8,7},{9,10},{10,... | collective-permute-start | bytes 307208 | tf_op jit(solution)/shard_map/ppermute | solution.py:43
  60.0 1.4 %coefficients.1 = (f32[3,18,16,128]{3,2,1,0:T(8,128)S(1)}, f32[32,32,128]{2,1,0:T(8,128)S(1)}, f32[32,32,128]{2,1,0:T(8,128)S(1)}, f32[32,32,128]{2,1,0:T(8,128)...) custom-call(f32[2,1296,128]{2,1,0:T(8,128)S(1)} %get-tuple-element.4, ...), custom_call_target="tpu_custom_call" | custom-call | flops 679477248 | bytes 4636672 | tf_op jit(solution)/shard_map/coefficients/pallas_call | solution.py:405
  61.4 0.0 collective-permute-done.4.r0
  61.4 2.5 %collective-permute-done.5.r1 = f32[200,128]{1,0:T(8,128)S(1)} collective-permute-done((f32[200,128]{1,0:T(8,128)S(1)}, f32[200,128]{1,0:T(8,128)S(1)}, u32[]{:S(2)}, u32[]{:S(2)}) %collective-permute-start.5) | collective-permute-done | bytes 102432 | tf_op jit(solution)/shard_map/ppermute | solution.py:43
  63.9 0.2 join_y.1
  64.1 12.2 %collective-permute-start.6 = (f32[38,8,128]{2,1,0:T(8,128)S(1)}, f32[38,8,128]{2,1,0:T(8,128)S(1)}, u32[]{:S(2)}, u32[]{:S(2)}) collective-permute-start(f32[38,8,128]{2,1,0:T(8,128)S(1)} %get-tuple-element.53), channel_id=1, source_target_pairs={{0,16},{16,0},{32,48},{48,32},{64,80},{80,64},{96,112},{112,96},{1... | collective-permute-start | bytes 466952 | tf_op jit(solution)/shard_map/ppermute | solution.py:43
  76.3 1.9 %collective-permute-start.7 = (f32[38,8,128]{2,1,0:T(8,128)S(1)}, f32[38,8,128]{2,1,0:T(8,128)S(1)}, u32[]{:S(2)}, u32[]{:S(2)}) collective-permute-start(f32[38,8,128]{2,1,0:T(8,128)S(1)} %get-tuple-element.54), channel_id=1, source_target_pairs={{0,496},{16,32},{32,16},{48,64},{64,48},{80,96},{96,80},{112,128},... | collective-permute-start | bytes 466952 | tf_op jit(solution)/shard_map/ppermute | solution.py:43
  78.2 0.0 collective-permute-done.6.r0
  78.2 4.9 %collective-permute-done.7.r1 = f32[38,8,128]{2,1,0:T(8,128)S(1)} collective-permute-done((f32[38,8,128]{2,1,0:T(8,128)S(1)}, f32[38,8,128]{2,1,0:T(8,128)S(1)}, u32[]{:S(2)}, u32[]{:S(2)}) %collective-permute-start.7) | collective-permute-done | bytes 155680 | tf_op jit(solution)/shard_map/ppermute | solution.py:43
  83.2 2.6 %sweeps.1 = (f32[16,16,128]{2,1,0:T(8,128)}, f32[3,16,16,128]{3,2,1,0:T(8,128)}) custom-call(f32[32,32,128]{2,1,0:T(8,128)S(1)} %get-tuple-element.51.dext, f32[3,18,16,128]{3,2,1,0:T(8,128)S(1)} %get-tuple-element.52.fcore, f32[38,8,128]{2,1,0:T(8,128)S(1)} %collective-permute-done.6.r0, f32[38,8,128]{2,1,0:T(8,128)S(1)} %collective-permute-done.7.r1, ...), custom_call_target="tpu_custom_call" | custom-call | flops 20971520 | bytes 524288 | tf_op jit(solution)/shard_map/sweeps/pallas_call | solution.py:417
  (1 shorter events, 0.0 us)
Async XLA Ops:
  1.3 1.0 %copy-start = (f32[3,16,16,128]{3,2,1,0:T(8,128)S(1)}, f32[3,16,16,128]{3,2,1,0:T(8,128)}, u32[]{:S(2)}) copy-start(f32[3,16,16,128]{3,2,1,0:T(8,128)} %conc_h.1) | copy-start | bytes 1179652
  2.3 0.9 %copy-start.1 = (f32[128,4,128]{2,1,0:T(4,128)S(1)}, f32[128,4,128]{2,1,0:T(4,128)}, u32[]{:S(2)}) copy-start(f32[128,4,128]{2,1,0:T(4,128)} %rec_h.1) | copy-start | bytes 786436
  3.2 0.9 %copy-start.2 = (f32[16,16,128]{2,1,0:T(8,128)S(1)}, f32[16,16,128]{2,1,0:T(8,128)}, u32[]{:S(2)}) copy-start(f32[16,16,128]{2,1,0:T(8,128)} %pot_h.1) | copy-start | bytes 393220
  4.1 0.9 %copy-start.3 = (f32[16,16,128]{2,1,0:T(8,128)S(1)}, f32[16,16,128]{2,1,0:T(8,128)}, u32[]{:S(2)}) copy-start(f32[16,16,128]{2,1,0:T(8,128)} %eps_h.1) | copy-start | bytes 393220
  5.0 0.8 copy-start.4
  5.9 0.7 copy-start.6
  6.6 0.7 copy-start.7
  12.0 10.3 %collective-permute-start = (f32[46,8,128]{2,1,0:T(8,128)S(1)}, f32[46,8,128]{2,1,0:T(8,128)S(1)}, u32[]{:S(2)}, u32[]{:S(2)}) collective-permute-start(f32[46,8,128]{2,1,0:T(8,128)S(1)} %get-tuple-element.37), channel_id=1, source_target_pairs={{0,1},{1,0},{2,3},{3,2},{4,5},{5,4},{6,7},{7,6},{8,9},{9,8},{10,11... | collective-permute-start | bytes 565256 | tf_op jit(solution)/shard_map/ppermute | solution.py:43
  17.4 10.0 %collective-permute-start.1 = (f32[46,8,128]{2,1,0:T(8,128)S(1)}, f32[46,8,128]{2,1,0:T(8,128)S(1)}, u32[]{:S(2)}, u32[]{:S(2)}) collective-permute-start(f32[46,8,128]{2,1,0:T(8,128)S(1)} %get-tuple-element.38), channel_id=1, source_target_pairs={{0,15},{1,2},{2,1},{3,4},{4,3},{5,6},{6,5},{7,8},{8,7},{9,10},{10,... | collective-permute-start | bytes 565256 | tf_op jit(solution)/shard_map/ppermute | solution.py:43
  27.4 17.2 %collective-permute-start.2 = (f32[78,8,128]{2,1,0:T(8,128)S(1)}, f32[78,8,128]{2,1,0:T(8,128)S(1)}, u32[]{:S(2)}, u32[]{:S(2)}) collective-permute-start(f32[78,8,128]{2,1,0:T(8,128)S(1)} %get-tuple-element.42), channel_id=1, source_target_pairs={{0,16},{16,0},{32,48},{48,32},{64,80},{80,64},{96,112},{112,96},{1... | collective-permute-start | bytes 958472 | tf_op jit(solution)/shard_map/ppermute | solution.py:43
  35.8 8.8 %collective-permute-start.3 = (f32[78,8,128]{2,1,0:T(8,128)S(1)}, f32[78,8,128]{2,1,0:T(8,128)S(1)}, u32[]{:S(2)}, u32[]{:S(2)}) collective-permute-start(f32[78,8,128]{2,1,0:T(8,128)S(1)} %get-tuple-element.43), channel_id=1, source_target_pairs={{0,496},{16,32},{32,16},{48,64},{64,48},{80,96},{96,80},{112,128},... | collective-permute-start | bytes 958472 | tf_op jit(solution)/shard_map/ppermute | solution.py:43
  37.8 2.9 %copy-start.5 = (s32[1,4,16,128]{3,2,1,0:T(8,128)S(1)}, s32[1,4,16,128]{3,2,1,0:T(8,128)}, u32[]{:S(2)}) copy-start(s32[1,4,16,128]{3,2,1,0:T(8,128)} %nodes.3) | copy-start | bytes 98308
  51.0 10.4 %collective-permute-start.4 = (f32[200,128]{1,0:T(8,128)S(1)}, f32[200,128]{1,0:T(8,128)S(1)}, u32[]{:S(2)}, u32[]{:S(2)}) collective-permute-start(f32[200,128]{1,0:T(8,128)S(1)} %get-tuple-element.49), channel_id=1, source_target_pairs={{0,1},{1,0},{2,3},{3,2},{4,5},{5,4},{6,7},{7,6},{8,9},{9,8},{10,11... | collective-permute-start | bytes 307208 | tf_op jit(solution)/shard_map/ppermute | solution.py:43
  54.9 9.0 %collective-permute-start.5 = (f32[200,128]{1,0:T(8,128)S(1)}, f32[200,128]{1,0:T(8,128)S(1)}, u32[]{:S(2)}, u32[]{:S(2)}) collective-permute-start(f32[200,128]{1,0:T(8,128)S(1)} %get-tuple-element.50), channel_id=1, source_target_pairs={{0,15},{1,2},{2,1},{3,4},{4,3},{5,6},{6,5},{7,8},{8,7},{9,10},{10,... | collective-permute-start | bytes 307208 | tf_op jit(solution)/shard_map/ppermute | solution.py:43
  64.1 14.2 %collective-permute-start.6 = (f32[38,8,128]{2,1,0:T(8,128)S(1)}, f32[38,8,128]{2,1,0:T(8,128)S(1)}, u32[]{:S(2)}, u32[]{:S(2)}) collective-permute-start(f32[38,8,128]{2,1,0:T(8,128)S(1)} %get-tuple-element.53), channel_id=1, source_target_pairs={{0,16},{16,0},{32,48},{48,32},{64,80},{80,64},{96,112},{112,96},{1... | collective-permute-start | bytes 466952 | tf_op jit(solution)/shard_map/ppermute | solution.py:43
  76.3 6.8 %collective-permute-start.7 = (f32[38,8,128]{2,1,0:T(8,128)S(1)}, f32[38,8,128]{2,1,0:T(8,128)S(1)}, u32[]{:S(2)}, u32[]{:S(2)}) collective-permute-start(f32[38,8,128]{2,1,0:T(8,128)S(1)} %get-tuple-element.54), channel_id=1, source_target_pairs={{0,496},{16,32},{32,16},{48,64},{64,48},{80,96},{96,80},{112,128},... | collective-permute-start | bytes 466952 | tf_op jit(solution)/shard_map/ppermute | solution.py:43

commit v3 on v2

--- a/solution.py
+++ b/solution.py
@@ -21,7 +21,6 @@
 PAIRS = WIDE * WIDE // 2
 ROWS = PAIRS * 2 * CHANNELS
 GROUP = 8
-LATER = 24
 
 Y_CONC, Y_POT, Y_EPS, Y_END = 8, 14, 30, 46
 X_CONC, X_POT, X_EPS, X_END = 8, 14, 46, 78
@@ -80,12 +79,46 @@
     lax.fori_loop(1, groups, group, 0)
 
 
-def first_kernel(
-    conc_h, pot_h, eps_h, rec_h, nodes_h, count_h, slots_h, counts_h,
-    conc, pot, eps, y0, y1, xr, kept_rec, kept_nodes, acc,
-    rec, nodes, count, slots, counts, gone, order, a_s, b_s, sems,
+def way_of(axis, odd):
+    p = parity(axis)
+    up = 1 - p if odd == 0 else p
+    return up, (1 if axis == "gx" else 3) - up
+
+
+def pack_records(out, rec, slots, number, way):
+    for k in range(MOVERS):
+        row = rec[slots[0, way, k]]
+        out[k // 2, (k % 2) * 4 : (k % 2) * 4 + 4] = jnp.where(k < number, row, 0.0)
+
+
+def first_kernel(conc_h, pot_h, eps_h, rec_h, slots_h, counts_h, s0, s1, conc, rec, slots, counts, sems):
+    copies = [(slots_h, slots), (counts_h, counts), (rec_h, rec), (conc_h, conc)]
+    for odd, out in enumerate((s0, s1)):
+        start = pl.multiple_of(way_of("gy", odd)[0] * W, W)
+        copies.append((pot_h.at[:, pl.ds(start, W)], out.at[pl.ds(Y_POT, BX)]))
+        copies.append((eps_h.at[:, pl.ds(start, W)], out.at[pl.ds(Y_EPS, BX)]))
+    copies = [pltpu.make_async_copy(a, b, sems.at[n]) for n, (a, b) in enumerate(copies)]
+    for copy in copies:
+        copy.start()
+    for copy in copies:
+        copy.wait()
+    for odd, out in enumerate((s0, s1)):
+        up, way = way_of("gy", odd)
+        pack_records(out, rec, slots, counts[0, way], way)
+        for s in range(3):
+            face = jnp.where(up == 1, conc[s, :, BY - 1], conc[s, :, 0])
+            out[Y_CONC + 2 * s : Y_CONC + 2 * s + 2] = face.reshape(2, 8, NZ)
+
+
+def kept_kernel(
+    conc_h, pot_h, eps_h, rec_h, nodes_h, arrive_h, slots_h, counts_h, count,
+    conc, pot, eps, arrive, xr, acc,
+    rec, nodes, slots, counts, gone, order, a_s, b_s, sems,
 ):
-    pairs = ((slots_h, slots), (counts_h, counts), (count_h, count), (rec_h, rec), (pot_h, pot), (eps_h, eps), (conc_h, conc), (nodes_h, nodes))
+    pairs = (
+        (slots_h, slots), (counts_h, counts), (rec_h, rec), (nodes_h, nodes),
+        (conc_h, conc), (pot_h, pot), (eps_h, eps), (arrive_h, arrive),
+    )
     copies = [pltpu.make_async_copy(a, b, sems.at[n]) for n, (a, b) in enumerate(pairs)]
     for copy in copies:
         copy.start()
@@ -96,7 +129,7 @@
         return 0
 
     lax.fori_loop(0, SLOTS, clear, 0, unroll=16)
-    for copy in copies[:3]:
+    for copy in copies[:2]:
         copy.wait()
     for way in range(4):
 
@@ -113,49 +146,26 @@
         return found + stays.astype(jnp.int32)
 
     found = lax.fori_loop(0, SLOTS, gather, 0, unroll=16)
-    for copy in copies[3:]:
+    for copy in copies[2:]:
         copy.wait()
-
-    for n, (axis, odd) in enumerate((("gy", 0), ("gy", 1), ("gx", 0), ("gx", 1))):
-        p = parity(axis)
-        up = 1 - p if odd == 0 else p
-        way = (1 if axis == "gx" else 3) - up
-        number = counts[0, way]
-        out = (y0, y1, xr.at[0], xr.at[1])[n]
-        for k in range(MOVERS):
-            row = rec[slots[0, way, k]]
-            out[k // 2, (k % 2) * 4 : (k % 2) * 4 + 4] = jnp.where(k < number, row, 0.0)
-        if axis == "gx":
-            out[X_CONC:X_POT] = conc[:, up * (BX - 1)].reshape(6, 8, NZ)
-        else:
-            for s in range(3):
-                face = jnp.where(up == 1, conc[s, :, BY - 1], conc[s, :, 0])
-                out[Y_CONC + 2 * s : Y_CONC + 2 * s + 2] = face.reshape(2, 8, NZ)
-            start = pl.multiple_of(up * W, W)
-            out[Y_POT:Y_EPS] = pot[:, pl.ds(start, W)]
-            out[Y_EPS:Y_END] = eps[:, pl.ds(start, W)]
-
-    def kept_row(at):
-        inside = at < found
-        slot = jnp.where(inside, order[at], 0)
-        return nodes[pl.ds(slot, 1), :], jnp.where(inside, rec[slot], 0.0)
-
-    for r in range(LATER):
-        cell, value = kept_row(r)
-        kept_nodes[r : r + 1] = cell
-        kept_rec[r] = value
+    for odd in range(2):
+        up, way = way_of("gx", odd)
+        pack_records(xr.at[odd], rec, slots, counts[0, way], way)
+        xr[odd, X_CONC:X_POT] = conc[:, up * (BX - 1)].reshape(6, 8, NZ)
 
     def group(c, _):
-        left, right = hot_group(lambda g: kept_row(c * GROUP + g), a_s, b_s)
+        def kept_row(g):
+            at = c * GROUP + g
+            inside = at < found
+            slot = jnp.where(inside, order[at], 0)
+            return nodes[pl.ds(slot, 1), :], jnp.where(inside, rec[slot], 0.0)
+
+        left, right = hot_group(kept_row, a_s, b_s)
         acc[0] += left
         acc[1] += right
         return 0
 
-    lax.fori_loop(LATER // GROUP, (found + GROUP - 1) // GROUP, group, 0)
-
-
-def kept_kernel(acc_in, rec, nodes, acc, a_s, b_s):
-    spread_groups(LATER // GROUP, lambda r: (nodes[pl.ds(r, 1), :], rec[r]), acc_in, acc, a_s, b_s)
+    lax.fori_loop(0, (found + GROUP - 1) // GROUP, group, 0)
 
 
 def pack_x_kernel(xr, pot, eps, y0, y1, s0, s1):
@@ -371,27 +381,34 @@
     field = shape(EXT, EXT, NZ)
     core = shape(BX, BY, NZ)
 
-    conc_v, pot_v, eps_v, a0, a1, xr, kept_rec, kept_nodes, acc = call(
+    ins = [pltpu.with_memory_space_constraint(x, pltpu.HBM) for x in (conc, pot, eps, records)]
+    lists = [pltpu.with_memory_space_constraint(x, pltpu.HBM) for x in (slots, counts)]
+    more = [pltpu.with_memory_space_constraint(x, pltpu.HBM) for x in (own_nodes, arrive_nodes)]
+    small = [pltpu.SMEM((1, 4, MOVERS), jnp.int32), pltpu.SMEM((1, 4), jnp.int32)]
+    rec = pltpu.VMEM((SLOTS, CHANNELS, NODES), F32)
+    a0, a1 = call(
         first_kernel,
         "first",
-        [HBM] * 8,
+        [HBM] * 6,
+        [shape(Y_END, 8, NZ)] * 2,
+        [pltpu.VMEM((3, BX, BY, NZ), F32), rec, *small, pltpu.SemaphoreType.DMA((8,))],
+    )(*ins, *lists)
+    y0, y1 = swap(a0, "gy", 0), swap(a1, "gy", 1)
+    conc_v, pot_v, eps_v, arrive_v, xr, acc = call(
+        kept_kernel,
+        "spread_kept",
+        [HBM] * 8 + [SMEM],
+        [shape(3, BX, BY, NZ), core, core, jax.ShapeDtypeStruct((1, 4, MOVERS, NODES), jnp.int32), shape(2, X_POT, 8, NZ), sums],
         [
-            shape(3, BX, BY, NZ), core, core, shape(Y_END, 8, NZ), shape(Y_END, 8, NZ), shape(2, X_POT, 8, NZ),
-            shape(LATER, CHANNELS, NODES), jax.ShapeDtypeStruct((LATER, NODES), jnp.int32), sums,
-        ],
-        [
-            pltpu.VMEM((SLOTS, CHANNELS, NODES), F32), pltpu.VMEM((SLOTS, NODES), jnp.int32), pltpu.SMEM((1,), jnp.int32),
-            pltpu.SMEM((1, 4, MOVERS), jnp.int32), pltpu.SMEM((1, 4), jnp.int32), pltpu.SMEM((SLOTS,), jnp.int32),
+            rec, pltpu.VMEM((SLOTS, NODES), jnp.int32), *small, pltpu.SMEM((SLOTS,), jnp.int32),
             pltpu.SMEM((SLOTS + GROUP,), jnp.int32), *hot, pltpu.SemaphoreType.DMA((8,)),
         ],
-        flops=row_flops * 32,
-    )(conc, pot, eps, records, own_nodes, count, slots, counts)
-    y0, y1 = swap(a0, "gy", 0), swap(a1, "gy", 1)
-    (acc,) = call(kept_kernel, "spread_kept", [VMEM] * 3, [sums], hot, flops=row_flops * LATER)(acc, kept_rec, kept_nodes)
+        flops=row_flops * 64,
+    )(*ins, *more, *lists, count)
     b0, b1 = call(pack_x_kernel, "pack_x", [VMEM] * 5, [shape(X_END, 8, NZ)] * 2)(xr, pot_v, eps_v, y0, y1)
     x1, x0 = swap(b1, "gx", 1), swap(b0, "gx", 0)
     (acc,) = call(arrive_y_kernel, "spread_y", [VMEM] * 4, [sums], hot + some, flops=row_flops * 2 * MOVERS)(
-        acc, y0, y1, arrive_nodes
+        acc, y0, y1, arrive_v
     )
     conc_next, acc, dens, c0, c1 = call(
         arrive_x_kernel,
@@ -400,7 +417,7 @@
         [shape(3, BX, BY, NZ), sums, shape(WIDE, EXT, NZ), shape(DY_END, NZ), shape(DY_END, NZ)],
         hot + some + [pltpu.VMEM((4, WIDE, 32, NZ), F32)],
         flops=row_flops * 2 * MOVERS,
-    )(acc, x0, x1, y0, y1, arrive_nodes, conc_v, pot_v)
+    )(acc, x0, x1, y0, y1, arrive_v, conc_v, pot_v)
     r0, r1 = swap(c0, "gy", 0), swap(c1, "gy", 1)
     force, phi, *weights = call(
         coefficient_kernel,

time: 86.2 us -> 74.8 us (0.87)
  the two profiles are of different devices: /device:TPU:1 before, /device:TPU:24 now
where the time goes in v3:
time: 74.8 us; the launch traced here: 74.4 us
  starting transfers between devices  38.6 us (52%)
  Pallas kernels  22.1 us (30%)
  waiting for transfers between devices  12.4 us (17%)
  between operations  1.41 us (2%)
    ppermute x8, starting transfers between devices, swap(): return lax.ppermute(block, axis, route)  38.6 us
    ppermute x8, waiting for transfers between devices, swap(): return lax.ppermute(block, axis, route)  12.4 us
    pallas_call x1, Pallas kernels, body(): call(kept_kernel, 'spread_kept', [HBM] * 8 + [SMEM], [shape(3, BX, BY, NZ...  6.49 us
    pallas_call x1, Pallas kernels, body(): call(arrive_x_kernel, 'spread_x', [VMEM] * 8, [shape(3, BX, BY, NZ), sums...  6.29 us
    pallas_call x1, Pallas kernels, body(): call(arrive_y_kernel, 'spread_y', [VMEM] * 4, [sums], hot + some, flops=r...  3.88 us
    pallas_call x1, Pallas kernels, body(): call(sweep_kernel, 'sweeps', [VMEM] * 12, [core, shape(3, BX, BY, NZ)], [...  2.57 us
  transfers between devices with their start and end apart: 8, of which 4 were waited for; matrix products, arithmetic and copies ran while one was open for 0% of the time, Pallas kernels for 16%

profile of v3, /device:TPU:24, one launch (start us, length us, event | category | flops | bytes accessed | tf_op | source)
XLA Modules:
  0.0 74.4 jit_solution(14174928189867222924)
XLA Ops:
  0.6 1.3 %first.1 = (f32[46,8,128]{2,1,0:T(8,128)S(1)}, f32[46,8,128]{2,1,0:T(8,128)S(1)}) custom-call(f32[3,16,16,128]{3,2,1,0:T(8,128)} %conc_h.3, f32[16,16,128]{2,1,0:T(8,128)} %pot_h.3, f32[16,16,128]{2,1,0:T(8,128)} %eps_h.3, f32[128,4,128]{2,1,0:T(4,128)} %rec_h.3, s32[1,4,16]{2,1,0:T(4,128)} %slots_h.3, s32[1,4]{1,0:T(1,128)} %counts_h.3), custom_call_target="tpu_custom_call" | custom-call | bytes 376832 | tf_op jit(solution)/shard_map/first/pallas_call | solution.py:389
  1.9 4.9 %collective-permute-start = (f32[46,8,128]{2,1,0:T(8,128)S(1)}, f32[46,8,128]{2,1,0:T(8,128)S(1)}, u32[]{:S(2)}, u32[]{:S(2)}) collective-permute-start(f32[46,8,128]{2,1,0:T(8,128)S(1)} %get-tuple-element.34), channel_id=1, source_target_pairs={{0,1},{1,0},{2,3},{3,2},{4,5},{5,4},{6,7},{7,6},{8,9},{9,8},{10,11... | collective-permute-start | bytes 565256 | tf_op jit(solution)/shard_map/ppermute | solution.py:42
  6.8 2.3 %collective-permute-start.1 = (f32[46,8,128]{2,1,0:T(8,128)S(1)}, f32[46,8,128]{2,1,0:T(8,128)S(1)}, u32[]{:S(2)}, u32[]{:S(2)}) collective-permute-start(f32[46,8,128]{2,1,0:T(8,128)S(1)} %get-tuple-element.35), channel_id=1, source_target_pairs={{0,15},{1,2},{2,1},{3,4},{4,3},{5,6},{6,5},{7,8},{8,7},{9,10},{10,... | collective-permute-start | bytes 565256 | tf_op jit(solution)/shard_map/ppermute | solution.py:42
  9.8 6.5 %spread_kept.1 = (f32[3,16,16,128]{3,2,1,0:T(8,128)S(1)}, f32[16,16,128]{2,1,0:T(8,128)S(1)}, f32[16,16,128]{2,1,0:T(8,128)S(1)}, s32[1,4,16,128]{3,2,1,0:T(8,12...) custom-call(f32[3,16,16,128]{3,2,1,0:T(8,128)} %conc_h.3, f32[16,16,128]{2,1,0:T(8,128)} %pot_h.3, ...), custom_call_target="tpu_custom_call" | custom-call | flops 5435817984 | bytes 2129920 | tf_op jit(solution)/shard_map/spread_kept/pallas_call | solution.py:397
  16.3 0.0 collective-permute-done.y0
  16.3 1.0 %collective-permute-done.1.y1 = f32[46,8,128]{2,1,0:T(8,128)S(1)} collective-permute-done((f32[46,8,128]{2,1,0:T(8,128)S(1)}, f32[46,8,128]{2,1,0:T(8,128)S(1)}, u32[]{:S(2)}, u32[]{:S(2)}) %collective-permute-start.1) | collective-permute-done | bytes 188448 | tf_op jit(solution)/shard_map/ppermute | solution.py:42
  17.4 1.9 %collective-permute-start.2 = (f32[78,8,128]{2,1,0:T(8,128)S(1)}, f32[78,8,128]{2,1,0:T(8,128)S(1)}, u32[]{:S(2)}, u32[]{:S(2)}) collective-permute-start(f32[78,8,128]{2,1,0:T(8,128)S(1)} %get-tuple-element.40), channel_id=1, source_target_pairs={{0,16},{16,0},{32,48},{48,32},{64,80},{80,64},{96,112},{112,96},{1... | collective-permute-start | bytes 958472 | tf_op jit(solution)/shard_map/ppermute | solution.py:42
  19.3 15.8 %collective-permute-start.3 = (f32[78,8,128]{2,1,0:T(8,128)S(1)}, f32[78,8,128]{2,1,0:T(8,128)S(1)}, u32[]{:S(2)}, u32[]{:S(2)}) collective-permute-start(f32[78,8,128]{2,1,0:T(8,128)S(1)} %get-tuple-element.41), channel_id=1, source_target_pairs={{0,496},{16,32},{32,16},{48,64},{64,48},{80,96},{96,80},{112,128},... | collective-permute-start | bytes 958472 | tf_op jit(solution)/shard_map/ppermute | solution.py:42
  35.1 3.9 %spread_y.1.acc_in = f32[2,1296,128]{2,1,0:T(8,128)S(1)} custom-call(f32[2,1296,128]{2,1,0:T(8,128)S(1)} %get-tuple-element.33.acc_in, f32[46,8,128]{2,1,0:T(8,128)S(1)} %collective-permute-done.y0, f32[46,8,128]{2,1,0:T(8,128)S(1)} %collective-permute-done.1.y1, s32[1,4,16,128]{3,2,1,0:T(8,128)S(1)} %get-tuple-element.36.nodes), custom_call_target="tpu_custom_call" | custom-call | flops 2717908992 | bytes 1327104 | tf_op jit(solution)/shard_map/spread_y/pallas_call | solution.py:410
  39.0 0.0 collective-permute-done.2.x0
  39.0 0.8 %collective-permute-done.3.x1 = f32[78,8,128]{2,1,0:T(8,128)S(1)} collective-permute-done((f32[78,8,128]{2,1,0:T(8,128)S(1)}, f32[78,8,128]{2,1,0:T(8,128)S(1)}, u32[]{:S(2)}, u32[]{:S(2)}) %collective-permute-start.3) | collective-permute-done | bytes 319520 | tf_op jit(solution)/shard_map/ppermute | solution.py:42
  39.8 6.3 %spread_x.1 = (f32[3,16,16,128]{3,2,1,0:T(8,128)}, f32[2,1296,128]{2,1,0:T(8,128)S(1)}, f32[18,32,128]{2,1,0:T(8,128)S(1)}, f32[200,128]{1,0:T(8,128)S(1)}, f32[200,128]{1,0:T(8,128)S(1)}) custom-call(f32[2,1296,128]{2,1,0:T(8,128)S(1)} %spread_y.1.acc_in, f32[78,8,128]{2,1,0:T(8,128)S(1)} %collective-permute-done.2.x0, ...), custom_call_target="tpu_custom_call" | custom-call | flops 2717908992 | bytes 2220032 | tf_op jit(solution)/shard_map/spread_x/pallas_call | solution.py:413
  46.1 6.0 %collective-permute-start.4 = (f32[200,128]{1,0:T(8,128)S(1)}, f32[200,128]{1,0:T(8,128)S(1)}, u32[]{:S(2)}, u32[]{:S(2)}) collective-permute-start(f32[200,128]{1,0:T(8,128)S(1)} %get-tuple-element.47), channel_id=1, source_target_pairs={{0,1},{1,0},{2,3},{3,2},{4,5},{5,4},{6,7},{7,6},{8,9},{9,8},{10,11... | collective-permute-start | bytes 307208 | tf_op jit(solution)/shard_map/ppermute | solution.py:42
  52.1 1.9 %collective-permute-start.5 = (f32[200,128]{1,0:T(8,128)S(1)}, f32[200,128]{1,0:T(8,128)S(1)}, u32[]{:S(2)}, u32[]{:S(2)}) collective-permute-start(f32[200,128]{1,0:T(8,128)S(1)} %get-tuple-element.48), channel_id=1, source_target_pairs={{0,15},{1,2},{2,1},{3,4},{4,3},{5,6},{6,5},{7,8},{8,7},{9,10},{10,... | collective-permute-start | bytes 307208 | tf_op jit(solution)/shard_map/ppermute | solution.py:42
  54.0 1.4 %coefficients.1 = (f32[3,18,16,128]{3,2,1,0:T(8,128)S(1)}, f32[32,32,128]{2,1,0:T(8,128)S(1)}, f32[32,32,128]{2,1,0:T(8,128)S(1)}, f32[32,32,128]{2,1,0:T(8,128)...) custom-call(f32[2,1296,128]{2,1,0:T(8,128)S(1)} %get-tuple-element.4, ...), custom_call_target="tpu_custom_call" | custom-call | flops 679477248 | bytes 4636672 | tf_op jit(solution)/shard_map/coefficients/pallas_call | solution.py:422
  55.4 0.0 collective-permute-done.4.r0
  55.4 5.6 %collective-permute-done.5.r1 = f32[200,128]{1,0:T(8,128)S(1)} collective-permute-done((f32[200,128]{1,0:T(8,128)S(1)}, f32[200,128]{1,0:T(8,128)S(1)}, u32[]{:S(2)}, u32[]{:S(2)}) %collective-permute-start.5) | collective-permute-done | bytes 102432 | tf_op jit(solution)/shard_map/ppermute | solution.py:42
  61.1 0.2 join_y.1
  61.3 1.9 %collective-permute-start.6 = (f32[38,8,128]{2,1,0:T(8,128)S(1)}, f32[38,8,128]{2,1,0:T(8,128)S(1)}, u32[]{:S(2)}, u32[]{:S(2)}) collective-permute-start(f32[38,8,128]{2,1,0:T(8,128)S(1)} %get-tuple-element.51), channel_id=1, source_target_pairs={{0,16},{16,0},{32,48},{48,32},{64,80},{80,64},{96,112},{112,96},{1... | collective-permute-start | bytes 466952 | tf_op jit(solution)/shard_map/ppermute | solution.py:42
  63.2 3.7 %collective-permute-start.7 = (f32[38,8,128]{2,1,0:T(8,128)S(1)}, f32[38,8,128]{2,1,0:T(8,128)S(1)}, u32[]{:S(2)}, u32[]{:S(2)}) collective-permute-start(f32[38,8,128]{2,1,0:T(8,128)S(1)} %get-tuple-element.52), channel_id=1, source_target_pairs={{0,496},{16,32},{32,16},{48,64},{64,48},{80,96},{96,80},{112,128},... | collective-permute-start | bytes 466952 | tf_op jit(solution)/shard_map/ppermute | solution.py:42
  66.9 0.0 collective-permute-done.6.r0
  66.9 4.9 %collective-permute-done.7.r1 = f32[38,8,128]{2,1,0:T(8,128)S(1)} collective-permute-done((f32[38,8,128]{2,1,0:T(8,128)S(1)}, f32[38,8,128]{2,1,0:T(8,128)S(1)}, u32[]{:S(2)}, u32[]{:S(2)}) %collective-permute-start.7) | collective-permute-done | bytes 155680 | tf_op jit(solution)/shard_map/ppermute | solution.py:42
  71.8 2.6 %sweeps.1 = (f32[16,16,128]{2,1,0:T(8,128)}, f32[3,16,16,128]{3,2,1,0:T(8,128)}) custom-call(f32[32,32,128]{2,1,0:T(8,128)S(1)} %get-tuple-element.49.dext, f32[3,18,16,128]{3,2,1,0:T(8,128)S(1)} %get-tuple-element.50.fcore, f32[38,8,128]{2,1,0:T(8,128)S(1)} %collective-permute-done.6.r0, f32[38,8,128]{2,1,0:T(8,128)S(1)} %collective-permute-done.7.r1, ...), custom_call_target="tpu_custom_call" | custom-call | flops 20971520 | bytes 524288 | tf_op jit(solution)/shard_map/sweeps/pallas_call | solution.py:434
  (1 shorter events, 0.0 us)
Async XLA Ops:
  1.9 14.4 %collective-permute-start = (f32[46,8,128]{2,1,0:T(8,128)S(1)}, f32[46,8,128]{2,1,0:T(8,128)S(1)}, u32[]{:S(2)}, u32[]{:S(2)}) collective-permute-start(f32[46,8,128]{2,1,0:T(8,128)S(1)} %get-tuple-element.34), channel_id=1, source_target_pairs={{0,1},{1,0},{2,3},{3,2},{4,5},{5,4},{6,7},{7,6},{8,9},{9,8},{10,11... | collective-permute-start | bytes 565256 | tf_op jit(solution)/shard_map/ppermute | solution.py:42
  6.8 10.5 %collective-permute-start.1 = (f32[46,8,128]{2,1,0:T(8,128)S(1)}, f32[46,8,128]{2,1,0:T(8,128)S(1)}, u32[]{:S(2)}, u32[]{:S(2)}) collective-permute-start(f32[46,8,128]{2,1,0:T(8,128)S(1)} %get-tuple-element.35), channel_id=1, source_target_pairs={{0,15},{1,2},{2,1},{3,4},{4,3},{5,6},{6,5},{7,8},{8,7},{9,10},{10,... | collective-permute-start | bytes 565256 | tf_op jit(solution)/shard_map/ppermute | solution.py:42
  17.4 21.7 %collective-permute-start.2 = (f32[78,8,128]{2,1,0:T(8,128)S(1)}, f32[78,8,128]{2,1,0:T(8,128)S(1)}, u32[]{:S(2)}, u32[]{:S(2)}) collective-permute-start(f32[78,8,128]{2,1,0:T(8,128)S(1)} %get-tuple-element.40), channel_id=1, source_target_pairs={{0,16},{16,0},{32,48},{48,32},{64,80},{80,64},{96,112},{112,96},{1... | collective-permute-start | bytes 958472 | tf_op jit(solution)/shard_map/ppermute | solution.py:42
  19.3 20.5 %collective-permute-start.3 = (f32[78,8,128]{2,1,0:T(8,128)S(1)}, f32[78,8,128]{2,1,0:T(8,128)S(1)}, u32[]{:S(2)}, u32[]{:S(2)}) collective-permute-start(f32[78,8,128]{2,1,0:T(8,128)S(1)} %get-tuple-element.41), channel_id=1, source_target_pairs={{0,496},{16,32},{32,16},{48,64},{64,48},{80,96},{96,80},{112,128},... | collective-permute-start | bytes 958472 | tf_op jit(solution)/shard_map/ppermute | solution.py:42
  46.1 9.3 %collective-permute-start.4 = (f32[200,128]{1,0:T(8,128)S(1)}, f32[200,128]{1,0:T(8,128)S(1)}, u32[]{:S(2)}, u32[]{:S(2)}) collective-permute-start(f32[200,128]{1,0:T(8,128)S(1)} %get-tuple-element.47), channel_id=1, source_target_pairs={{0,1},{1,0},{2,3},{3,2},{4,5},{5,4},{6,7},{7,6},{8,9},{9,8},{10,11... | collective-permute-start | bytes 307208 | tf_op jit(solution)/shard_map/ppermute | solution.py:42
  52.1 9.0 %collective-permute-start.5 = (f32[200,128]{1,0:T(8,128)S(1)}, f32[200,128]{1,0:T(8,128)S(1)}, u32[]{:S(2)}, u32[]{:S(2)}) collective-permute-start(f32[200,128]{1,0:T(8,128)S(1)} %get-tuple-element.48), channel_id=1, source_target_pairs={{0,15},{1,2},{2,1},{3,4},{4,3},{5,6},{6,5},{7,8},{8,7},{9,10},{10,... | collective-permute-start | bytes 307208 | tf_op jit(solution)/shard_map/ppermute | solution.py:42
  61.3 5.7 %collective-permute-start.6 = (f32[38,8,128]{2,1,0:T(8,128)S(1)}, f32[38,8,128]{2,1,0:T(8,128)S(1)}, u32[]{:S(2)}, u32[]{:S(2)}) collective-permute-start(f32[38,8,128]{2,1,0:T(8,128)S(1)} %get-tuple-element.51), channel_id=1, source_target_pairs={{0,16},{16,0},{32,48},{48,32},{64,80},{80,64},{96,112},{112,96},{1... | collective-permute-start | bytes 466952 | tf_op jit(solution)/shard_map/ppermute | solution.py:42
  63.2 8.7 %collective-permute-start.7 = (f32[38,8,128]{2,1,0:T(8,128)S(1)}, f32[38,8,128]{2,1,0:T(8,128)S(1)}, u32[]{:S(2)}, u32[]{:S(2)}) collective-permute-start(f32[38,8,128]{2,1,0:T(8,128)S(1)} %get-tuple-element.52), channel_id=1, source_target_pairs={{0,496},{16,32},{32,16},{48,64},{64,48},{80,96},{96,80},{112,128},... | collective-permute-start | bytes 466952 | tf_op jit(solution)/shard_map/ppermute | solution.py:42

commit v4 on v3

--- a/solution.py
+++ b/solution.py
@@ -21,9 +21,11 @@
 PAIRS = WIDE * WIDE // 2
 ROWS = PAIRS * 2 * CHANNELS
 GROUP = 8
-
-Y_CONC, Y_POT, Y_EPS, Y_END = 8, 14, 30, 46
-X_CONC, X_POT, X_EPS, X_END = 8, 14, 46, 78
+EARLY = 5
+STORE = SLOTS + GROUP
+
+Y_CONC, Y_POT, Y_EPS, Y_NUM, Y_END = 8, 14, 30, 46, 47
+X_CONC, X_POT, X_EPS, X_NUM, X_END = 8, 14, 46, 78, 79
 DY_FORCE, DY_END = WIDE * W, WIDE * W + 56
 DX_FORCE, DX_END = 32, 38
 
@@ -42,12 +44,12 @@
     return lax.ppermute(block, axis, route)
 
 
-def hot_group(rows_of, a_s, b_s):
+def hot_group(first, rec, cells, a_s, b_s):
     sub = lax.broadcasted_iota(jnp.int32, (16, NODES), 0)
     second = (sub >= 8).astype(F32)
     subf = sub.astype(F32)
     for g in range(GROUP):
-        cell, value = rows_of(g)
+        cell, value = cells[first + g], rec[first + g]
         half = (cell >= PAIRS * NZ).astype(jnp.int32)
         high = ((cell - half * (PAIRS * NZ)) >> 7).astype(F32)
         low = ((cell & (NZ - 1)) + half * NZ).astype(F32)
@@ -65,18 +67,25 @@
     return sums[:, :NZ], sums[:, NZ:]
 
 
-def spread_groups(groups, rows_of, acc_in, acc, a_s, b_s):
-    left, right = hot_group(lambda g: rows_of(g), a_s, b_s)
-    acc[0] = acc_in[0] + left
-    acc[1] = acc_in[1] + right
-
+def spread_groups(start, stop, rec, cells, acc, a_s, b_s):
     def group(c, _):
-        left, right = hot_group(lambda g: rows_of(c * GROUP + g), a_s, b_s)
+        left, right = hot_group(c * GROUP, rec, cells, a_s, b_s)
         acc[0] += left
         acc[1] += right
         return 0
 
-    lax.fori_loop(1, groups, group, 0)
+    lax.fori_loop(start, stop, group, 0)
+
+
+def number_in(tile):
+    return jnp.max(tile).astype(jnp.int32)
+
+
+def append(total, buf, number_tile, way, nodes, rec, cells):
+    for k in range(MOVERS):
+        rec[total + k] = buf[k // 2, (k % 2) * 4 : (k % 2) * 4 + 4]
+        cells[total + k] = nodes[0, way, k : k + 1]
+    return total + number_in(buf[number_tile])
 
 
 def way_of(axis, odd):
@@ -85,13 +94,14 @@
     return up, (1 if axis == "gx" else 3) - up
 
 
-def pack_records(out, rec, slots, number, way):
+def pack_records(out, rec, slots, number, way, number_tile):
+    out[number_tile] = jnp.full((8, NZ), number.astype(F32))
     for k in range(MOVERS):
         row = rec[slots[0, way, k]]
         out[k // 2, (k % 2) * 4 : (k % 2) * 4 + 4] = jnp.where(k < number, row, 0.0)
 
 
-def first_kernel(conc_h, pot_h, eps_h, rec_h, slots_h, counts_h, s0, s1, conc, rec, slots, counts, sems):
+def first_kernel(conc_h, pot_h, eps_h, rec_h, slots_h, counts_h, s1, s0, conc, rec, slots, counts, sems):
     copies = [(slots_h, slots), (counts_h, counts), (rec_h, rec), (conc_h, conc)]
     for odd, out in enumerate((s0, s1)):
         start = pl.multiple_of(way_of("gy", odd)[0] * W, W)
@@ -104,7 +114,7 @@
         copy.wait()
     for odd, out in enumerate((s0, s1)):
         up, way = way_of("gy", odd)
-        pack_records(out, rec, slots, counts[0, way], way)
+        pack_records(out, rec, slots, counts[0, way], way, Y_NUM)
         for s in range(3):
             face = jnp.where(up == 1, conc[s, :, BY - 1], conc[s, :, 0])
             out[Y_CONC + 2 * s : Y_CONC + 2 * s + 2] = face.reshape(2, 8, NZ)
@@ -112,8 +122,8 @@
 
 def kept_kernel(
     conc_h, pot_h, eps_h, rec_h, nodes_h, arrive_h, slots_h, counts_h, count,
-    conc, pot, eps, arrive, xr, acc,
-    rec, nodes, slots, counts, gone, order, a_s, b_s, sems,
+    conc, pot, eps, arrive, xr, rows, cells, state, acc,
+    rec, nodes, slots, counts, gone, a_s, b_s, sems,
 ):
     pairs = (
         (slots_h, slots), (counts_h, counts), (rec_h, rec), (nodes_h, nodes),
@@ -139,39 +149,29 @@
 
         lax.fori_loop(0, counts[0, way], mark, 0)
     live = count[0]
+    for copy in copies[2:]:
+        copy.wait()
 
     def gather(c, found):
-        order[found] = c
+        rows[found] = rec[c]
+        cells[found] = nodes[pl.ds(c, 1), :]
         stays = jnp.logical_and(c < live, gone[c] == 0)
         return found + stays.astype(jnp.int32)
 
     found = lax.fori_loop(0, SLOTS, gather, 0, unroll=16)
-    for copy in copies[2:]:
-        copy.wait()
+    state[...] = jnp.full((8, NZ), found.astype(F32))
     for odd in range(2):
         up, way = way_of("gx", odd)
-        pack_records(xr.at[odd], rec, slots, counts[0, way], way)
+        pack_records(xr.at[odd], rec, slots, counts[0, way], way, X_POT)
         xr[odd, X_CONC:X_POT] = conc[:, up * (BX - 1)].reshape(6, 8, NZ)
-
-    def group(c, _):
-        def kept_row(g):
-            at = c * GROUP + g
-            inside = at < found
-            slot = jnp.where(inside, order[at], 0)
-            return nodes[pl.ds(slot, 1), :], jnp.where(inside, rec[slot], 0.0)
-
-        left, right = hot_group(kept_row, a_s, b_s)
-        acc[0] += left
-        acc[1] += right
-        return 0
-
-    lax.fori_loop(0, (found + GROUP - 1) // GROUP, group, 0)
-
-
-def pack_x_kernel(xr, pot, eps, y0, y1, s0, s1):
+    spread_groups(0, jnp.minimum(EARLY, found // GROUP), rows, cells, acc, a_s, b_s)
+
+
+def pack_x_kernel(xr, pot, eps, y0, y1, s1, s0):
     px, py = parity("gx"), parity("gy")
     for n, (out, up) in enumerate(((s0, 1 - px), (s1, px))):
-        out[0:X_POT] = xr[n]
+        out[0:X_POT] = xr[n, 0:X_POT]
+        out[X_NUM] = xr[n, X_POT]
         for first, own, tile in ((X_POT, pot, Y_POT), (X_EPS, eps, Y_EPS)):
             own = own[pl.ds(up * W, W)]
             a, b = y0[pl.ds(tile + up * W, W)], y1[pl.ds(tile + up * W, W)]
@@ -183,18 +183,20 @@
                 out[first + 4 * x + 3] = high[x]
 
 
-def collect(buf0, buf1, way0, way1, nodes, rec, cells):
-    for b, (buf, way) in enumerate(((buf0, way0), (buf1, way1))):
-        for t in range(8):
-            rec[b * 16 + 2 * t] = buf[t, 0:4]
-            rec[b * 16 + 2 * t + 1] = buf[t, 4:8]
-        cells[b * 16 : (b + 1) * 16] = nodes[0, way]
-
-
-def arrive_y_kernel(acc_in, y0, y1, nodes, acc, a_s, b_s, rec, cells):
+def arrive_y_kernel(acc_in, rows_in, cells_in, state, y0, y1, nodes, rows, cells, state_out, acc, a_s, b_s, rec, cell):
     py = parity("gy")
-    collect(y0, y1, 3 - py, 2 + py, nodes, rec, cells)
-    spread_groups(2 * MOVERS // GROUP, lambda r: (cells[pl.ds(r, 1), :], rec[r]), acc_in, acc, a_s, b_s)
+    acc[...] = acc_in[...]
+    rec[0:STORE] = rows_in[...]
+    cell[0:STORE] = cells_in[...]
+    found = number_in(state[...])
+    total = append(found, y0, Y_NUM, 3 - py, nodes, rec, cell)
+    total = append(total, y1, Y_NUM, 2 + py, nodes, rec, cell)
+    done = total // GROUP
+    spread_groups(jnp.minimum(EARLY, found // GROUP), done, rec, cell, acc, a_s, b_s)
+    for g in range(GROUP):
+        rows[g] = rec[done * GROUP + g]
+        cells[g] = cell[done * GROUP + g]
+    state_out[...] = jnp.full((8, NZ), (total - done * GROUP).astype(F32))
 
 
 def face_flux(s, upper, lower, step):
@@ -207,11 +209,22 @@
     return acc[half, pl.ds(base, number, stride=8)] + acc[half, pl.ds(base + 4, number, stride=8)]
 
 
-def arrive_x_kernel(acc_in, x0, x1, y0, y1, nodes, conc, pot, conc_next, acc, dens, s0, s1, a_s, b_s, rec, cells, wide):
+def arrive_x_kernel(
+    acc_in, rows, cells, state, x0, x1, y0, y1, nodes, conc, pot,
+    conc_next, acc, dens, s1, s0,
+    a_s, b_s, rec, cell, wide,
+):
     px, py = parity("gx"), parity("gy")
     x_low_first, y_low_first = px == 1, py == 1
-    collect(x0, x1, 1 - px, px, nodes, rec, cells)
-    spread_groups(2 * MOVERS // GROUP, lambda r: (cells[pl.ds(r, 1), :], rec[r]), acc_in, acc, a_s, b_s)
+    acc[...] = acc_in[...]
+    rec[0:GROUP] = rows[...]
+    cell[0:GROUP] = cells[...]
+    total = append(number_in(state[...]), x0, X_NUM, 1 - px, nodes, rec, cell)
+    total = append(total, x1, X_NUM, px, nodes, rec, cell)
+    for g in range(GROUP):
+        rec[total + g] = jnp.zeros((CHANNELS, NODES), F32)
+        cell[total + g] = jnp.zeros((1, NODES), jnp.int32)
+    spread_groups(0, (total + GROUP - 1) // GROUP, rec, cell, acc, a_s, b_s)
 
     for f in range(4):
         wide[f, 1 : BX + 1, 8 : 8 + BY] = conc[f] if f < 3 else pot[...]
@@ -299,7 +312,7 @@
         buf[EXT - 1] = jnp.zeros((EXT, NZ), F32)
 
 
-def join_y_kernel(dens, force, r0, r1, dext, fcore, s0, s1):
+def join_y_kernel(dens, force, r0, r1, dext, fcore, s1, s0):
     px, py = parity("gx"), parity("gy")
     low_first = py == 1
     dext[0:7] = jnp.zeros((7, EXT, NZ), F32)
@@ -375,7 +388,9 @@
 
 def body(conc, pot, eps, records, count, slots, counts, own_nodes, arrive_nodes):
     hot = [pltpu.VMEM((ROWS, GROUP * NODES), BF16), pltpu.VMEM((2 * NZ, GROUP * NODES), BF16)]
-    some = [pltpu.VMEM((2 * MOVERS, CHANNELS, NODES), F32), pltpu.VMEM((2 * MOVERS, NODES), jnp.int32)]
+    def store(number, kind=pltpu.VMEM):
+        return [kind((number, CHANNELS, NODES), F32), kind((number, 1, NODES), jnp.int32)]
+
     sums = shape(2, ROWS, NZ)
     row_flops = 2 * ROWS * 2 * NZ * NODES
     field = shape(EXT, EXT, NZ)
@@ -386,7 +401,7 @@
     more = [pltpu.with_memory_space_constraint(x, pltpu.HBM) for x in (own_nodes, arrive_nodes)]
     small = [pltpu.SMEM((1, 4, MOVERS), jnp.int32), pltpu.SMEM((1, 4), jnp.int32)]
     rec = pltpu.VMEM((SLOTS, CHANNELS, NODES), F32)
-    a0, a1 = call(
+    a1, a0 = call(
         first_kernel,
         "first",
         [HBM] * 6,
@@ -394,30 +409,35 @@
         [pltpu.VMEM((3, BX, BY, NZ), F32), rec, *small, pltpu.SemaphoreType.DMA((8,))],
     )(*ins, *lists)
     y0, y1 = swap(a0, "gy", 0), swap(a1, "gy", 1)
-    conc_v, pot_v, eps_v, arrive_v, xr, acc = call(
+    conc_v, pot_v, eps_v, arrive_v, xr, rows, cells, state, acc = call(
         kept_kernel,
         "spread_kept",
         [HBM] * 8 + [SMEM],
-        [shape(3, BX, BY, NZ), core, core, jax.ShapeDtypeStruct((1, 4, MOVERS, NODES), jnp.int32), shape(2, X_POT, 8, NZ), sums],
         [
-            rec, pltpu.VMEM((SLOTS, NODES), jnp.int32), *small, pltpu.SMEM((SLOTS,), jnp.int32),
-            pltpu.SMEM((SLOTS + GROUP,), jnp.int32), *hot, pltpu.SemaphoreType.DMA((8,)),
+            shape(3, BX, BY, NZ), core, core, jax.ShapeDtypeStruct((1, 4, MOVERS, NODES), jnp.int32),
+            shape(2, X_POT + 1, 8, NZ), *store(STORE, jax.ShapeDtypeStruct), shape(8, NZ), sums,
         ],
-        flops=row_flops * 64,
+        [rec, pltpu.VMEM((SLOTS, NODES), jnp.int32), *small, pltpu.SMEM((SLOTS,), jnp.int32), *hot, pltpu.SemaphoreType.DMA((8,))],
+        flops=row_flops * EARLY * GROUP,
     )(*ins, *more, *lists, count)
-    b0, b1 = call(pack_x_kernel, "pack_x", [VMEM] * 5, [shape(X_END, 8, NZ)] * 2)(xr, pot_v, eps_v, y0, y1)
+    b1, b0 = call(pack_x_kernel, "pack_x", [VMEM] * 5, [shape(X_END, 8, NZ)] * 2)(xr, pot_v, eps_v, y0, y1)
     x1, x0 = swap(b1, "gx", 1), swap(b0, "gx", 0)
-    (acc,) = call(arrive_y_kernel, "spread_y", [VMEM] * 4, [sums], hot + some, flops=row_flops * 2 * MOVERS)(
-        acc, y0, y1, arrive_v
-    )
-    conc_next, acc, dens, c0, c1 = call(
+    rows, cells, state, acc = call(
+        arrive_y_kernel,
+        "spread_y",
+        [VMEM] * 7,
+        [*store(GROUP, jax.ShapeDtypeStruct), shape(8, NZ), sums],
+        hot + store(STORE + 2 * MOVERS + GROUP),
+        flops=row_flops * 48,
+    )(acc, rows, cells, state, y0, y1, arrive_v)
+    conc_next, acc, dens, c1, c0 = call(
         arrive_x_kernel,
         "spread_x",
-        [VMEM] * 8,
+        [VMEM] * 11,
         [shape(3, BX, BY, NZ), sums, shape(WIDE, EXT, NZ), shape(DY_END, NZ), shape(DY_END, NZ)],
-        hot + some + [pltpu.VMEM((4, WIDE, 32, NZ), F32)],
+        hot + store(2 * MOVERS + 2 * GROUP) + [pltpu.VMEM((4, WIDE, 32, NZ), F32)],
         flops=row_flops * 2 * MOVERS,
-    )(acc, x0, x1, y0, y1, arrive_v, conc_v, pot_v)
+    )(acc, rows, cells, state, x0, x1, y0, y1, arrive_v, conc_v, pot_v)
     r0, r1 = swap(c0, "gy", 0), swap(c1, "gy", 1)
     force, phi, *weights = call(
         coefficient_kernel,
@@ -427,7 +447,7 @@
         [pltpu.VMEM((EXT, EXT, NZ), F32)],
         flops=row_flops * 8,
     )(acc, x0, x1, y0, y1, pot_v, eps_v)
-    dext, fcore, e0, e1 = call(
+    dext, fcore, e1, e0 = call(
         join_y_kernel, "join_y", [VMEM] * 4, [field, shape(3, WIDE, BY, NZ), shape(DX_END, 8, NZ), shape(DX_END, 8, NZ)]
     )(dens, force, r0, r1)
     g1, g0 = swap(e1, "gx", 1), swap(e0, "gx", 0)

time: 74.8 us -> 73.3 us (0.980)
  the two profiles are of different devices: /device:TPU:24 before, /device:TPU:56 now
where the time goes in v4:
time: 73.3 us; the launch traced here: 72.9 us
  starting transfers between devices  36.3 us (50%)
  Pallas kernels  21.1 us (29%)
  waiting for transfers between devices  14 us (19%)
  between operations  1.41 us (2%)
    ppermute x8, starting transfers between devices, swap(): return lax.ppermute(block, axis, route)  36.3 us
    ppermute x8, waiting for transfers between devices, swap(): return lax.ppermute(block, axis, route)  14 us
    pallas_call x1, Pallas kernels, body(): call(kept_kernel, 'spread_kept', [HBM] * 8 + [SMEM], [shape(3, BX, BY, NZ...  6.66 us
    pallas_call x1, Pallas kernels, body(): call(arrive_x_kernel, 'spread_x', [VMEM] * 11, [shape(3, BX, BY, NZ), sum...  5.45 us
    pallas_call x1, Pallas kernels, body(): call(arrive_y_kernel, 'spread_y', [VMEM] * 7, [*store(GROUP, jax.ShapeDty...  3.11 us
    pallas_call x1, Pallas kernels, body(): call(sweep_kernel, 'sweeps', [VMEM] * 12, [core, shape(3, BX, BY, NZ)], [...  3.06 us
  transfers between devices with their start and end apart: 8, of which 3 were waited for; matrix products, arithmetic and copies ran while one was open for 0% of the time, Pallas kernels for 15%

profile of v4, /device:TPU:56, one launch (start us, length us, event | category | flops | bytes accessed | tf_op | source)
XLA Modules:
  0.0 72.9 jit_solution(7910001919804098308)
XLA Ops:
  0.6 1.3 %first.1 = (f32[47,8,128]{2,1,0:T(8,128)S(1)}, f32[47,8,128]{2,1,0:T(8,128)S(1)}) custom-call(f32[3,16,16,128]{3,2,1,0:T(8,128)} %conc_h.3, f32[16,16,128]{2,1,0:T(8,128)} %pot_h.3, f32[16,16,128]{2,1,0:T(8,128)} %eps_h.3, f32[128,4,128]{2,1,0:T(4,128)} %rec_h.3, s32[1,4,16]{2,1,0:T(4,128)} %slots_h.3, s32[1,4]{1,0:T(1,128)} %counts_h.3), custom_call_target="tpu_custom_call" | custom-call | bytes 385024 | tf_op jit(solution)/shard_map/first/pallas_call | solution.py:404
  1.9 4.9 %collective-permute-start = (f32[47,8,128]{2,1,0:T(8,128)S(1)}, f32[47,8,128]{2,1,0:T(8,128)S(1)}, u32[]{:S(2)}, u32[]{:S(2)}) collective-permute-start(f32[47,8,128]{2,1,0:T(8,128)S(1)} %get-tuple-element.44), channel_id=1, source_target_pairs={{0,1},{1,0},{2,3},{3,2},{4,5},{5,4},{6,7},{7,6},{8,9},{9,8},{10,11... | collective-permute-start | bytes 577544 | tf_op jit(solution)/shard_map/ppermute | solution.py:44
  6.8 3.2 %collective-permute-start.1 = (f32[47,8,128]{2,1,0:T(8,128)S(1)}, f32[47,8,128]{2,1,0:T(8,128)S(1)}, u32[]{:S(2)}, u32[]{:S(2)}) collective-permute-start(f32[47,8,128]{2,1,0:T(8,128)S(1)} %get-tuple-element.45), channel_id=1, source_target_pairs={{0,15},{1,2},{2,1},{3,4},{4,3},{5,6},{6,5},{7,8},{8,7},{9,10},{10,... | collective-permute-start | bytes 577544 | tf_op jit(solution)/shard_map/ppermute | solution.py:44
  10.7 6.7 %spread_kept.1 = (f32[3,16,16,128]{3,2,1,0:T(8,128)S(1)}, f32[16,16,128]{2,1,0:T(8,128)S(1)}, f32[16,16,128]{2,1,0:T(8,128)S(1)}, s32[1,4,16,128]{3,2,1,0:T(8,12...) custom-call(f32[3,16,16,128]{3,2,1,0:T(8,128)} %conc_h.3, ...), custom_call_target="tpu_custom_call" | custom-call | flops 3397386240 | bytes 2490368 | tf_op jit(solution)/shard_map/spread_kept/pallas_call | solution.py:412
  17.4 0.0 collective-permute-done.y0
  17.4 0.0 collective-permute-done.1.y1
  17.4 0.1 pack_x.1
  17.5 1.9 %collective-permute-start.2 = (f32[79,8,128]{2,1,0:T(8,128)S(1)}, f32[79,8,128]{2,1,0:T(8,128)S(1)}, u32[]{:S(2)}, u32[]{:S(2)}) collective-permute-start(f32[79,8,128]{2,1,0:T(8,128)S(1)} %get-tuple-element.54), channel_id=1, source_target_pairs={{0,16},{16,0},{32,48},{48,32},{64,80},{80,64},{96,112},{112,96},{1... | collective-permute-start | bytes 970760 | tf_op jit(solution)/shard_map/ppermute | solution.py:44
  19.4 12.0 %collective-permute-start.3 = (f32[79,8,128]{2,1,0:T(8,128)S(1)}, f32[79,8,128]{2,1,0:T(8,128)S(1)}, u32[]{:S(2)}, u32[]{:S(2)}) collective-permute-start(f32[79,8,128]{2,1,0:T(8,128)S(1)} %get-tuple-element.55), channel_id=1, source_target_pairs={{0,496},{16,32},{32,16},{48,64},{64,48},{80,96},{96,80},{112,128},... | collective-permute-start | bytes 970760 | tf_op jit(solution)/shard_map/ppermute | solution.py:44
  31.4 3.1 %spread_y.1 = (f32[8,4,128]{2,1,0:T(4,128)S(1)}, s32[8,1,128]{2,1,0:T(1,128)S(1)}, f32[8,128]{1,0:T(8,128)S(1)}, f32[2,1296,128]{2,1,0:T(8,128)S(1)}) custom-call(f32[2,1296,128]{2,1,0:T(8,128)S(1)} %get-tuple-element.40.acc_in, f32[136,4,128]{2,1,0:T(4,128)S(1)} %get-tuple-element.41.rows_in, s32[136,1,128]{2,1,0:T(1,128)S(1)} %get-tuple-element.42.cells_in, ...), custom_call_target="tpu_custom_call" | custom-call | flops 4076863488 | bytes 1351680 | tf_op jit(solution)/shard_map/spread_y/pallas_call | solution.py:425
  34.5 0.0 collective-permute-done.2.x0
  34.5 1.6 %collective-permute-done.3.x1 = f32[79,8,128]{2,1,0:T(8,128)S(1)} collective-permute-done((f32[79,8,128]{2,1,0:T(8,128)S(1)}, f32[79,8,128]{2,1,0:T(8,128)S(1)}, u32[]{:S(2)}, u32[]{:S(2)}) %collective-permute-start.3) | collective-permute-done | bytes 323616 | tf_op jit(solution)/shard_map/ppermute | solution.py:44
  36.1 5.5 %spread_x.1 = (f32[3,16,16,128]{3,2,1,0:T(8,128)}, f32[2,1296,128]{2,1,0:T(8,128)S(1)}, f32[18,32,128]{2,1,0:T(8,128)S(1)}, f32[200,128]{1,0:T(8,128)S(1)}, f32[200,128]{1,0:T(8,128)S(1)}) custom-call(f32[2,1296,128]{2,1,0:T(8,128)S(1)} %get-tuple-element.47.acc_in, f32[8,4,128]{2,1,0:T(4,128)S(1)} %get-tuple-element.48.rows, ...), custom_call_target="tpu_custom_call" | custom-call | flops 2717908992 | bytes 2220032 | tf_op jit(solution)/shard_map/spread_x/pallas_call | solution.py:433
  41.5 8.5 %collective-permute-start.4 = (f32[200,128]{1,0:T(8,128)S(1)}, f32[200,128]{1,0:T(8,128)S(1)}, u32[]{:S(2)}, u32[]{:S(2)}) collective-permute-start(f32[200,128]{1,0:T(8,128)S(1)} %get-tuple-element.61), channel_id=1, source_target_pairs={{0,1},{1,0},{2,3},{3,2},{4,5},{5,4},{6,7},{7,6},{8,9},{9,8},{10,11... | collective-permute-start | bytes 307208 | tf_op jit(solution)/shard_map/ppermute | solution.py:44
  50.1 1.9 %collective-permute-start.5 = (f32[200,128]{1,0:T(8,128)S(1)}, f32[200,128]{1,0:T(8,128)S(1)}, u32[]{:S(2)}, u32[]{:S(2)}) collective-permute-start(f32[200,128]{1,0:T(8,128)S(1)} %get-tuple-element.62), channel_id=1, source_target_pairs={{0,15},{1,2},{2,1},{3,4},{4,3},{5,6},{6,5},{7,8},{8,7},{9,10},{10,... | collective-permute-start | bytes 307208 | tf_op jit(solution)/shard_map/ppermute | solution.py:44
  52.0 1.4 %coefficients.1 = (f32[3,18,16,128]{3,2,1,0:T(8,128)S(1)}, f32[32,32,128]{2,1,0:T(8,128)S(1)}, f32[32,32,128]{2,1,0:T(8,128)S(1)}, f32[32,32,128]{2,1,0:T(8,128)...) custom-call(f32[2,1296,128]{2,1,0:T(8,128)S(1)} %get-tuple-element.5, ...), custom_call_target="tpu_custom_call" | custom-call | flops 679477248 | bytes 4636672 | tf_op jit(solution)/shard_map/coefficients/pallas_call | solution.py:442
  53.4 0.0 collective-permute-done.4.r0
  53.4 5.7 %collective-permute-done.5.r1 = f32[200,128]{1,0:T(8,128)S(1)} collective-permute-done((f32[200,128]{1,0:T(8,128)S(1)}, f32[200,128]{1,0:T(8,128)S(1)}, u32[]{:S(2)}, u32[]{:S(2)}) %collective-permute-start.5) | collective-permute-done | bytes 102432 | tf_op jit(solution)/shard_map/ppermute | solution.py:44
  59.0 0.2 join_y.1
  59.2 1.9 %collective-permute-start.6 = (f32[38,8,128]{2,1,0:T(8,128)S(1)}, f32[38,8,128]{2,1,0:T(8,128)S(1)}, u32[]{:S(2)}, u32[]{:S(2)}) collective-permute-start(f32[38,8,128]{2,1,0:T(8,128)S(1)} %get-tuple-element.65), channel_id=1, source_target_pairs={{0,16},{16,0},{32,48},{48,32},{64,80},{80,64},{96,112},{112,96},{1... | collective-permute-start | bytes 466952 | tf_op jit(solution)/shard_map/ppermute | solution.py:44
  61.1 1.9 %collective-permute-start.7 = (f32[38,8,128]{2,1,0:T(8,128)S(1)}, f32[38,8,128]{2,1,0:T(8,128)S(1)}, u32[]{:S(2)}, u32[]{:S(2)}) collective-permute-start(f32[38,8,128]{2,1,0:T(8,128)S(1)} %get-tuple-element.66), channel_id=1, source_target_pairs={{0,496},{16,32},{32,16},{48,64},{64,48},{80,96},{96,80},{112,128},... | collective-permute-start | bytes 466952 | tf_op jit(solution)/shard_map/ppermute | solution.py:44
  63.1 0.0 collective-permute-done.6.r0
  63.1 6.7 %collective-permute-done.7.r1 = f32[38,8,128]{2,1,0:T(8,128)S(1)} collective-permute-done((f32[38,8,128]{2,1,0:T(8,128)S(1)}, f32[38,8,128]{2,1,0:T(8,128)S(1)}, u32[]{:S(2)}, u32[]{:S(2)}) %collective-permute-start.7) | collective-permute-done | bytes 155680 | tf_op jit(solution)/shard_map/ppermute | solution.py:44
  69.8 3.1 %sweeps.1 = (f32[16,16,128]{2,1,0:T(8,128)}, f32[3,16,16,128]{3,2,1,0:T(8,128)}) custom-call(f32[32,32,128]{2,1,0:T(8,128)S(1)} %get-tuple-element.63.dext, f32[3,18,16,128]{3,2,1,0:T(8,128)S(1)} %get-tuple-element.64.fcore, f32[38,8,128]{2,1,0:T(8,128)S(1)} %collective-permute-done.6.r0, f32[38,8,128]{2,1,0:T(8,128)S(1)} %collective-permute-done.7.r1, ...), custom_call_target="tpu_custom_call" | custom-call | flops 20971520 | bytes 524288 | tf_op jit(solution)/shard_map/sweeps/pallas_call | solution.py:454
Async XLA Ops:
  1.9 15.5 %collective-permute-start = (f32[47,8,128]{2,1,0:T(8,128)S(1)}, f32[47,8,128]{2,1,0:T(8,128)S(1)}, u32[]{:S(2)}, u32[]{:S(2)}) collective-permute-start(f32[47,8,128]{2,1,0:T(8,128)S(1)} %get-tuple-element.44), channel_id=1, source_target_pairs={{0,1},{1,0},{2,3},{3,2},{4,5},{5,4},{6,7},{7,6},{8,9},{9,8},{10,11... | collective-permute-start | bytes 577544 | tf_op jit(solution)/shard_map/ppermute | solution.py:44
  6.8 10.6 %collective-permute-start.1 = (f32[47,8,128]{2,1,0:T(8,128)S(1)}, f32[47,8,128]{2,1,0:T(8,128)S(1)}, u32[]{:S(2)}, u32[]{:S(2)}) collective-permute-start(f32[47,8,128]{2,1,0:T(8,128)S(1)} %get-tuple-element.45), channel_id=1, source_target_pairs={{0,15},{1,2},{2,1},{3,4},{4,3},{5,6},{6,5},{7,8},{8,7},{9,10},{10,... | collective-permute-start | bytes 577544 | tf_op jit(solution)/shard_map/ppermute | solution.py:44
  17.5 17.0 %collective-permute-start.2 = (f32[79,8,128]{2,1,0:T(8,128)S(1)}, f32[79,8,128]{2,1,0:T(8,128)S(1)}, u32[]{:S(2)}, u32[]{:S(2)}) collective-permute-start(f32[79,8,128]{2,1,0:T(8,128)S(1)} %get-tuple-element.54), channel_id=1, source_target_pairs={{0,16},{16,0},{32,48},{48,32},{64,80},{80,64},{96,112},{112,96},{1... | collective-permute-start | bytes 970760 | tf_op jit(solution)/shard_map/ppermute | solution.py:44
  19.4 16.7 %collective-permute-start.3 = (f32[79,8,128]{2,1,0:T(8,128)S(1)}, f32[79,8,128]{2,1,0:T(8,128)S(1)}, u32[]{:S(2)}, u32[]{:S(2)}) collective-permute-start(f32[79,8,128]{2,1,0:T(8,128)S(1)} %get-tuple-element.55), channel_id=1, source_target_pairs={{0,496},{16,32},{32,16},{48,64},{64,48},{80,96},{96,80},{112,128},... | collective-permute-start | bytes 970760 | tf_op jit(solution)/shard_map/ppermute | solution.py:44
  41.5 11.8 %collective-permute-start.4 = (f32[200,128]{1,0:T(8,128)S(1)}, f32[200,128]{1,0:T(8,128)S(1)}, u32[]{:S(2)}, u32[]{:S(2)}) collective-permute-start(f32[200,128]{1,0:T(8,128)S(1)} %get-tuple-element.61), channel_id=1, source_target_pairs={{0,1},{1,0},{2,3},{3,2},{4,5},{5,4},{6,7},{7,6},{8,9},{9,8},{10,11... | collective-permute-start | bytes 307208 | tf_op jit(solution)/shard_map/ppermute | solution.py:44
  50.1 9.0 %collective-permute-start.5 = (f32[200,128]{1,0:T(8,128)S(1)}, f32[200,128]{1,0:T(8,128)S(1)}, u32[]{:S(2)}, u32[]{:S(2)}) collective-permute-start(f32[200,128]{1,0:T(8,128)S(1)} %get-tuple-element.62), channel_id=1, source_target_pairs={{0,15},{1,2},{2,1},{3,4},{4,3},{5,6},{6,5},{7,8},{8,7},{9,10},{10,... | collective-permute-start | bytes 307208 | tf_op jit(solution)/shard_map/ppermute | solution.py:44
  59.2 3.9 %collective-permute-start.6 = (f32[38,8,128]{2,1,0:T(8,128)S(1)}, f32[38,8,128]{2,1,0:T(8,128)S(1)}, u32[]{:S(2)}, u32[]{:S(2)}) collective-permute-start(f32[38,8,128]{2,1,0:T(8,128)S(1)} %get-tuple-element.65), channel_id=1, source_target_pairs={{0,16},{16,0},{32,48},{48,32},{64,80},{80,64},{96,112},{112,96},{1... | collective-permute-start | bytes 466952 | tf_op jit(solution)/shard_map/ppermute | solution.py:44
  61.1 8.7 %collective-permute-start.7 = (f32[38,8,128]{2,1,0:T(8,128)S(1)}, f32[38,8,128]{2,1,0:T(8,128)S(1)}, u32[]{:S(2)}, u32[]{:S(2)}) collective-permute-start(f32[38,8,128]{2,1,0:T(8,128)S(1)} %get-tuple-element.66), channel_id=1, source_target_pairs={{0,496},{16,32},{32,16},{48,64},{64,48},{80,96},{96,80},{112,128},... | collective-permute-start | bytes 466952 | tf_op jit(solution)/shard_map/ppermute | solution.py:44

commit v5 on v4

--- a/solution.py
+++ b/solution.py
@@ -21,13 +21,14 @@
 PAIRS = WIDE * WIDE // 2
 ROWS = PAIRS * 2 * CHANNELS
 GROUP = 8
-EARLY = 5
+EARLY = 7
 STORE = SLOTS + GROUP
 
 Y_CONC, Y_POT, Y_EPS, Y_NUM, Y_END = 8, 14, 30, 46, 47
 X_CONC, X_POT, X_EPS, X_NUM, X_END = 8, 14, 46, 78, 79
 DY_FORCE, DY_END = WIDE * W, WIDE * W + 56
-DX_FORCE, DX_END = 32, 38
+DX_AT = [sum(EXT - 2 - 2 * d for d in range(n)) for n in range(W + 1)]
+DX_FORCE, DX_END = DX_AT[W], DX_AT[W] + 3 * BY
 
 VMEM = pl.BlockSpec(memory_space=pltpu.VMEM)
 SMEM = pl.BlockSpec(memory_space=pltpu.SMEM)
@@ -44,10 +45,11 @@
     return lax.ppermute(block, axis, route)
 
 
-def hot_group(first, rec, cells, a_s, b_s):
+def hot_group(first, rec, cells):
     sub = lax.broadcasted_iota(jnp.int32, (16, NODES), 0)
     second = (sub >= 8).astype(F32)
     subf = sub.astype(F32)
+    left, right = [], []
     for g in range(GROUP):
         cell, value = cells[first + g], rec[first + g]
         half = (cell >= PAIRS * NZ).astype(jnp.int32)
@@ -58,18 +60,16 @@
         lead = value.astype(BF16).astype(F32)
         rest = value - lead
         parts = jnp.concatenate([lead, rest, lead, rest], axis=0).astype(BF16)
-        lanes = slice(g * NODES, (g + 1) * NODES)
-        for m in range(ROWS // 16):
-            a_s[m * 16 : (m + 1) * 16, lanes] = jnp.where(high == BF16(2 * m), parts, BF16(0))
-        for m in range(16):
-            b_s[m * 16 : (m + 1) * 16, lanes] = jnp.where(low == BF16(16 * m), BF16(1), BF16(0))
-    sums = lax.dot_general(a_s[...], b_s[...], (((1,), (1,)), ((), ())), preferred_element_type=F32)
+        left.append(jnp.concatenate([jnp.where(high == BF16(2 * m), parts, BF16(0)) for m in range(ROWS // 16)], axis=0))
+        right.append(jnp.concatenate([jnp.where(low == BF16(16 * m), BF16(1), BF16(0)) for m in range(16)], axis=0))
+    left, right = jnp.concatenate(left, axis=1), jnp.concatenate(right, axis=1)
+    sums = lax.dot_general(left, right, (((1,), (1,)), ((), ())), preferred_element_type=F32)
     return sums[:, :NZ], sums[:, NZ:]
 
 
-def spread_groups(start, stop, rec, cells, acc, a_s, b_s):
+def spread_groups(start, stop, rec, cells, acc):
     def group(c, _):
-        left, right = hot_group(c * GROUP, rec, cells, a_s, b_s)
+        left, right = hot_group(c * GROUP, rec, cells)
         acc[0] += left
         acc[1] += right
         return 0
@@ -101,17 +101,51 @@
         out[k // 2, (k % 2) * 4 : (k % 2) * 4 + 4] = jnp.where(k < number, row, 0.0)
 
 
-def first_kernel(conc_h, pot_h, eps_h, rec_h, slots_h, counts_h, s1, s0, conc, rec, slots, counts, sems):
-    copies = [(slots_h, slots), (counts_h, counts), (rec_h, rec), (conc_h, conc)]
+def first_kernel(
+    conc_h, pot_h, eps_h, rec_h, nodes_h, arrive_h, slots_h, counts_h, count,
+    s1, s0, conc, pot, eps, arrive, xr, rows, cells, state,
+    rec, nodes, slots, counts, gone, sems,
+):
+    copies = [(slots_h, slots), (counts_h, counts), (rec_h, rec), (nodes_h, nodes), (conc_h, conc)]
     for odd, out in enumerate((s0, s1)):
         start = pl.multiple_of(way_of("gy", odd)[0] * W, W)
         copies.append((pot_h.at[:, pl.ds(start, W)], out.at[pl.ds(Y_POT, BX)]))
         copies.append((eps_h.at[:, pl.ds(start, W)], out.at[pl.ds(Y_EPS, BX)]))
+    copies += [(pot_h, pot), (eps_h, eps), (arrive_h, arrive)]
     copies = [pltpu.make_async_copy(a, b, sems.at[n]) for n, (a, b) in enumerate(copies)]
     for copy in copies:
         copy.start()
-    for copy in copies:
+
+    def clear(c, _):
+        gone[c] = 0
+        return 0
+
+    lax.fori_loop(0, SLOTS, clear, 0, unroll=16)
+    for copy in copies[:2]:
         copy.wait()
+    for way in range(4):
+
+        def mark(k, _, way=way):
+            gone[slots[0, way, k]] = 1
+            return 0
+
+        lax.fori_loop(0, counts[0, way], mark, 0)
+    live = count[0]
+    for copy in copies[2:]:
+        copy.wait()
+
+    def gather(c, found):
+        rows[found] = rec[c]
+        cells[found] = nodes[pl.ds(c, 1), :]
+        stays = jnp.logical_and(c < live, gone[c] == 0)
+        return found + stays.astype(jnp.int32)
+
+    found = lax.fori_loop(0, SLOTS, gather, 0, unroll=16)
+    state[...] = jnp.full((8, NZ), found.astype(F32))
+    for odd in range(2):
+        up, way = way_of("gx", odd)
+        pack_records(xr.at[odd], rec, slots, counts[0, way], way, X_POT)
+        xr[odd, X_CONC:X_POT] = conc[:, up * (BX - 1)].reshape(6, 8, NZ)
     for odd, out in enumerate((s0, s1)):
         up, way = way_of("gy", odd)
         pack_records(out, rec, slots, counts[0, way], way, Y_NUM)
@@ -120,54 +154,14 @@
             out[Y_CONC + 2 * s : Y_CONC + 2 * s + 2] = face.reshape(2, 8, NZ)
 
 
-def kept_kernel(
-    conc_h, pot_h, eps_h, rec_h, nodes_h, arrive_h, slots_h, counts_h, count,
-    conc, pot, eps, arrive, xr, rows, cells, state, acc,
-    rec, nodes, slots, counts, gone, a_s, b_s, sems,
-):
-    pairs = (
-        (slots_h, slots), (counts_h, counts), (rec_h, rec), (nodes_h, nodes),
-        (conc_h, conc), (pot_h, pot), (eps_h, eps), (arrive_h, arrive),
-    )
-    copies = [pltpu.make_async_copy(a, b, sems.at[n]) for n, (a, b) in enumerate(pairs)]
-    for copy in copies:
-        copy.start()
+def kept_kernel(rows, cells, state, state_out, acc):
+    state_out[...] = state[...]
     acc[...] = jnp.zeros_like(acc)
-
-    def clear(c, _):
-        gone[c] = 0
-        return 0
-
-    lax.fori_loop(0, SLOTS, clear, 0, unroll=16)
-    for copy in copies[:2]:
-        copy.wait()
-    for way in range(4):
-
-        def mark(k, _, way=way):
-            gone[slots[0, way, k]] = 1
-            return 0
-
-        lax.fori_loop(0, counts[0, way], mark, 0)
-    live = count[0]
-    for copy in copies[2:]:
-        copy.wait()
-
-    def gather(c, found):
-        rows[found] = rec[c]
-        cells[found] = nodes[pl.ds(c, 1), :]
-        stays = jnp.logical_and(c < live, gone[c] == 0)
-        return found + stays.astype(jnp.int32)
-
-    found = lax.fori_loop(0, SLOTS, gather, 0, unroll=16)
-    state[...] = jnp.full((8, NZ), found.astype(F32))
-    for odd in range(2):
-        up, way = way_of("gx", odd)
-        pack_records(xr.at[odd], rec, slots, counts[0, way], way, X_POT)
-        xr[odd, X_CONC:X_POT] = conc[:, up * (BX - 1)].reshape(6, 8, NZ)
-    spread_groups(0, jnp.minimum(EARLY, found // GROUP), rows, cells, acc, a_s, b_s)
-
-
-def pack_x_kernel(xr, pot, eps, y0, y1, s1, s0):
+    spread_groups(0, jnp.minimum(EARLY, number_in(state[...]) // GROUP), rows, cells, acc)
+
+
+def pack_x_kernel(xr, pot, eps, y0, y1, state, s1, s0):
+    del state
     px, py = parity("gx"), parity("gy")
     for n, (out, up) in enumerate(((s0, 1 - px), (s1, px))):
         out[0:X_POT] = xr[n, 0:X_POT]
@@ -183,7 +177,7 @@
                 out[first + 4 * x + 3] = high[x]
 
 
-def arrive_y_kernel(acc_in, rows_in, cells_in, state, y0, y1, nodes, rows, cells, state_out, acc, a_s, b_s, rec, cell):
+def arrive_y_kernel(acc_in, rows_in, cells_in, state, y0, y1, nodes, rows, cells, state_out, acc, rec, cell):
     py = parity("gy")
     acc[...] = acc_in[...]
     rec[0:STORE] = rows_in[...]
@@ -192,7 +186,7 @@
     total = append(found, y0, Y_NUM, 3 - py, nodes, rec, cell)
     total = append(total, y1, Y_NUM, 2 + py, nodes, rec, cell)
     done = total // GROUP
-    spread_groups(jnp.minimum(EARLY, found // GROUP), done, rec, cell, acc, a_s, b_s)
+    spread_groups(jnp.minimum(EARLY, found // GROUP), done, rec, cell, acc)
     for g in range(GROUP):
         rows[g] = rec[done * GROUP + g]
         cells[g] = cell[done * GROUP + g]
@@ -210,9 +204,9 @@
 
 
 def arrive_x_kernel(
-    acc_in, rows, cells, state, x0, x1, y0, y1, nodes, conc, pot,
+    acc_in, rows, cells, state, x1, x0, y0, y1, nodes, conc, pot,
     conc_next, acc, dens, s1, s0,
-    a_s, b_s, rec, cell, wide,
+    rec, cell, wide,
 ):
     px, py = parity("gx"), parity("gy")
     x_low_first, y_low_first = px == 1, py == 1
@@ -224,7 +218,7 @@
     for g in range(GROUP):
         rec[total + g] = jnp.zeros((CHANNELS, NODES), F32)
         cell[total + g] = jnp.zeros((1, NODES), jnp.int32)
-    spread_groups(0, (total + GROUP - 1) // GROUP, rec, cell, acc, a_s, b_s)
+    spread_groups(0, (total + GROUP - 1) // GROUP, rec, cell, acc)
 
     for f in range(4):
         wide[f, 1 : BX + 1, 8 : 8 + BY] = conc[f] if f < 3 else pot[...]
@@ -248,20 +242,21 @@
     for ex in range(WIDE):
         dens[ex, 7 : 7 + WIDE] = spread_rows(acc, 0, ex, 0, WIDE)
 
+    before = [face_flux(s, wide[s, 1, 8:24], wide[s, 0, 8:24], wide[3, 1, 8:24] - wide[3, 0, 8:24]) for s in range(3)]
     for x in range(BX):
-        pc, pe, pw = wide[3, x + 1, 8:24], wide[3, x + 2, 8:24], wide[3, x, 8:24]
+        pc, pe = wide[3, x + 1, 8:24], wide[3, x + 2, 8:24]
         pn, ps = wide[3, x + 1, 9:25], wide[3, x + 1, 7:23]
         pz = pltpu.roll(pc, NZ - 1, 1)
-        dx, dw, dn, ds, dz = pe - pc, pc - pw, pn - pc, pc - ps, pz - pc
+        dx, dn, ds, dz = pe - pc, pn - pc, pc - ps, pz - pc
         total = dens[x + 1, 8:24]
         for s in range(3):
             c = wide[s, x + 1, 8:24]
             flux_x = face_flux(s, wide[s, x + 2, 8:24], c, dx)
-            flux_w = face_flux(s, c, wide[s, x, 8:24], dw)
             flux_n = face_flux(s, wide[s, x + 1, 9:25], c, dn)
             flux_s = face_flux(s, c, wide[s, x + 1, 7:23], ds)
             flux_z = face_flux(s, pltpu.roll(c, NZ - 1, 1), c, dz)
-            div = ((flux_x - flux_w) + (flux_n - flux_s)) + (flux_z - pltpu.roll(flux_z, 1, 1))
+            div = ((flux_x - before[s]) + (flux_n - flux_s)) + (flux_z - pltpu.roll(flux_z, 1, 1))
+            before[s] = flux_x
             later = c - TIME_STEP * div
             conc_next[s, x] = later
             total = total + VALENCE[s] * later
@@ -329,24 +324,26 @@
         fcore[c, :, 0] += jnp.where(low_first, a, b)
         fcore[c, :, BY - 1] += jnp.where(low_first, b, a)
     for out, up in ((s0, 1 - px), (s1, px)):
-        out[0:DX_FORCE] = dext[pl.ds(7 + 10 * up, 8)].reshape(32, 8, NZ)
-        out[DX_FORCE:DX_END] = fcore[:, up * (WIDE - 1)].reshape(6, 8, NZ)
-
-
-def sweep_kernel(dext, fcore, r0, r1, phi, xp, xm, yp, ym, zp, zm, inv, pot_next, force, phi_a, phi_b, rhs):
+        for d in range(W):
+            plane = jnp.where(up == 1, dext[24 - d, d + 1 : 31 - d], dext[7 + d, d + 1 : 31 - d])
+            out[DX_AT[d] : DX_AT[d + 1]] = plane
+        for c in range(3):
+            out[DX_FORCE + c * BY : DX_FORCE + (c + 1) * BY] = fcore[c, up * (WIDE - 1)]
+
+
+def sweep_kernel(dext, fcore, r1, r0, phi, xp, xm, yp, ym, zp, zm, inv, pot_next, force, phi_a, phi_b, rhs):
     low_first = parity("gx") == 1
     force[...] = fcore[:, 1 : BX + 1]
     a, b = (r[DX_FORCE:DX_END].reshape(3, BY, NZ) for r in (r0, r1))
     force[:, 0] += jnp.where(low_first, a, b)
     force[:, BX - 1] += jnp.where(low_first, b, a)
 
-    for x in range(1, EXT - 1):
-        total = dext[x]
-        if x < 9 or x > 22:
-            t = 4 * (x - 1 if x < 9 else x - 23)
-            a, b = (r[t : t + 4].reshape(EXT, NZ) for r in (r0, r1))
-            total = total + (jnp.where(low_first, a, b) if x < 9 else jnp.where(low_first, b, a))
-        rhs[x] = total * inv[x]
+    rhs[1 : EXT - 1] = dext[1 : EXT - 1]
+    for d in range(W):
+        a, b = (r[DX_AT[d] : DX_AT[d + 1]] for r in (r0, r1))
+        rhs[8 - d, d + 1 : 31 - d] += jnp.where(low_first, a, b)
+        rhs[23 + d, d + 1 : 31 - d] += jnp.where(low_first, b, a)
+    rhs[1 : EXT - 1] = rhs[1 : EXT - 1] * inv[1 : EXT - 1]
 
     for k in range(1, SWEEPS + 1):
         old = phi if k == 1 else (phi_a, phi_b)[k % 2]
@@ -387,7 +384,6 @@
 
 
 def body(conc, pot, eps, records, count, slots, counts, own_nodes, arrive_nodes):
-    hot = [pltpu.VMEM((ROWS, GROUP * NODES), BF16), pltpu.VMEM((2 * NZ, GROUP * NODES), BF16)]
     def store(number, kind=pltpu.VMEM):
         return [kind((number, CHANNELS, NODES), F32), kind((number, 1, NODES), jnp.int32)]
 
@@ -401,33 +397,29 @@
     more = [pltpu.with_memory_space_constraint(x, pltpu.HBM) for x in (own_nodes, arrive_nodes)]
     small = [pltpu.SMEM((1, 4, MOVERS), jnp.int32), pltpu.SMEM((1, 4), jnp.int32)]
     rec = pltpu.VMEM((SLOTS, CHANNELS, NODES), F32)
-    a1, a0 = call(
+    a1, a0, conc_v, pot_v, eps_v, arrive_v, xr, rows, cells, state = call(
         first_kernel,
         "first",
-        [HBM] * 6,
-        [shape(Y_END, 8, NZ)] * 2,
-        [pltpu.VMEM((3, BX, BY, NZ), F32), rec, *small, pltpu.SemaphoreType.DMA((8,))],
-    )(*ins, *lists)
-    y0, y1 = swap(a0, "gy", 0), swap(a1, "gy", 1)
-    conc_v, pot_v, eps_v, arrive_v, xr, rows, cells, state, acc = call(
-        kept_kernel,
-        "spread_kept",
         [HBM] * 8 + [SMEM],
         [
-            shape(3, BX, BY, NZ), core, core, jax.ShapeDtypeStruct((1, 4, MOVERS, NODES), jnp.int32),
-            shape(2, X_POT + 1, 8, NZ), *store(STORE, jax.ShapeDtypeStruct), shape(8, NZ), sums,
+            shape(Y_END, 8, NZ), shape(Y_END, 8, NZ), shape(3, BX, BY, NZ), core, core,
+            jax.ShapeDtypeStruct((1, 4, MOVERS, NODES), jnp.int32),
+            shape(2, X_POT + 1, 8, NZ), *store(STORE, jax.ShapeDtypeStruct), shape(8, NZ),
         ],
-        [rec, pltpu.VMEM((SLOTS, NODES), jnp.int32), *small, pltpu.SMEM((SLOTS,), jnp.int32), *hot, pltpu.SemaphoreType.DMA((8,))],
-        flops=row_flops * EARLY * GROUP,
+        [rec, pltpu.VMEM((SLOTS, NODES), jnp.int32), *small, pltpu.SMEM((SLOTS,), jnp.int32), pltpu.SemaphoreType.DMA((12,))],
     )(*ins, *more, *lists, count)
-    b1, b0 = call(pack_x_kernel, "pack_x", [VMEM] * 5, [shape(X_END, 8, NZ)] * 2)(xr, pot_v, eps_v, y0, y1)
+    y0, y1 = swap(a0, "gy", 0), swap(a1, "gy", 1)
+    late, acc = call(kept_kernel, "spread_kept", [VMEM] * 3, [shape(8, NZ), sums], flops=row_flops * EARLY * GROUP)(
+        rows, cells, state
+    )
+    b1, b0 = call(pack_x_kernel, "pack_x", [VMEM] * 6, [shape(X_END, 8, NZ)] * 2)(xr, pot_v, eps_v, y0, y1, late)
     x1, x0 = swap(b1, "gx", 1), swap(b0, "gx", 0)
     rows, cells, state, acc = call(
         arrive_y_kernel,
         "spread_y",
         [VMEM] * 7,
         [*store(GROUP, jax.ShapeDtypeStruct), shape(8, NZ), sums],
-        hot + store(STORE + 2 * MOVERS + GROUP),
+        store(STORE + 2 * MOVERS + GROUP),
         flops=row_flops * 48,
     )(acc, rows, cells, state, y0, y1, arrive_v)
     conc_next, acc, dens, c1, c0 = call(
@@ -435,9 +427,9 @@
         "spread_x",
         [VMEM] * 11,
         [shape(3, BX, BY, NZ), sums, shape(WIDE, EXT, NZ), shape(DY_END, NZ), shape(DY_END, NZ)],
-        hot + store(2 * MOVERS + 2 * GROUP) + [pltpu.VMEM((4, WIDE, 32, NZ), F32)],
+        store(2 * MOVERS + 2 * GROUP) + [pltpu.VMEM((4, WIDE, 32, NZ), F32)],
         flops=row_flops * 2 * MOVERS,
-    )(acc, rows, cells, state, x0, x1, y0, y1, arrive_v, conc_v, pot_v)
+    )(acc, rows, cells, state, x1, x0, y0, y1, arrive_v, conc_v, pot_v)
     r0, r1 = swap(c0, "gy", 0), swap(c1, "gy", 1)
     force, phi, *weights = call(
         coefficient_kernel,
@@ -448,7 +440,7 @@
         flops=row_flops * 8,
     )(acc, x0, x1, y0, y1, pot_v, eps_v)
     dext, fcore, e1, e0 = call(
-        join_y_kernel, "join_y", [VMEM] * 4, [field, shape(3, WIDE, BY, NZ), shape(DX_END, 8, NZ), shape(DX_END, 8, NZ)]
+        join_y_kernel, "join_y", [VMEM] * 4, [field, shape(3, WIDE, BY, NZ), shape(DX_END, NZ), shape(DX_END, NZ)]
     )(dens, force, r0, r1)
     g1, g0 = swap(e1, "gx", 1), swap(e0, "gx", 0)
     pot_next, body_force = call(
@@ -458,7 +450,7 @@
         [core, shape(3, BX, BY, NZ)],
         [pltpu.VMEM((EXT, EXT, NZ), F32)] * 3,
         flops=20 * SWEEPS * EXT * EXT * NZ,
-    )(dext, fcore, g0, g1, phi, *weights)
+    )(dext, fcore, g1, g0, phi, *weights)
     return conc_next, pot_next, body_force
 
 

time: 73.3 us -> 66.9 us (0.913)
  the two profiles are of different devices: /device:TPU:56 before, /device:TPU:60 now
where the time goes in v5:
time: 66.9 us; the launch traced here: 66.5 us
  starting transfers between devices  33.5 us (50%)
  Pallas kernels  20.3 us (30%)
  waiting for transfers between devices  11.3 us (17%)
  between operations  1.41 us (2%)
    ppermute x8, starting transfers between devices, swap(): return lax.ppermute(block, axis, route)  33.5 us
    ppermute x8, waiting for transfers between devices, swap(): return lax.ppermute(block, axis, route)  11.3 us
    pallas_call x1, Pallas kernels, body(): call(arrive_x_kernel, 'spread_x', [VMEM] * 11, [shape(3, BX, BY, NZ), sum...  5.23 us
    pallas_call x1, Pallas kernels, body(): call(kept_kernel, 'spread_kept', [VMEM] * 3, [shape(8, NZ), sums], flops=...  4.65 us
    pallas_call x1, Pallas kernels, body(): call(arrive_y_kernel, 'spread_y', [VMEM] * 7, [*store(GROUP, jax.ShapeDty...  3.79 us
    pallas_call x1, Pallas kernels, body(): call(sweep_kernel, 'sweeps', [VMEM] * 12, [core, shape(3, BX, BY, NZ)], [...  3.08 us
    pallas_call x1, Pallas kernels, body(): call(first_kernel, 'first', [HBM] * 8 + [SMEM], [shape(Y_END, 8, NZ), sha...  1.98 us
    pallas_call x1, Pallas kernels, body(): call(coefficient_kernel, 'coefficients', [VMEM] * 7, [shape(3, WIDE, BY,...  1.36 us
  transfers between devices with their start and end apart: 8, of which 4 were waited for; matrix products, arithmetic and copies ran while one was open for 0% of the time, Pallas kernels for 15%

profile of v5, /device:TPU:60, one launch (start us, length us, event | category | flops | bytes accessed | tf_op | source)
XLA Modules:
  0.0 66.5 jit_solution(3563124114436083560)
XLA Ops:
  1.3 2.0 %first.1 = (f32[47,8,128]{2,1,0:T(8,128)S(1)}, f32[47,8,128]{2,1,0:T(8,128)S(1)}, f32[3,16,16,128]{3,2,1,0:T(8,128)S(1)}, f32[16,16,128]{2,1,0:T(8,128)S(1)}, f3...) custom-call(f32[3,16,16,128]{3,2,1,0:T(8,128)} %conc_h.1, ...), custom_call_target="tpu_custom_call" | custom-call | bytes 1548288 | tf_op jit(solution)/shard_map/first/pallas_call | solution.py:400
  3.3 2.4 %collective-permute-start = (f32[47,8,128]{2,1,0:T(8,128)S(1)}, f32[47,8,128]{2,1,0:T(8,128)S(1)}, u32[]{:S(2)}, u32[]{:S(2)}) collective-permute-start(f32[47,8,128]{2,1,0:T(8,128)S(1)} %get-tuple-element.45), channel_id=1, source_target_pairs={{0,1},{1,0},{2,3},{3,2},{4,5},{5,4},{6,7},{7,6},{8,9},{9,8},{10,11... | collective-permute-start | bytes 577544 | tf_op jit(solution)/shard_map/ppermute | solution.py:45
  5.7 6.5 %collective-permute-start.1 = (f32[47,8,128]{2,1,0:T(8,128)S(1)}, f32[47,8,128]{2,1,0:T(8,128)S(1)}, u32[]{:S(2)}, u32[]{:S(2)}) collective-permute-start(f32[47,8,128]{2,1,0:T(8,128)S(1)} %get-tuple-element.46), channel_id=1, source_target_pairs={{0,15},{1,2},{2,1},{3,4},{4,3},{5,6},{6,5},{7,8},{8,7},{9,10},{10,... | collective-permute-start | bytes 577544 | tf_op jit(solution)/shard_map/ppermute | solution.py:45
  12.2 4.7 %spread_kept.1 = (f32[8,128]{1,0:T(8,128)S(1)}, f32[2,1296,128]{2,1,0:T(8,128)S(1)}) custom-call(f32[136,4,128]{2,1,0:T(4,128)S(1)} %get-tuple-element.41.rows.rows_in, s32[136,1,128]{2,1,0:T(1,128)S(1)} %get-tuple-element.42.cells.cells_in, f32[8,128]{1,0:T(8,128)S(1)} %get-tuple-element.43.state), custom_call_target="tpu_custom_call" | custom-call | flops 4756340736 | bytes 1331200 | tf_op jit(solution)/shard_map/spread_kept/pallas_call | solution.py:412
  16.9 0.0 collective-permute-done.y0
  16.9 0.6 collective-permute-done.1.y1
  17.5 0.1 pack_x.1
  17.5 10.7 %collective-permute-start.2 = (f32[79,8,128]{2,1,0:T(8,128)S(1)}, f32[79,8,128]{2,1,0:T(8,128)S(1)}, u32[]{:S(2)}, u32[]{:S(2)}) collective-permute-start(f32[79,8,128]{2,1,0:T(8,128)S(1)} %get-tuple-element.56), channel_id=1, source_target_pairs={{0,496},{16,32},{32,16},{48,64},{64,48},{80,96},{96,80},{112,128},... | collective-permute-start | bytes 970760 | tf_op jit(solution)/shard_map/ppermute | solution.py:45
  28.3 1.9 %collective-permute-start.3 = (f32[79,8,128]{2,1,0:T(8,128)S(1)}, f32[79,8,128]{2,1,0:T(8,128)S(1)}, u32[]{:S(2)}, u32[]{:S(2)}) collective-permute-start(f32[79,8,128]{2,1,0:T(8,128)S(1)} %get-tuple-element.57), channel_id=1, source_target_pairs={{0,16},{16,0},{32,48},{48,32},{64,80},{80,64},{96,112},{112,96},{1... | collective-permute-start | bytes 970760 | tf_op jit(solution)/shard_map/ppermute | solution.py:45
  30.2 3.8 %spread_y.1 = (f32[8,4,128]{2,1,0:T(4,128)S(1)}, s32[8,1,128]{2,1,0:T(1,128)S(1)}, f32[8,128]{1,0:T(8,128)S(1)}, f32[2,1296,128]{2,1,0:T(8,128)S(1)}) custom-call(f32[2,1296,128]{2,1,0:T(8,128)S(1)} %get-tuple-element.44.acc_in, f32[136,4,128]{2,1,0:T(4,128)S(1)} %get-tuple-element.41.rows.rows_in, s32[136,1,128]{2,1,0:T(1,128)S(1)} %get-tuple-element.42.cells.cells_in, ...), custom_call_target="tpu_custom_call" | custom-call | flops 4076863488 | bytes 1351680 | tf_op jit(solution)/shard_map/spread_y/pallas_call | solution.py:417
  34.0 0.0 collective-permute-done.2.x1
  34.0 0.0 collective-permute-done.3.x0
  34.0 5.2 %spread_x.1 = (f32[3,16,16,128]{3,2,1,0:T(8,128)}, f32[2,1296,128]{2,1,0:T(8,128)S(1)}, f32[18,32,128]{2,1,0:T(8,128)S(1)}, f32[200,128]{1,0:T(8,128)S(1)}, f32[200,128]{1,0:T(8,128)S(1)}) custom-call(f32[2,1296,128]{2,1,0:T(8,128)S(1)} %get-tuple-element.48.acc_in, f32[8,4,128]{2,1,0:T(4,128)S(1)} %get-tuple-element.49.rows, ...), custom_call_target="tpu_custom_call" | custom-call | flops 2717908992 | bytes 2220032 | tf_op jit(solution)/shard_map/spread_x/pallas_call | solution.py:425
  39.2 5.6 %collective-permute-start.4 = (f32[200,128]{1,0:T(8,128)S(1)}, f32[200,128]{1,0:T(8,128)S(1)}, u32[]{:S(2)}, u32[]{:S(2)}) collective-permute-start(f32[200,128]{1,0:T(8,128)S(1)} %get-tuple-element.63), channel_id=1, source_target_pairs={{0,1},{1,0},{2,3},{3,2},{4,5},{5,4},{6,7},{7,6},{8,9},{9,8},{10,11... | collective-permute-start | bytes 307208 | tf_op jit(solution)/shard_map/ppermute | solution.py:45
  44.8 1.9 %collective-permute-start.5 = (f32[200,128]{1,0:T(8,128)S(1)}, f32[200,128]{1,0:T(8,128)S(1)}, u32[]{:S(2)}, u32[]{:S(2)}) collective-permute-start(f32[200,128]{1,0:T(8,128)S(1)} %get-tuple-element.64), channel_id=1, source_target_pairs={{0,15},{1,2},{2,1},{3,4},{4,3},{5,6},{6,5},{7,8},{8,7},{9,10},{10,... | collective-permute-start | bytes 307208 | tf_op jit(solution)/shard_map/ppermute | solution.py:45
  46.8 1.4 %coefficients.1 = (f32[3,18,16,128]{3,2,1,0:T(8,128)S(1)}, f32[32,32,128]{2,1,0:T(8,128)S(1)}, f32[32,32,128]{2,1,0:T(8,128)S(1)}, f32[32,32,128]{2,1,0:T(8,128)...) custom-call(f32[2,1296,128]{2,1,0:T(8,128)S(1)} %get-tuple-element.6, ...), custom_call_target="tpu_custom_call" | custom-call | flops 679477248 | bytes 4636672 | tf_op jit(solution)/shard_map/coefficients/pallas_call | solution.py:434
  48.1 0.2 collective-permute-done.4.r0
  48.3 6.7 %collective-permute-done.5.r1 = f32[200,128]{1,0:T(8,128)S(1)} collective-permute-done((f32[200,128]{1,0:T(8,128)S(1)}, f32[200,128]{1,0:T(8,128)S(1)}, u32[]{:S(2)}, u32[]{:S(2)}) %collective-permute-start.5) | collective-permute-done | bytes 102432 | tf_op jit(solution)/shard_map/ppermute | solution.py:45
  55.0 0.2 join_y.1
  55.2 2.5 %collective-permute-start.6 = (f32[232,128]{1,0:T(8,128)S(1)}, f32[232,128]{1,0:T(8,128)S(1)}, u32[]{:S(2)}, u32[]{:S(2)}) collective-permute-start(f32[232,128]{1,0:T(8,128)S(1)} %get-tuple-element.67), channel_id=1, source_target_pairs={{0,496},{16,32},{32,16},{48,64},{64,48},{80,96},{96,80},{112,128},... | collective-permute-start | bytes 356360 | tf_op jit(solution)/shard_map/ppermute | solution.py:45
  57.7 1.9 %collective-permute-start.7 = (f32[232,128]{1,0:T(8,128)S(1)}, f32[232,128]{1,0:T(8,128)S(1)}, u32[]{:S(2)}, u32[]{:S(2)}) collective-permute-start(f32[232,128]{1,0:T(8,128)S(1)} %get-tuple-element.68), channel_id=1, source_target_pairs={{0,16},{16,0},{32,48},{48,32},{64,80},{80,64},{96,112},{112,96},{1... | collective-permute-start | bytes 356360 | tf_op jit(solution)/shard_map/ppermute | solution.py:45
  59.6 3.8 %collective-permute-done.6.r1 = f32[232,128]{1,0:T(8,128)S(1)} collective-permute-done((f32[232,128]{1,0:T(8,128)S(1)}, f32[232,128]{1,0:T(8,128)S(1)}, u32[]{:S(2)}, u32[]{:S(2)}) %collective-permute-start.6) | collective-permute-done | bytes 118816 | tf_op jit(solution)/shard_map/ppermute | solution.py:45
  63.5 0.0 collective-permute-done.7.r0
  63.5 3.1 %sweeps.1 = (f32[16,16,128]{2,1,0:T(8,128)}, f32[3,16,16,128]{3,2,1,0:T(8,128)}) custom-call(f32[32,32,128]{2,1,0:T(8,128)S(1)} %get-tuple-element.65.dext, f32[3,18,16,128]{3,2,1,0:T(8,128)S(1)} %get-tuple-element.66.fcore, f32[232,128]{1,0:T(8,128)S(1)} %collective-permute-done.6.r1, f32[232,128]{1,0:T(8,128)S(1)} %collective-permute-done.7.r0, ...), custom_call_target="tpu_custom_call" | custom-call | flops 20971520 | bytes 524288 | tf_op jit(solution)/shard_map/sweeps/pallas_call | solution.py:446
Async XLA Ops:
  3.3 13.6 %collective-permute-start = (f32[47,8,128]{2,1,0:T(8,128)S(1)}, f32[47,8,128]{2,1,0:T(8,128)S(1)}, u32[]{:S(2)}, u32[]{:S(2)}) collective-permute-start(f32[47,8,128]{2,1,0:T(8,128)S(1)} %get-tuple-element.45), channel_id=1, source_target_pairs={{0,1},{1,0},{2,3},{3,2},{4,5},{5,4},{6,7},{7,6},{8,9},{9,8},{10,11... | collective-permute-start | bytes 577544 | tf_op jit(solution)/shard_map/ppermute | solution.py:45
  5.7 11.8 %collective-permute-start.1 = (f32[47,8,128]{2,1,0:T(8,128)S(1)}, f32[47,8,128]{2,1,0:T(8,128)S(1)}, u32[]{:S(2)}, u32[]{:S(2)}) collective-permute-start(f32[47,8,128]{2,1,0:T(8,128)S(1)} %get-tuple-element.46), channel_id=1, source_target_pairs={{0,15},{1,2},{2,1},{3,4},{4,3},{5,6},{6,5},{7,8},{8,7},{9,10},{10,... | collective-permute-start | bytes 577544 | tf_op jit(solution)/shard_map/ppermute | solution.py:45
  17.5 16.5 %collective-permute-start.2 = (f32[79,8,128]{2,1,0:T(8,128)S(1)}, f32[79,8,128]{2,1,0:T(8,128)S(1)}, u32[]{:S(2)}, u32[]{:S(2)}) collective-permute-start(f32[79,8,128]{2,1,0:T(8,128)S(1)} %get-tuple-element.56), channel_id=1, source_target_pairs={{0,496},{16,32},{32,16},{48,64},{64,48},{80,96},{96,80},{112,128},... | collective-permute-start | bytes 970760 | tf_op jit(solution)/shard_map/ppermute | solution.py:45
  28.3 5.7 %collective-permute-start.3 = (f32[79,8,128]{2,1,0:T(8,128)S(1)}, f32[79,8,128]{2,1,0:T(8,128)S(1)}, u32[]{:S(2)}, u32[]{:S(2)}) collective-permute-start(f32[79,8,128]{2,1,0:T(8,128)S(1)} %get-tuple-element.57), channel_id=1, source_target_pairs={{0,16},{16,0},{32,48},{48,32},{64,80},{80,64},{96,112},{112,96},{1... | collective-permute-start | bytes 970760 | tf_op jit(solution)/shard_map/ppermute | solution.py:45
  39.2 9.1 %collective-permute-start.4 = (f32[200,128]{1,0:T(8,128)S(1)}, f32[200,128]{1,0:T(8,128)S(1)}, u32[]{:S(2)}, u32[]{:S(2)}) collective-permute-start(f32[200,128]{1,0:T(8,128)S(1)} %get-tuple-element.63), channel_id=1, source_target_pairs={{0,1},{1,0},{2,3},{3,2},{4,5},{5,4},{6,7},{7,6},{8,9},{9,8},{10,11... | collective-permute-start | bytes 307208 | tf_op jit(solution)/shard_map/ppermute | solution.py:45
  44.8 10.2 %collective-permute-start.5 = (f32[200,128]{1,0:T(8,128)S(1)}, f32[200,128]{1,0:T(8,128)S(1)}, u32[]{:S(2)}, u32[]{:S(2)}) collective-permute-start(f32[200,128]{1,0:T(8,128)S(1)} %get-tuple-element.64), channel_id=1, source_target_pairs={{0,15},{1,2},{2,1},{3,4},{4,3},{5,6},{6,5},{7,8},{8,7},{9,10},{10,... | collective-permute-start | bytes 307208 | tf_op jit(solution)/shard_map/ppermute | solution.py:45
  55.2 8.3 %collective-permute-start.6 = (f32[232,128]{1,0:T(8,128)S(1)}, f32[232,128]{1,0:T(8,128)S(1)}, u32[]{:S(2)}, u32[]{:S(2)}) collective-permute-start(f32[232,128]{1,0:T(8,128)S(1)} %get-tuple-element.67), channel_id=1, source_target_pairs={{0,496},{16,32},{32,16},{48,64},{64,48},{80,96},{96,80},{112,128},... | collective-permute-start | bytes 356360 | tf_op jit(solution)/shard_map/ppermute | solution.py:45
  57.7 5.8 %collective-permute-start.7 = (f32[232,128]{1,0:T(8,128)S(1)}, f32[232,128]{1,0:T(8,128)S(1)}, u32[]{:S(2)}, u32[]{:S(2)}) collective-permute-start(f32[232,128]{1,0:T(8,128)S(1)} %get-tuple-element.68), channel_id=1, source_target_pairs={{0,16},{16,0},{32,48},{48,32},{64,80},{80,64},{96,112},{112,96},{1... | collective-permute-start | bytes 356360 | tf_op jit(solution)/shard_map/ppermute | solution.py:45

commit v6 on v5

--- a/solution.py
+++ b/solution.py
@@ -45,12 +45,17 @@
     return lax.ppermute(block, axis, route)
 
 
-def hot_group(first, rec, cells):
+def chip_pair(block):
+    pairs = [[i, i + 1] for i in range(0, lax.axis_size("gx"), 2)]
+    return lax.all_gather(block, "gx", axis_index_groups=pairs)
+
+
+def hot_group(first, number, rec, cells):
     sub = lax.broadcasted_iota(jnp.int32, (16, NODES), 0)
     second = (sub >= 8).astype(F32)
     subf = sub.astype(F32)
     left, right = [], []
-    for g in range(GROUP):
+    for g in range(number):
         cell, value = cells[first + g], rec[first + g]
         half = (cell >= PAIRS * NZ).astype(jnp.int32)
         high = ((cell - half * (PAIRS * NZ)) >> 7).astype(F32)
@@ -68,13 +73,22 @@
 
 
 def spread_groups(start, stop, rec, cells, acc):
-    def group(c, _):
-        left, right = hot_group(c * GROUP, rec, cells)
-        acc[0] += left
-        acc[1] += right
-        return 0
-
-    lax.fori_loop(start, stop, group, 0)
+    def groups(number):
+        def group(c, first):
+            left, right = hot_group(first, number, rec, cells)
+            acc[0] += left
+            acc[1] += right
+            return first + number
+
+        return group
+
+    count = stop - start
+    first = lax.fori_loop(0, count // 2, groups(2 * GROUP), start * GROUP)
+    lax.fori_loop(0, lax.rem(count, 2), groups(GROUP), first)
+
+
+def mirrored(px, low, high):
+    return jnp.where(px == 1, high, low)
 
 
 def number_in(tile):
@@ -160,7 +174,7 @@
     spread_groups(0, jnp.minimum(EARLY, number_in(state[...]) // GROUP), rows, cells, acc)
 
 
-def pack_x_kernel(xr, pot, eps, y0, y1, state, s1, s0):
+def pack_x_kernel(xr, pot, eps, y1, y0, state, s1, s0):
     del state
     px, py = parity("gx"), parity("gy")
     for n, (out, up) in enumerate(((s0, 1 - px), (s1, px))):
@@ -179,7 +193,7 @@
 
 def arrive_y_kernel(acc_in, rows_in, cells_in, state, y0, y1, nodes, rows, cells, state_out, acc, rec, cell):
     py = parity("gy")
-    acc[...] = acc_in[...]
+    del acc_in
     rec[0:STORE] = rows_in[...]
     cell[0:STORE] = cells_in[...]
     found = number_in(state[...])
@@ -210,7 +224,7 @@
 ):
     px, py = parity("gx"), parity("gy")
     x_low_first, y_low_first = px == 1, py == 1
-    acc[...] = acc_in[...]
+    del acc_in
     rec[0:GROUP] = rows[...]
     cell[0:GROUP] = cells[...]
     total = append(number_in(state[...]), x0, X_NUM, 1 - px, nodes, rec, cell)
@@ -278,19 +292,21 @@
 
 
 def coefficient_kernel(acc, x0, x1, y0, y1, pot, eps, force, phi, xp, xm, yp, ym, zp, zm, inv, ew):
-    px, py = parity("gx"), parity("gy")
-    x_low_first, y_low_first = px == 1, py == 1
+    px, y_low_first = parity("gx"), parity("gy") == 1
     for c in range(3):
         for ex in range(WIDE):
             force[c, ex] = spread_rows(acc, c + 1, ex, 1, BY)
     for buf, own, x_tile, y_tile in ((phi, pot, X_POT, Y_POT), (ew, eps, X_EPS, Y_EPS)):
-        buf[W : W + BX, W : W + BY] = own[...]
-        a, b = y0[y_tile : y_tile + BX], y1[y_tile : y_tile + BX]
-        buf[W : W + BX, 0:W] = jnp.where(y_low_first, a, b)
-        buf[W : W + BX, W + BY : EXT] = jnp.where(y_low_first, b, a)
-        a, b = (x[x_tile : x_tile + 4 * W].reshape(W, EXT, NZ) for x in (x0, x1))
-        buf[0:W] = jnp.where(x_low_first, a, b)
-        buf[W + BX : EXT] = jnp.where(x_low_first, b, a)
+        for n in range(BX):
+            x = mirrored(px, n, BX - 1 - n)
+            a, b = y0[y_tile + x], y1[y_tile + x]
+            buf[W + n, 0:W] = jnp.where(y_low_first, a, b)
+            buf[W + n, W : W + BY] = own[x]
+            buf[W + n, W + BY : EXT] = jnp.where(y_low_first, b, a)
+        for n in range(W):
+            at = pl.ds(x_tile + 4 * mirrored(px, n, W - 1 - n), 4)
+            buf[n] = x1[at].reshape(EXT, NZ)
+            buf[W + BX + n] = x0[at].reshape(EXT, NZ)
     for x in range(1, EXT - 1):
         e = ew[x]
         up, down = e + ew[x + 1], e + ew[x - 1]
@@ -307,69 +323,102 @@
         buf[EXT - 1] = jnp.zeros((EXT, NZ), F32)
 
 
-def join_y_kernel(dens, force, r0, r1, dext, fcore, s1, s0):
+def join_y_kernel(dens, force, r1, r0, dext, fcore, s1, s0):
     px, py = parity("gx"), parity("gy")
     low_first = py == 1
     dext[0:7] = jnp.zeros((7, EXT, NZ), F32)
     dext[25:32] = jnp.zeros((7, EXT, NZ), F32)
-    for ex in range(WIDE):
-        dext[ex + 7] = dens[ex]
-        a, b = r0[ex * 8 : ex * 8 + 8], r1[ex * 8 : ex * 8 + 8]
-        dext[ex + 7, 1:9] += jnp.where(low_first, a, b)
-        dext[ex + 7, 23:31] += jnp.where(low_first, b, a)
+    for n in range(WIDE):
+        ex = mirrored(px, n, WIDE - 1 - n)
+        dext[n + 7] = dens[ex]
+        at = pl.ds(pl.multiple_of(ex * 8, 8), 8)
+        a, b = r0[at], r1[at]
+        dext[n + 7, 1:9] += jnp.where(low_first, a, b)
+        dext[n + 7, 23:31] += jnp.where(low_first, b, a)
     fcore[...] = force[...]
     for c in range(3):
         r = DY_FORCE + c * WIDE
         a, b = r0[r : r + WIDE], r1[r : r + WIDE]
         fcore[c, :, 0] += jnp.where(low_first, a, b)
         fcore[c, :, BY - 1] += jnp.where(low_first, b, a)
-    for out, up in ((s0, 1 - px), (s1, px)):
-        for d in range(W):
-            plane = jnp.where(up == 1, dext[24 - d, d + 1 : 31 - d], dext[7 + d, d + 1 : 31 - d])
-            out[DX_AT[d] : DX_AT[d + 1]] = plane
-        for c in range(3):
-            out[DX_FORCE + c * BY : DX_FORCE + (c + 1) * BY] = fcore[c, up * (WIDE - 1)]
-
-
-def sweep_kernel(dext, fcore, r1, r0, phi, xp, xm, yp, ym, zp, zm, inv, pot_next, force, phi_a, phi_b, rhs):
-    low_first = parity("gx") == 1
-    force[...] = fcore[:, 1 : BX + 1]
-    a, b = (r[DX_FORCE:DX_END].reshape(3, BY, NZ) for r in (r0, r1))
-    force[:, 0] += jnp.where(low_first, a, b)
-    force[:, BX - 1] += jnp.where(low_first, b, a)
-
-    rhs[1 : EXT - 1] = dext[1 : EXT - 1]
+    pack_rims(dext, fcore, s1, px, 7, 1)
+    pack_rims(dext, fcore, s0, 1 - px, 24, -1)
+
+
+def pack_rims(dext, fcore, out, up, first, way):
     for d in range(W):
-        a, b = (r[DX_AT[d] : DX_AT[d + 1]] for r in (r0, r1))
-        rhs[8 - d, d + 1 : 31 - d] += jnp.where(low_first, a, b)
-        rhs[23 + d, d + 1 : 31 - d] += jnp.where(low_first, b, a)
-    rhs[1 : EXT - 1] = rhs[1 : EXT - 1] * inv[1 : EXT - 1]
-
+        out[DX_AT[d] : DX_AT[d + 1]] = dext[first + way * d, d + 1 : 31 - d]
+    for c in range(3):
+        out[DX_FORCE + c * BY : DX_FORCE + (c + 1) * BY] = fcore[c, up * (WIDE - 1)]
+
+
+def sweep_plane(k, x, west, here, east, weights, rhs):
+    xp, xm, yp, ym, zp, zm = weights
+    if k < SWEEPS:
+        f = slice(0, EXT)
+        north, south = pltpu.roll(here[...], EXT - 1, 0), pltpu.roll(here[...], 1, 0)
+    else:
+        f = slice(W, W + BY)
+        north, south = here[W + 1 : W + BY + 1], here[W - 1 : W + BY - 1]
+    centre = here[f]
+    total = (xp[x, f] * east[f] + xm[x, f] * west[f]) + (yp[x, f] * north + ym[x, f] * south)
+    return total + ((zp[x, f] * pltpu.roll(centre, NZ - 1, 1) + zm[x, f] * pltpu.roll(centre, 1, 1)) + rhs[x, f])
+
+
+def near_kernel(dext, r0, phi, xp, xm, yp, ym, zp, zm, inv, near, edges, phi_a, phi_b, rhs):
+    weights, other = (xp, xm, yp, ym, zp, zm), 1 - parity("gx")
+    rhs[9 : EXT - 1] = dext[9 : EXT - 1]
+    for d in range(W):
+        rhs[23 + d, d + 1 : 31 - d] += r0[other, DX_AT[d] : DX_AT[d + 1]]
+    rhs[9 : EXT - 1] = rhs[9 : EXT - 1] * inv[9 : EXT - 1]
     for k in range(1, SWEEPS + 1):
         old = phi if k == 1 else (phi_a, phi_b)[k % 2]
         new = (phi_a, phi_b)[(k + 1) % 2]
-        for x in range(k, EXT - k):
+        for x in range(W + k, EXT - k):
+            total = sweep_plane(k, x, old.at[x - 1], old.at[x], old.at[x + 1], weights, rhs)
+            if k == SWEEPS:
+                near[x - 16] = total
+                continue
+            new[x] = total
+            if x < W + k + 2:
+                edges[2 * k - 2 + x - W - k] = total
+
+
+def far_kernel(dext, r1, r0, fcore, phi, xp, xm, yp, ym, zp, zm, inv, near, edges, pot_next, force, phi_a, phi_b, rhs):
+    px = parity("gx")
+    weights = (xp, xm, yp, ym, zp, zm)
+    rhs[1:16] = dext[1:16]
+    for d in range(W):
+        rhs[8 - d, d + 1 : 31 - d] += r1[DX_AT[d] : DX_AT[d + 1]]
+    rhs[1:16] = rhs[1:16] * inv[1:16]
+
+    def plane(k, x):
+        if k == 0:
+            return phi.at[x]
+        return edges.at[2 * k - 2 + x - W - k] if x >= W + k else (phi_a, phi_b)[(k + 1) % 2].at[x]
+
+    for k in range(1, SWEEPS + 1):
+        for x in range(k, W + k):
+            total = sweep_plane(k, x, plane(k - 1, x - 1), plane(k - 1, x), plane(k - 1, x + 1), weights, rhs)
             if k < SWEEPS:
-                f = slice(0, EXT)
-                here = old[x]
-                north, south = pltpu.roll(here, EXT - 1, 0), pltpu.roll(here, 1, 0)
+                plane(k, x)[...] = total
             else:
-                f = slice(W, W + BY)
-                here = old[x, f]
-                north, south = old[x, W + 1 : W + BY + 1], old[x, W - 1 : W + BY - 1]
-            total = (xp[x, f] * old[x + 1, f] + xm[x, f] * old[x - 1, f]) + (yp[x, f] * north + ym[x, f] * south)
-            total += (zp[x, f] * pltpu.roll(here, NZ - 1, 1) + zm[x, f] * pltpu.roll(here, 1, 1)) + rhs[x, f]
-            if k < SWEEPS:
-                new[x] = total
-            else:
-                pot_next[x - W] = total
+                pot_next[mirrored(px, x - W, 23 - x)] = total
+    for x in range(16, 24):
+        pot_next[mirrored(px, x - W, 23 - x)] = near[x - 16]
+
+    low_first = px == 1
+    force[...] = fcore[:, 1 : BX + 1]
+    a, b = (r[DX_FORCE:DX_END].reshape(3, BY, NZ) for r in (r0.at[1 - px], r1))
+    force[:, 0] += jnp.where(low_first, a, b)
+    force[:, BX - 1] += jnp.where(low_first, b, a)
 
 
 def shape(*dims):
     return jax.ShapeDtypeStruct(dims, F32)
 
 
-def call(kernel, name, ins, outs, scratch=(), flops=0):
+def call(kernel, name, ins, outs, scratch=(), flops=0, aliases=None):
     moved = 4 * sum(int(o.size) for o in outs)
     return pl.pallas_call(
         kernel,
@@ -378,6 +427,7 @@
         out_specs=[VMEM] * len(outs),
         out_shape=outs,
         scratch_shapes=scratch,
+        input_output_aliases=aliases or {},
         compiler_params=pltpu.CompilerParams(vmem_limit_bytes=32 << 20),
         cost_estimate=pl.CostEstimate(flops=flops, bytes_accessed=moved, transcendentals=0),
     )
@@ -412,7 +462,7 @@
     late, acc = call(kept_kernel, "spread_kept", [VMEM] * 3, [shape(8, NZ), sums], flops=row_flops * EARLY * GROUP)(
         rows, cells, state
     )
-    b1, b0 = call(pack_x_kernel, "pack_x", [VMEM] * 6, [shape(X_END, 8, NZ)] * 2)(xr, pot_v, eps_v, y0, y1, late)
+    b1, b0 = call(pack_x_kernel, "pack_x", [VMEM] * 6, [shape(X_END, 8, NZ)] * 2)(xr, pot_v, eps_v, y1, y0, late)
     x1, x0 = swap(b1, "gx", 1), swap(b0, "gx", 0)
     rows, cells, state, acc = call(
         arrive_y_kernel,
@@ -421,6 +471,7 @@
         [*store(GROUP, jax.ShapeDtypeStruct), shape(8, NZ), sums],
         store(STORE + 2 * MOVERS + GROUP),
         flops=row_flops * 48,
+        aliases={0: 3},
     )(acc, rows, cells, state, y0, y1, arrive_v)
     conc_next, acc, dens, c1, c0 = call(
         arrive_x_kernel,
@@ -429,6 +480,7 @@
         [shape(3, BX, BY, NZ), sums, shape(WIDE, EXT, NZ), shape(DY_END, NZ), shape(DY_END, NZ)],
         store(2 * MOVERS + 2 * GROUP) + [pltpu.VMEM((4, WIDE, 32, NZ), F32)],
         flops=row_flops * 2 * MOVERS,
+        aliases={0: 1},
     )(acc, rows, cells, state, x1, x0, y0, y1, arrive_v, conc_v, pot_v)
     r0, r1 = swap(c0, "gy", 0), swap(c1, "gy", 1)
     force, phi, *weights = call(
@@ -441,16 +493,25 @@
     )(acc, x0, x1, y0, y1, pot_v, eps_v)
     dext, fcore, e1, e0 = call(
         join_y_kernel, "join_y", [VMEM] * 4, [field, shape(3, WIDE, BY, NZ), shape(DX_END, NZ), shape(DX_END, NZ)]
-    )(dens, force, r0, r1)
-    g1, g0 = swap(e1, "gx", 1), swap(e0, "gx", 0)
+    )(dens, force, r1, r0)
+    g1, g0 = swap(e1, "gx", 1), chip_pair(e0)
+    scratch = [pltpu.VMEM((EXT, EXT, NZ), F32)] * 3
+    near, edges = call(
+        near_kernel,
+        "sweeps_near",
+        [VMEM] * 10,
+        [shape(BX // 2, BY, NZ), shape(2 * SWEEPS - 2, EXT, NZ)],
+        scratch,
+        flops=12 * SWEEPS * EXT * EXT * NZ,
+    )(dext, g0, phi, *weights)
     pot_next, body_force = call(
-        sweep_kernel,
-        "sweeps",
-        [VMEM] * 12,
+        far_kernel,
+        "sweeps_far",
+        [VMEM] * 14,
         [core, shape(3, BX, BY, NZ)],
-        [pltpu.VMEM((EXT, EXT, NZ), F32)] * 3,
-        flops=20 * SWEEPS * EXT * EXT * NZ,
-    )(dext, fcore, g1, g0, phi, *weights)
+        scratch,
+        flops=8 * SWEEPS * EXT * EXT * NZ,
+    )(dext, g1, g0, fcore, phi, *weights, near, edges)
     return conc_next, pot_next, body_force
 
 

time: 66.9 us -> 66 us (0.987)
  the two profiles are of different devices: /device:TPU:60 before, /device:TPU:1 now
where the time goes in v6:
time: 66 us; the launch traced here: 64.8 us
  starting transfers between devices  35.5 us (54%)
  Pallas kernels  19.9 us (30%)
  waiting for transfers between devices  5.05 us (8%)
  blocking collectives  3.02 us (5%)
  between operations  1.42 us (2%)
    ppermute x7, starting transfers between devices, swap(): return lax.ppermute(block, axis, route)  35.5 us
    pallas_call x1, Pallas kernels, body(): call(kept_kernel, 'spread_kept', [VMEM] * 3, [shape(8, NZ), sums], flops=...  5.82 us
    ppermute x7, waiting for transfers between devices, swap(): return lax.ppermute(block, axis, route)  5.05 us
    pallas_call x1, Pallas kernels, body(): call(arrive_x_kernel, 'spread_x', [VMEM] * 11, [shape(3, BX, BY, NZ), sum...  5.01 us
    all_gather x1, blocking collectives, chip_pair(): return lax.all_gather(block, 'gx', axis_index_groups=pairs)  3.02 us
    pallas_call x1, Pallas kernels, body(): call(arrive_y_kernel, 'spread_y', [VMEM] * 7, [*store(GROUP, jax.ShapeDty...  2.64 us
    pallas_call x1, Pallas kernels, body(): call(first_kernel, 'first', [HBM] * 8 + [SMEM], [shape(Y_END, 8, NZ), sha...  1.98 us
    pallas_call x1, Pallas kernels, body(): call(far_kernel, 'sweeps_far', [VMEM] * 14, [core, shape(3, BX, BY, NZ)],...  1.6 us
  transfers between devices with their start and end apart: 7, of which 1 were waited for; matrix products, arithmetic and copies ran while one was open for 0% of the time, Pallas kernels for 17%

profile of v6, /device:TPU:1, one launch (start us, length us, event | category | flops | bytes accessed | tf_op | source)
XLA Modules:
  0.0 64.8 jit_solution(13035449993076665587)
XLA Ops:
  1.3 2.0 %first.1 = (f32[47,8,128]{2,1,0:T(8,128)S(1)}, f32[47,8,128]{2,1,0:T(8,128)S(1)}, f32[3,16,16,128]{3,2,1,0:T(8,128)S(1)}, f32[16,16,128]{2,1,0:T(8,128)S(1)}, f3...) custom-call(f32[3,16,16,128]{3,2,1,0:T(8,128)} %conc_h.1, ...), custom_call_target="tpu_custom_call" | custom-call | bytes 1548288 | tf_op jit(solution)/shard_map/first/pallas_call | solution.py:450
  3.3 5.5 %collective-permute-start = (f32[47,8,128]{2,1,0:T(8,128)S(1)}, f32[47,8,128]{2,1,0:T(8,128)S(1)}, u32[]{:S(2)}, u32[]{:S(2)}) collective-permute-start(f32[47,8,128]{2,1,0:T(8,128)S(1)} %get-tuple-element.47), channel_id=1, source_target_pairs={{0,1},{1,0},{2,3},{3,2},{4,5},{5,4},{6,7},{7,6},{8,9},{9,8},{10,11... | collective-permute-start | bytes 577544 | tf_op jit(solution)/shard_map/ppermute | solution.py:45
  8.8 5.0 %collective-permute-start.1 = (f32[47,8,128]{2,1,0:T(8,128)S(1)}, f32[47,8,128]{2,1,0:T(8,128)S(1)}, u32[]{:S(2)}, u32[]{:S(2)}) collective-permute-start(f32[47,8,128]{2,1,0:T(8,128)S(1)} %get-tuple-element.48), channel_id=1, source_target_pairs={{0,15},{1,2},{2,1},{3,4},{4,3},{5,6},{6,5},{7,8},{8,7},{9,10},{10,... | collective-permute-start | bytes 577544 | tf_op jit(solution)/shard_map/ppermute | solution.py:45
  13.8 5.8 %spread_kept.1 = (f32[8,128]{1,0:T(8,128)S(1)}, f32[2,1296,128]{2,1,0:T(8,128)S(1)}) custom-call(f32[136,4,128]{2,1,0:T(4,128)S(1)} %get-tuple-element.43.rows.rows_in, s32[136,1,128]{2,1,0:T(1,128)S(1)} %get-tuple-element.44.cells.cells_in, f32[8,128]{1,0:T(8,128)S(1)} %get-tuple-element.45.state), custom_call_target="tpu_custom_call" | custom-call | flops 4756340736 | bytes 1331200 | tf_op jit(solution)/shard_map/spread_kept/pallas_call | solution.py:462
  19.6 0.0 collective-permute-done.y0
  19.6 0.0 collective-permute-done.1.y1
  19.7 0.1 pack_x.1
  19.7 5.7 %collective-permute-start.2 = (f32[79,8,128]{2,1,0:T(8,128)S(1)}, f32[79,8,128]{2,1,0:T(8,128)S(1)}, u32[]{:S(2)}, u32[]{:S(2)}) collective-permute-start(f32[79,8,128]{2,1,0:T(8,128)S(1)} %get-tuple-element.58), channel_id=1, source_target_pairs={{0,496},{16,32},{32,16},{48,64},{64,48},{80,96},{96,80},{112,128},... | collective-permute-start | bytes 970760 | tf_op jit(solution)/shard_map/ppermute | solution.py:45
  25.5 8.2 %collective-permute-start.3 = (f32[79,8,128]{2,1,0:T(8,128)S(1)}, f32[79,8,128]{2,1,0:T(8,128)S(1)}, u32[]{:S(2)}, u32[]{:S(2)}) collective-permute-start(f32[79,8,128]{2,1,0:T(8,128)S(1)} %get-tuple-element.59), channel_id=1, source_target_pairs={{0,16},{16,0},{32,48},{48,32},{64,80},{80,64},{96,112},{112,96},{1... | collective-permute-start | bytes 970760 | tf_op jit(solution)/shard_map/ppermute | solution.py:45
  33.7 2.6 %spread_y.1 = (f32[8,4,128]{2,1,0:T(4,128)S(1)}, s32[8,1,128]{2,1,0:T(1,128)S(1)}, f32[8,128]{1,0:T(8,128)S(1)}, f32[2,1296,128]{2,1,0:T(8,128)S(1)}) custom-call(f32[2,1296,128]{2,1,0:T(8,128)S(1)} %get-tuple-element.46.acc_in, f32[136,4,128]{2,1,0:T(4,128)S(1)} %get-tuple-element.43.rows.rows_in, ...), custom_call_target="tpu_custom_call", output_to_operand_aliasing={{3}: (0, {})} | custom-call | flops 4076863488 | bytes 1351680 | tf_op jit(solution)/shard_map/spread_y/pallas_call | solution.py:467
  36.3 0.0 collective-permute-done.2.x1
  36.3 0.0 collective-permute-done.3.x0
  36.3 5.0 %spread_x.1 = (f32[3,16,16,128]{3,2,1,0:T(8,128)}, f32[2,1296,128]{2,1,0:T(8,128)S(1)}, f32[18,32,128]{2,1,0:T(8,128)S(1)}, f32[200,128]{1,0:T(8,128)S(1)}, f32[200,128]{1,0:T(8,128)S(1)}) custom-call(f32[2,1296,128]{2,1,0:T(8,128)S(1)} %get-tuple-element.50.acc_in, f32[8,4,128]{2,1,0:T(4,128)S(1)} %get-tuple-element.51.rows, ...), custom_call_target="tpu_custom_call", output_to_operand_aliasing={{1}: (0, {})} | custom-call | flops 2717908992 | bytes 2220032 | tf_op jit(solution)/shard_map/spread_x/pallas_call | solution.py:476
  41.3 7.2 %collective-permute-start.4 = (f32[200,128]{1,0:T(8,128)S(1)}, f32[200,128]{1,0:T(8,128)S(1)}, u32[]{:S(2)}, u32[]{:S(2)}) collective-permute-start(f32[200,128]{1,0:T(8,128)S(1)} %get-tuple-element.65), channel_id=1, source_target_pairs={{0,15},{1,2},{2,1},{3,4},{4,3},{5,6},{6,5},{7,8},{8,7},{9,10},{10,... | collective-permute-start | bytes 307208 | tf_op jit(solution)/shard_map/ppermute | solution.py:45
  48.5 1.9 %collective-permute-start.5 = (f32[200,128]{1,0:T(8,128)S(1)}, f32[200,128]{1,0:T(8,128)S(1)}, u32[]{:S(2)}, u32[]{:S(2)}) collective-permute-start(f32[200,128]{1,0:T(8,128)S(1)} %get-tuple-element.66), channel_id=1, source_target_pairs={{0,1},{1,0},{2,3},{3,2},{4,5},{5,4},{6,7},{7,6},{8,9},{9,8},{10,11... | collective-permute-start | bytes 307208 | tf_op jit(solution)/shard_map/ppermute | solution.py:45
  50.4 1.2 %coefficients.1 = (f32[3,18,16,128]{3,2,1,0:T(8,128)S(1)}, f32[32,32,128]{2,1,0:T(8,128)S(1)}, f32[32,32,128]{2,1,0:T(8,128)S(1)}, f32[32,32,128]{2,1,0:T(8,128)...) custom-call(f32[2,1296,128]{2,1,0:T(8,128)S(1)} %get-tuple-element.6, ...), custom_call_target="tpu_custom_call" | custom-call | flops 679477248 | bytes 4636672 | tf_op jit(solution)/shard_map/coefficients/pallas_call | solution.py:486
  51.7 0.0 collective-permute-done.4.r1
  51.7 5.0 %collective-permute-done.5.r0 = f32[200,128]{1,0:T(8,128)S(1)} collective-permute-done((f32[200,128]{1,0:T(8,128)S(1)}, f32[200,128]{1,0:T(8,128)S(1)}, u32[]{:S(2)}, u32[]{:S(2)}) %collective-permute-start.5) | collective-permute-done | bytes 102432 | tf_op jit(solution)/shard_map/ppermute | solution.py:45
  56.7 0.2 join_y.1
  56.9 1.9 %collective-permute-start.6 = (f32[232,128]{1,0:T(8,128)S(1)}, f32[232,128]{1,0:T(8,128)S(1)}, u32[]{:S(2)}, u32[]{:S(2)}) collective-permute-start(f32[232,128]{1,0:T(8,128)S(1)} %get-tuple-element.68), channel_id=1, source_target_pairs={{0,496},{16,32},{32,16},{48,64},{64,48},{80,96},{96,80},{112,128},... | collective-permute-start | bytes 356360 | tf_op jit(solution)/shard_map/ppermute | solution.py:45
  58.8 3.0 %all-gather = f32[464,128]{1,0:T(8,128)S(1)} all-gather(f32[232,128]{1,0:T(8,128)S(1)} %get-tuple-element.69), channel_id=2, replica_groups={{0,16},{32,48},{64,80},{96,112},{128,144},{160,176},{192,208},{224,240}..., dimensions={0}, use_global_device_ids=true | all-gather | bytes 356352 | tf_op jit(solution)/shard_map/all_gather | solution.py:50
  61.9 1.3 %sweeps_near.1 = (f32[8,16,128]{2,1,0:T(8,128)S(1)}, f32[14,32,128]{2,1,0:T(8,128)S(1)}) custom-call(f32[32,32,128]{2,1,0:T(8,128)S(1)} %get-tuple-element.67.dext, f32[2,232,128]{2,1,0:T(8,128)S(1)} %bitcast.1, f32[32,32,128]{2,1,0:T(8,128)S(1)} %get-tuple-element.71.phi, f32[32,32,128]{2,1,0:T(8,128)S(1)} %get-tuple-element.72.xp, ...), custom_call_target="tpu_custom_call" | custom-call | flops 12582912 | bytes 294912 | tf_op jit(solution)/shard_map/sweeps_near/pallas_call | solution.py:499
  63.2 0.0 collective-permute-done.6.r1
  63.2 1.6 %sweeps_far.1 = (f32[16,16,128]{2,1,0:T(8,128)}, f32[3,16,16,128]{3,2,1,0:T(8,128)}) custom-call(f32[32,32,128]{2,1,0:T(8,128)S(1)} %get-tuple-element.67.dext, f32[232,128]{1,0:T(8,128)S(1)} %collective-permute-done.6.r1, f32[2,232,128]{2,1,0:T(8,128)S(1)} %bitcast.2, f32[3,18,16,128]{3,2,1,0:T(8,128)S(1)} %get-tuple-element.70.fcore, ...), custom_call_target="tpu_custom_call" | custom-call | flops 8388608 | bytes 524288 | tf_op jit(solution)/shard_map/sweeps_far/pallas_call | solution.py:507
Async XLA Ops:
  3.3 16.4 %collective-permute-start = (f32[47,8,128]{2,1,0:T(8,128)S(1)}, f32[47,8,128]{2,1,0:T(8,128)S(1)}, u32[]{:S(2)}, u32[]{:S(2)}) collective-permute-start(f32[47,8,128]{2,1,0:T(8,128)S(1)} %get-tuple-element.47), channel_id=1, source_target_pairs={{0,1},{1,0},{2,3},{3,2},{4,5},{5,4},{6,7},{7,6},{8,9},{9,8},{10,11... | collective-permute-start | bytes 577544 | tf_op jit(solution)/shard_map/ppermute | solution.py:45
  8.8 10.9 %collective-permute-start.1 = (f32[47,8,128]{2,1,0:T(8,128)S(1)}, f32[47,8,128]{2,1,0:T(8,128)S(1)}, u32[]{:S(2)}, u32[]{:S(2)}) collective-permute-start(f32[47,8,128]{2,1,0:T(8,128)S(1)} %get-tuple-element.48), channel_id=1, source_target_pairs={{0,15},{1,2},{2,1},{3,4},{4,3},{5,6},{6,5},{7,8},{8,7},{9,10},{10,... | collective-permute-start | bytes 577544 | tf_op jit(solution)/shard_map/ppermute | solution.py:45
  19.7 16.6 %collective-permute-start.2 = (f32[79,8,128]{2,1,0:T(8,128)S(1)}, f32[79,8,128]{2,1,0:T(8,128)S(1)}, u32[]{:S(2)}, u32[]{:S(2)}) collective-permute-start(f32[79,8,128]{2,1,0:T(8,128)S(1)} %get-tuple-element.58), channel_id=1, source_target_pairs={{0,496},{16,32},{32,16},{48,64},{64,48},{80,96},{96,80},{112,128},... | collective-permute-start | bytes 970760 | tf_op jit(solution)/shard_map/ppermute | solution.py:45
  25.5 10.9 %collective-permute-start.3 = (f32[79,8,128]{2,1,0:T(8,128)S(1)}, f32[79,8,128]{2,1,0:T(8,128)S(1)}, u32[]{:S(2)}, u32[]{:S(2)}) collective-permute-start(f32[79,8,128]{2,1,0:T(8,128)S(1)} %get-tuple-element.59), channel_id=1, source_target_pairs={{0,16},{16,0},{32,48},{48,32},{64,80},{80,64},{96,112},{112,96},{1... | collective-permute-start | bytes 970760 | tf_op jit(solution)/shard_map/ppermute | solution.py:45
  41.3 10.4 %collective-permute-start.4 = (f32[200,128]{1,0:T(8,128)S(1)}, f32[200,128]{1,0:T(8,128)S(1)}, u32[]{:S(2)}, u32[]{:S(2)}) collective-permute-start(f32[200,128]{1,0:T(8,128)S(1)} %get-tuple-element.65), channel_id=1, source_target_pairs={{0,15},{1,2},{2,1},{3,4},{4,3},{5,6},{6,5},{7,8},{8,7},{9,10},{10,... | collective-permute-start | bytes 307208 | tf_op jit(solution)/shard_map/ppermute | solution.py:45
  48.5 8.2 %collective-permute-start.5 = (f32[200,128]{1,0:T(8,128)S(1)}, f32[200,128]{1,0:T(8,128)S(1)}, u32[]{:S(2)}, u32[]{:S(2)}) collective-permute-start(f32[200,128]{1,0:T(8,128)S(1)} %get-tuple-element.66), channel_id=1, source_target_pairs={{0,1},{1,0},{2,3},{3,2},{4,5},{5,4},{6,7},{7,6},{8,9},{9,8},{10,11... | collective-permute-start | bytes 307208 | tf_op jit(solution)/shard_map/ppermute | solution.py:45
  56.9 6.3 %collective-permute-start.6 = (f32[232,128]{1,0:T(8,128)S(1)}, f32[232,128]{1,0:T(8,128)S(1)}, u32[]{:S(2)}, u32[]{:S(2)}) collective-permute-start(f32[232,128]{1,0:T(8,128)S(1)} %get-tuple-element.68), channel_id=1, source_target_pairs={{0,496},{16,32},{32,16},{48,64},{64,48},{80,96},{96,80},{112,128},... | collective-permute-start | bytes 356360 | tf_op jit(solution)/shard_map/ppermute | solution.py:45

commit v7 on v6

--- a/solution.py
+++ b/solution.py
@@ -21,7 +21,7 @@
 PAIRS = WIDE * WIDE // 2
 ROWS = PAIRS * 2 * CHANNELS
 GROUP = 8
-EARLY = 7
+EARLY = 9
 STORE = SLOTS + GROUP
 
 Y_CONC, Y_POT, Y_EPS, Y_NUM, Y_END = 8, 14, 30, 46, 47
@@ -207,10 +207,6 @@
     state_out[...] = jnp.full((8, NZ), (total - done * GROUP).astype(F32))
 
 
-def face_flux(s, upper, lower, step):
-    return -DIFFUSION[s] * ((upper - lower) + (VALENCE[s] * 0.5) * (upper + lower) * step)
-
-
 def spread_rows(acc, channel, ex, first, number):
     half, row = divmod(ex, WIDE // 2)
     base = (row * WIDE + first) * 8 + channel
@@ -256,22 +252,23 @@
     for ex in range(WIDE):
         dens[ex, 7 : 7 + WIDE] = spread_rows(acc, 0, ex, 0, WIDE)
 
-    before = [face_flux(s, wide[s, 1, 8:24], wide[s, 0, 8:24], wide[3, 1, 8:24] - wide[3, 0, 8:24]) for s in range(3)]
+    def around(f, x):
+        c = wide[f, x + 1, 8:24]
+        beside = (wide[f, x + 2, 8:24], wide[f, x, 8:24], wide[f, x + 1, 9:25], wide[f, x + 1, 7:23])
+        return c, (*beside, pltpu.roll(c, NZ - 1, 1), pltpu.roll(c, 1, 1))
+
+    def total_of(terms):
+        return ((terms[0] + terms[1]) + (terms[2] + terms[3])) + (terms[4] + terms[5])
+
     for x in range(BX):
-        pc, pe = wide[3, x + 1, 8:24], wide[3, x + 2, 8:24]
-        pn, ps = wide[3, x + 1, 9:25], wide[3, x + 1, 7:23]
-        pz = pltpu.roll(pc, NZ - 1, 1)
-        dx, dn, ds, dz = pe - pc, pn - pc, pc - ps, pz - pc
+        p, steps = around(3, x)
+        steps = [q - p for q in steps]
         total = dens[x + 1, 8:24]
         for s in range(3):
-            c = wide[s, x + 1, 8:24]
-            flux_x = face_flux(s, wide[s, x + 2, 8:24], c, dx)
-            flux_n = face_flux(s, wide[s, x + 1, 9:25], c, dn)
-            flux_s = face_flux(s, c, wide[s, x + 1, 7:23], ds)
-            flux_z = face_flux(s, pltpu.roll(c, NZ - 1, 1), c, dz)
-            div = ((flux_x - before[s]) + (flux_n - flux_s)) + (flux_z - pltpu.roll(flux_z, 1, 1))
-            before[s] = flux_x
-            later = c - TIME_STEP * div
+            c, beside = around(s, x)
+            plain = total_of([n - c for n in beside])
+            drift = total_of([(n + c) * q for n, q in zip(beside, steps)])
+            later = c + (TIME_STEP * DIFFUSION[s]) * (plain + (VALENCE[s] * 0.5) * drift)
             conc_next[s, x] = later
             total = total + VALENCE[s] * later
         dens[x + 1, 8:24] = total
@@ -291,7 +288,9 @@
         out[DY_FORCE + 54 : DY_END] = jnp.zeros((2, NZ), F32)
 
 
-def coefficient_kernel(acc, x0, x1, y0, y1, pot, eps, force, phi, xp, xm, yp, ym, zp, zm, inv, ew):
+def coefficient_kernel(acc, x0, x1, y0, y1, pot, eps, conc_next, conc_out, force, base, xp, xm, yp, ym, zp, zm, inv, phi, ew, sem):
+    copy = pltpu.make_async_copy(conc_next, conc_out, sem)
+    copy.start()
     px, y_low_first = parity("gx"), parity("gy") == 1
     for c in range(3):
         for ex in range(WIDE):
@@ -318,9 +317,12 @@
         yp[x], ym[x] = north * scale, south * scale
         zp[x], zm[x] = over * scale, under * scale
         inv[x] = 2.0 * scale
-    for buf in (xp, xm, yp, ym, zp, zm, inv):
+    for buf in (xp, xm, yp, ym, zp, zm, inv, base):
         buf[0] = jnp.zeros((EXT, NZ), F32)
         buf[EXT - 1] = jnp.zeros((EXT, NZ), F32)
+    for x in range(1, EXT - 1):
+        base[x] = sweep_plane(1, x, phi.at[x - 1], phi.at[x], phi.at[x + 1], (xp, xm, yp, ym, zp, zm), None)
+    copy.wait()
 
 
 def join_y_kernel(dens, force, r1, r0, dext, fcore, s1, s0):
@@ -362,20 +364,23 @@
         north, south = here[W + 1 : W + BY + 1], here[W - 1 : W + BY - 1]
     centre = here[f]
     total = (xp[x, f] * east[f] + xm[x, f] * west[f]) + (yp[x, f] * north + ym[x, f] * south)
-    return total + ((zp[x, f] * pltpu.roll(centre, NZ - 1, 1) + zm[x, f] * pltpu.roll(centre, 1, 1)) + rhs[x, f])
-
-
-def near_kernel(dext, r0, phi, xp, xm, yp, ym, zp, zm, inv, near, edges, phi_a, phi_b, rhs):
+    along = zp[x, f] * pltpu.roll(centre, NZ - 1, 1) + zm[x, f] * pltpu.roll(centre, 1, 1)
+    return total + (along if rhs is None else along + rhs[x, f])
+
+
+def near_kernel(dext, r0, base, xp, xm, yp, ym, zp, zm, inv, near, edges, phi_a, phi_b, rhs):
     weights, other = (xp, xm, yp, ym, zp, zm), 1 - parity("gx")
     rhs[9 : EXT - 1] = dext[9 : EXT - 1]
     for d in range(W):
         rhs[23 + d, d + 1 : 31 - d] += r0[other, DX_AT[d] : DX_AT[d + 1]]
     rhs[9 : EXT - 1] = rhs[9 : EXT - 1] * inv[9 : EXT - 1]
     for k in range(1, SWEEPS + 1):
-        old = phi if k == 1 else (phi_a, phi_b)[k % 2]
-        new = (phi_a, phi_b)[(k + 1) % 2]
+        old, new = (phi_a, phi_b)[k % 2], (phi_a, phi_b)[(k + 1) % 2]
         for x in range(W + k, EXT - k):
-            total = sweep_plane(k, x, old.at[x - 1], old.at[x], old.at[x + 1], weights, rhs)
+            if k == 1:
+                total = base[x] + rhs[x]
+            else:
+                total = sweep_plane(k, x, old.at[x - 1], old.at[x], old.at[x + 1], weights, rhs)
             if k == SWEEPS:
                 near[x - 16] = total
                 continue
@@ -384,47 +389,62 @@
                 edges[2 * k - 2 + x - W - k] = total
 
 
-def far_kernel(dext, r1, r0, fcore, phi, xp, xm, yp, ym, zp, zm, inv, near, edges, pot_next, force, phi_a, phi_b, rhs):
+def far_kernel(
+    dext, r1, r0, fcore, base, xp, xm, yp, ym, zp, zm, inv, near, edges,
+    pot_next, force_out,
+    phi_a, phi_b, rhs, force, lower, upper, sems,
+):
     px = parity("gx")
     weights = (xp, xm, yp, ym, zp, zm)
-    rhs[1:16] = dext[1:16]
-    for d in range(W):
-        rhs[8 - d, d + 1 : 31 - d] += r1[DX_AT[d] : DX_AT[d + 1]]
-    rhs[1:16] = rhs[1:16] * inv[1:16]
-
-    def plane(k, x):
-        if k == 0:
-            return phi.at[x]
-        return edges.at[2 * k - 2 + x - W - k] if x >= W + k else (phi_a, phi_b)[(k + 1) % 2].at[x]
-
-    for k in range(1, SWEEPS + 1):
-        for x in range(k, W + k):
-            total = sweep_plane(k, x, plane(k - 1, x - 1), plane(k - 1, x), plane(k - 1, x + 1), weights, rhs)
-            if k < SWEEPS:
-                plane(k, x)[...] = total
-            else:
-                pot_next[mirrored(px, x - W, 23 - x)] = total
-    for x in range(16, 24):
-        pot_next[mirrored(px, x - W, 23 - x)] = near[x - 16]
-
     low_first = px == 1
     force[...] = fcore[:, 1 : BX + 1]
     a, b = (r[DX_FORCE:DX_END].reshape(3, BY, NZ) for r in (r0.at[1 - px], r1))
     force[:, 0] += jnp.where(low_first, a, b)
     force[:, BX - 1] += jnp.where(low_first, b, a)
+    for n in range(W):
+        upper[n] = near[mirrored(px, n, W - 1 - n)]
+    copies = [
+        pltpu.make_async_copy(force, force_out, sems.at[0]),
+        pltpu.make_async_copy(upper, pot_next.at[pl.ds(mirrored(px, W, 0), W)], sems.at[1]),
+        pltpu.make_async_copy(lower, pot_next.at[pl.ds(mirrored(px, 0, W), W)], sems.at[2]),
+    ]
+    copies[0].start()
+    copies[1].start()
+
+    rhs[1:16] = dext[1:16]
+    for d in range(W):
+        rhs[8 - d, d + 1 : 31 - d] += r1[DX_AT[d] : DX_AT[d + 1]]
+    rhs[1:16] = rhs[1:16] * inv[1:16]
+
+    def plane(k, x):
+        return edges.at[2 * k - 2 + x - W - k] if x >= W + k else (phi_a, phi_b)[(k + 1) % 2].at[x]
+
+    for k in range(1, SWEEPS + 1):
+        for x in range(k, W + k):
+            if k == 1:
+                total = base[x] + rhs[x]
+            else:
+                total = sweep_plane(k, x, plane(k - 1, x - 1), plane(k - 1, x), plane(k - 1, x + 1), weights, rhs)
+            if k < SWEEPS:
+                plane(k, x)[...] = total
+            else:
+                lower[mirrored(px, x - W, 15 - x)] = total
+    copies[2].start()
+    for copy in copies:
+        copy.wait()
 
 
 def shape(*dims):
     return jax.ShapeDtypeStruct(dims, F32)
 
 
-def call(kernel, name, ins, outs, scratch=(), flops=0, aliases=None):
+def call(kernel, name, ins, outs, scratch=(), flops=0, aliases=None, far_outs=()):
     moved = 4 * sum(int(o.size) for o in outs)
     return pl.pallas_call(
         kernel,
         name=name,
         in_specs=ins,
-        out_specs=[VMEM] * len(outs),
+        out_specs=[HBM if n in far_outs else VMEM for n in range(len(outs))],
         out_shape=outs,
         scratch_shapes=scratch,
         input_output_aliases=aliases or {},
@@ -473,7 +493,7 @@
         flops=row_flops * 48,
         aliases={0: 3},
     )(acc, rows, cells, state, y0, y1, arrive_v)
-    conc_next, acc, dens, c1, c0 = call(
+    conc_near, acc, dens, c1, c0 = call(
         arrive_x_kernel,
         "spread_x",
         [VMEM] * 11,
@@ -483,14 +503,15 @@
         aliases={0: 1},
     )(acc, rows, cells, state, x1, x0, y0, y1, arrive_v, conc_v, pot_v)
     r0, r1 = swap(c0, "gy", 0), swap(c1, "gy", 1)
-    force, phi, *weights = call(
+    conc_next, force, base, *weights = call(
         coefficient_kernel,
         "coefficients",
-        [VMEM] * 7,
-        [shape(3, WIDE, BY, NZ)] + [field] * 8,
-        [pltpu.VMEM((EXT, EXT, NZ), F32)],
+        [VMEM] * 8,
+        [shape(3, BX, BY, NZ), shape(3, WIDE, BY, NZ)] + [field] * 8,
+        [pltpu.VMEM((EXT, EXT, NZ), F32)] * 2 + [pltpu.SemaphoreType.DMA],
         flops=row_flops * 8,
-    )(acc, x0, x1, y0, y1, pot_v, eps_v)
+        far_outs=(0,),
+    )(acc, x0, x1, y0, y1, pot_v, eps_v, conc_near)
     dext, fcore, e1, e0 = call(
         join_y_kernel, "join_y", [VMEM] * 4, [field, shape(3, WIDE, BY, NZ), shape(DX_END, NZ), shape(DX_END, NZ)]
     )(dens, force, r1, r0)
@@ -503,15 +524,16 @@
         [shape(BX // 2, BY, NZ), shape(2 * SWEEPS - 2, EXT, NZ)],
         scratch,
         flops=12 * SWEEPS * EXT * EXT * NZ,
-    )(dext, g0, phi, *weights)
+    )(dext, g0, base, *weights)
     pot_next, body_force = call(
         far_kernel,
         "sweeps_far",
         [VMEM] * 14,
         [core, shape(3, BX, BY, NZ)],
-        scratch,
+        scratch + [pltpu.VMEM((3, BX, BY, NZ), F32)] + [pltpu.VMEM((W, BY, NZ), F32)] * 2 + [pltpu.SemaphoreType.DMA((3,))],
         flops=8 * SWEEPS * EXT * EXT * NZ,
-    )(dext, g1, g0, fcore, phi, *weights, near, edges)
+        far_outs=(0, 1),
+    )(dext, g1, g0, fcore, base, *weights, near, edges)
     return conc_next, pot_next, body_force
 
 

time: 66 us -> 64.2 us (0.973); the launches traced: 64.8 us -> 63.8 us
  Pallas kernels: 19.9 us -> 17.6 us
  blocking collectives: 3.02 us -> 4.68 us
  waiting for transfers between devices: 5.05 us -> 3.73 us
  starting transfers between devices: 35.5 us -> 36.3 us
    all_gather x1, blocking collectives: 3.02 us -> 4.68 us  [chip_pair(): return lax.all_gather(block, 'gx', axis_index_groups=pairs)]
    pallas_call x1, Pallas kernels: 5.01 us -> 3.38 us  [body(): call(arrive_x_kernel, 'spread_x', [VMEM] * 11, [shape(3, BX, BY, NZ), sum...]
    ppermute x7, waiting for transfers between devices: 5.05 us -> 3.73 us  [swap(): return lax.ppermute(block, axis, route)]
    pallas_call x1, Pallas kernels: 1.24 us -> 2.52 us  [body(): call(coefficient_kernel, 'coefficients', [VMEM] * 8, [shape(3, BX, BY, NZ...]
    pallas_call x1, Pallas kernels: 2.64 us -> 1.75 us  [body(): call(arrive_y_kernel, 'spread_y', [VMEM] * 7, [*store(GROUP, jax.ShapeDty...]
    pallas_call x1, Pallas kernels: 5.82 us -> 4.92 us  [body(): call(kept_kernel, 'spread_kept', [VMEM] * 3, [shape(8, NZ), sums], flops=...]
    ppermute x7, starting transfers between devices: 35.5 us -> 36.3 us  [swap(): return lax.ppermute(block, axis, route)]
  transfers between devices with their start and end apart: 7 -> 7, of which waited for: 1 -> 2; matrix products, arithmetic and copies ran while one was open for 0% -> 0% of each run, Pallas kernels for 17% -> 16%
where the time goes in v7:
time: 64.2 us; the launch traced here: 63.8 us
  starting transfers between devices  36.3 us (57%)
  Pallas kernels  17.6 us (27%)
  blocking collectives  4.68 us (7%)
  waiting for transfers between devices  3.73 us (6%)
  between operations  1.42 us (2%)
    ppermute x7, starting transfers between devices, swap(): return lax.ppermute(block, axis, route)  36.3 us
    pallas_call x1, Pallas kernels, body(): call(kept_kernel, 'spread_kept', [VMEM] * 3, [shape(8, NZ), sums], flops=...  4.92 us
    all_gather x1, blocking collectives, chip_pair(): return lax.all_gather(block, 'gx', axis_index_groups=pairs)  4.68 us
    ppermute x7, waiting for transfers between devices, swap(): return lax.ppermute(block, axis, route)  3.73 us
    pallas_call x1, Pallas kernels, body(): call(arrive_x_kernel, 'spread_x', [VMEM] * 11, [shape(3, BX, BY, NZ), sum...  3.38 us
    pallas_call x1, Pallas kernels, body(): call(coefficient_kernel, 'coefficients', [VMEM] * 8, [shape(3, BX, BY, NZ...  2.52 us
    pallas_call x1, Pallas kernels, body(): call(first_kernel, 'first', [HBM] * 8 + [SMEM], [shape(Y_END, 8, NZ), sha...  1.98 us
    pallas_call x1, Pallas kernels, body(): call(arrive_y_kernel, 'spread_y', [VMEM] * 7, [*store(GROUP, jax.ShapeDty...  1.75 us
  transfers between devices with their start and end apart: 7, of which 2 were waited for; matrix products, arithmetic and copies ran while one was open for 0% of the time, Pallas kernels for 16%

profile of v7, /device:TPU:1, one launch (start us, length us, event | category | flops | bytes accessed | tf_op | source)
XLA Modules:
  0.0 63.8 jit_solution(8941444006487761545)
XLA Ops:
  1.3 2.0 %first.1 = (f32[47,8,128]{2,1,0:T(8,128)S(1)}, f32[47,8,128]{2,1,0:T(8,128)S(1)}, f32[3,16,16,128]{3,2,1,0:T(8,128)S(1)}, f32[16,16,128]{2,1,0:T(8,128)S(1)}, f3...) custom-call(f32[3,16,16,128]{3,2,1,0:T(8,128)} %conc_h.1, ...), custom_call_target="tpu_custom_call" | custom-call | bytes 1548288 | tf_op jit(solution)/shard_map/first/pallas_call | solution.py:470
  3.3 5.5 %collective-permute-start = (f32[47,8,128]{2,1,0:T(8,128)S(1)}, f32[47,8,128]{2,1,0:T(8,128)S(1)}, u32[]{:S(2)}, u32[]{:S(2)}) collective-permute-start(f32[47,8,128]{2,1,0:T(8,128)S(1)} %get-tuple-element.48), channel_id=1, source_target_pairs={{0,1},{1,0},{2,3},{3,2},{4,5},{5,4},{6,7},{7,6},{8,9},{9,8},{10,11... | collective-permute-start | bytes 577544 | tf_op jit(solution)/shard_map/ppermute | solution.py:45
  8.8 5.0 %collective-permute-start.1 = (f32[47,8,128]{2,1,0:T(8,128)S(1)}, f32[47,8,128]{2,1,0:T(8,128)S(1)}, u32[]{:S(2)}, u32[]{:S(2)}) collective-permute-start(f32[47,8,128]{2,1,0:T(8,128)S(1)} %get-tuple-element.49), channel_id=1, source_target_pairs={{0,15},{1,2},{2,1},{3,4},{4,3},{5,6},{6,5},{7,8},{8,7},{9,10},{10,... | collective-permute-start | bytes 577544 | tf_op jit(solution)/shard_map/ppermute | solution.py:45
  13.8 4.9 %spread_kept.1 = (f32[8,128]{1,0:T(8,128)S(1)}, f32[2,1296,128]{2,1,0:T(8,128)S(1)}) custom-call(f32[136,4,128]{2,1,0:T(4,128)S(1)} %get-tuple-element.44.rows.rows_in, s32[136,1,128]{2,1,0:T(1,128)S(1)} %get-tuple-element.45.cells.cells_in, f32[8,128]{1,0:T(8,128)S(1)} %get-tuple-element.46.state), custom_call_target="tpu_custom_call" | custom-call | flops 6115295232 | bytes 1331200 | tf_op jit(solution)/shard_map/spread_kept/pallas_call | solution.py:482
  18.7 0.0 collective-permute-done.y0
  18.7 0.1 collective-permute-done.1.y1
  18.8 0.1 pack_x.1
  18.9 7.5 %collective-permute-start.2 = (f32[79,8,128]{2,1,0:T(8,128)S(1)}, f32[79,8,128]{2,1,0:T(8,128)S(1)}, u32[]{:S(2)}, u32[]{:S(2)}) collective-permute-start(f32[79,8,128]{2,1,0:T(8,128)S(1)} %get-tuple-element.59), channel_id=1, source_target_pairs={{0,496},{16,32},{32,16},{48,64},{64,48},{80,96},{96,80},{112,128},... | collective-permute-start | bytes 970760 | tf_op jit(solution)/shard_map/ppermute | solution.py:45
  26.4 6.2 %collective-permute-start.3 = (f32[79,8,128]{2,1,0:T(8,128)S(1)}, f32[79,8,128]{2,1,0:T(8,128)S(1)}, u32[]{:S(2)}, u32[]{:S(2)}) collective-permute-start(f32[79,8,128]{2,1,0:T(8,128)S(1)} %get-tuple-element.60), channel_id=1, source_target_pairs={{0,16},{16,0},{32,48},{48,32},{64,80},{80,64},{96,112},{112,96},{1... | collective-permute-start | bytes 970760 | tf_op jit(solution)/shard_map/ppermute | solution.py:45
  32.7 1.7 %spread_y.1 = (f32[8,4,128]{2,1,0:T(4,128)S(1)}, s32[8,1,128]{2,1,0:T(1,128)S(1)}, f32[8,128]{1,0:T(8,128)S(1)}, f32[2,1296,128]{2,1,0:T(8,128)S(1)}) custom-call(f32[2,1296,128]{2,1,0:T(8,128)S(1)} %get-tuple-element.47.acc_in, f32[136,4,128]{2,1,0:T(4,128)S(1)} %get-tuple-element.44.rows.rows_in, ...), custom_call_target="tpu_custom_call", output_to_operand_aliasing={{3}: (0, {})} | custom-call | flops 4076863488 | bytes 1351680 | tf_op jit(solution)/shard_map/spread_y/pallas_call | solution.py:487
  34.5 0.0 collective-permute-done.2.x1
  34.5 0.0 collective-permute-done.3.x0
  34.5 3.4 %spread_x.1 = (f32[3,16,16,128]{3,2,1,0:T(8,128)S(1)}, f32[2,1296,128]{2,1,0:T(8,128)S(1)}, f32[18,32,128]{2,1,0:T(8,128)S(1)}, f32[200,128]{1,0:T(8,128)S(1)}, f32[200,128]{1,0:T(8,128)S(1)}) custom-call(f32[2,1296,128]{2,1,0:T(8,128)S(1)} %get-tuple-element.51.acc_in, f32[8,4,128]{2,1,0:T(4,128)S(1)} %get-tuple-element.52.rows, ...), custom_call_target="tpu_custom_call", output_to_operand_aliasing={{1}: (0, {})} | custom-call | flops 2717908992 | bytes 2220032 | tf_op jit(solution)/shard_map/spread_x/pallas_call | solution.py:496
  37.9 8.1 %collective-permute-start.4 = (f32[200,128]{1,0:T(8,128)S(1)}, f32[200,128]{1,0:T(8,128)S(1)}, u32[]{:S(2)}, u32[]{:S(2)}) collective-permute-start(f32[200,128]{1,0:T(8,128)S(1)} %get-tuple-element.67), channel_id=1, source_target_pairs={{0,15},{1,2},{2,1},{3,4},{4,3},{5,6},{6,5},{7,8},{8,7},{9,10},{10,... | collective-permute-start | bytes 307208 | tf_op jit(solution)/shard_map/ppermute | solution.py:45
  46.0 2.0 %collective-permute-start.5 = (f32[200,128]{1,0:T(8,128)S(1)}, f32[200,128]{1,0:T(8,128)S(1)}, u32[]{:S(2)}, u32[]{:S(2)}) collective-permute-start(f32[200,128]{1,0:T(8,128)S(1)} %get-tuple-element.68), channel_id=1, source_target_pairs={{0,1},{1,0},{2,3},{3,2},{4,5},{5,4},{6,7},{7,6},{8,9},{9,8},{10,11... | collective-permute-start | bytes 307208 | tf_op jit(solution)/shard_map/ppermute | solution.py:45
  48.0 2.5 %coefficients.1 = (f32[3,16,16,128]{3,2,1,0:T(8,128)}, f32[3,18,16,128]{3,2,1,0:T(8,128)S(1)}, f32[32,32,128]{2,1,0:T(8,128)S(1)}, f32[32,32,128]{2,1,0:T(8,128)...) custom-call(f32[2,1296,128]{2,1,0:T(8,128)S(1)} %get-tuple-element.6, ...), custom_call_target="tpu_custom_call" | custom-call | flops 679477248 | bytes 5029888 | tf_op jit(solution)/shard_map/coefficients/pallas_call | solution.py:506
  50.5 0.0 collective-permute-done.4.r1
  50.5 3.6 %collective-permute-done.5.r0 = f32[200,128]{1,0:T(8,128)S(1)} collective-permute-done((f32[200,128]{1,0:T(8,128)S(1)}, f32[200,128]{1,0:T(8,128)S(1)}, u32[]{:S(2)}, u32[]{:S(2)}) %collective-permute-start.5) | collective-permute-done | bytes 102432 | tf_op jit(solution)/shard_map/ppermute | solution.py:45
  54.2 0.2 join_y.1
  54.3 1.9 %collective-permute-start.6 = (f32[232,128]{1,0:T(8,128)S(1)}, f32[232,128]{1,0:T(8,128)S(1)}, u32[]{:S(2)}, u32[]{:S(2)}) collective-permute-start(f32[232,128]{1,0:T(8,128)S(1)} %get-tuple-element.70), channel_id=1, source_target_pairs={{0,496},{16,32},{32,16},{48,64},{64,48},{80,96},{96,80},{112,128},... | collective-permute-start | bytes 356360 | tf_op jit(solution)/shard_map/ppermute | solution.py:45
  56.3 4.7 %all-gather = f32[464,128]{1,0:T(8,128)S(1)} all-gather(f32[232,128]{1,0:T(8,128)S(1)} %get-tuple-element.71), channel_id=2, replica_groups={{0,16},{32,48},{64,80},{96,112},{128,144},{160,176},{192,208},{224,240}..., dimensions={0}, use_global_device_ids=true | all-gather | bytes 356352 | tf_op jit(solution)/shard_map/all_gather | solution.py:50
  60.9 1.2 %sweeps_near.1 = (f32[8,16,128]{2,1,0:T(8,128)S(1)}, f32[14,32,128]{2,1,0:T(8,128)S(1)}) custom-call(f32[32,32,128]{2,1,0:T(8,128)S(1)} %get-tuple-element.69.dext, f32[2,232,128]{2,1,0:T(8,128)S(1)} %bitcast.1, f32[32,32,128]{2,1,0:T(8,128)S(1)} %get-tuple-element.73.base, f32[32,32,128]{2,1,0:T(8,128)S(1)} %get-tuple-element.74.xp, ...), custom_call_target="tpu_custom_call" | custom-call | flops 12582912 | bytes 294912 | tf_op jit(solution)/shard_map/sweeps_near/pallas_call | solution.py:520
  62.2 0.0 collective-permute-done.6.r1
  62.2 1.6 %sweeps_far.1 = (f32[16,16,128]{2,1,0:T(8,128)}, f32[3,16,16,128]{3,2,1,0:T(8,128)}) custom-call(f32[32,32,128]{2,1,0:T(8,128)S(1)} %get-tuple-element.69.dext, f32[232,128]{1,0:T(8,128)S(1)} %collective-permute-done.6.r1, f32[2,232,128]{2,1,0:T(8,128)S(1)} %bitcast.2, f32[3,18,16,128]{3,2,1,0:T(8,128)S(1)} %get-tuple-element.72.fcore, ...), custom_call_target="tpu_custom_call" | custom-call | flops 8388608 | bytes 524288 | tf_op jit(solution)/shard_map/sweeps_far/pallas_call | solution.py:528
Async XLA Ops:
  3.3 15.5 %collective-permute-start = (f32[47,8,128]{2,1,0:T(8,128)S(1)}, f32[47,8,128]{2,1,0:T(8,128)S(1)}, u32[]{:S(2)}, u32[]{:S(2)}) collective-permute-start(f32[47,8,128]{2,1,0:T(8,128)S(1)} %get-tuple-element.48), channel_id=1, source_target_pairs={{0,1},{1,0},{2,3},{3,2},{4,5},{5,4},{6,7},{7,6},{8,9},{9,8},{10,11... | collective-permute-start | bytes 577544 | tf_op jit(solution)/shard_map/ppermute | solution.py:45
  8.8 10.1 %collective-permute-start.1 = (f32[47,8,128]{2,1,0:T(8,128)S(1)}, f32[47,8,128]{2,1,0:T(8,128)S(1)}, u32[]{:S(2)}, u32[]{:S(2)}) collective-permute-start(f32[47,8,128]{2,1,0:T(8,128)S(1)} %get-tuple-element.49), channel_id=1, source_target_pairs={{0,15},{1,2},{2,1},{3,4},{4,3},{5,6},{6,5},{7,8},{8,7},{9,10},{10,... | collective-permute-start | bytes 577544 | tf_op jit(solution)/shard_map/ppermute | solution.py:45
  18.9 15.6 %collective-permute-start.2 = (f32[79,8,128]{2,1,0:T(8,128)S(1)}, f32[79,8,128]{2,1,0:T(8,128)S(1)}, u32[]{:S(2)}, u32[]{:S(2)}) collective-permute-start(f32[79,8,128]{2,1,0:T(8,128)S(1)} %get-tuple-element.59), channel_id=1, source_target_pairs={{0,496},{16,32},{32,16},{48,64},{64,48},{80,96},{96,80},{112,128},... | collective-permute-start | bytes 970760 | tf_op jit(solution)/shard_map/ppermute | solution.py:45
  26.4 8.0 %collective-permute-start.3 = (f32[79,8,128]{2,1,0:T(8,128)S(1)}, f32[79,8,128]{2,1,0:T(8,128)S(1)}, u32[]{:S(2)}, u32[]{:S(2)}) collective-permute-start(f32[79,8,128]{2,1,0:T(8,128)S(1)} %get-tuple-element.60), channel_id=1, source_target_pairs={{0,16},{16,0},{32,48},{48,32},{64,80},{80,64},{96,112},{112,96},{1... | collective-permute-start | bytes 970760 | tf_op jit(solution)/shard_map/ppermute | solution.py:45
  37.9 12.7 %collective-permute-start.4 = (f32[200,128]{1,0:T(8,128)S(1)}, f32[200,128]{1,0:T(8,128)S(1)}, u32[]{:S(2)}, u32[]{:S(2)}) collective-permute-start(f32[200,128]{1,0:T(8,128)S(1)} %get-tuple-element.67), channel_id=1, source_target_pairs={{0,15},{1,2},{2,1},{3,4},{4,3},{5,6},{6,5},{7,8},{8,7},{9,10},{10,... | collective-permute-start | bytes 307208 | tf_op jit(solution)/shard_map/ppermute | solution.py:45
  46.0 8.1 %collective-permute-start.5 = (f32[200,128]{1,0:T(8,128)S(1)}, f32[200,128]{1,0:T(8,128)S(1)}, u32[]{:S(2)}, u32[]{:S(2)}) collective-permute-start(f32[200,128]{1,0:T(8,128)S(1)} %get-tuple-element.68), channel_id=1, source_target_pairs={{0,1},{1,0},{2,3},{3,2},{4,5},{5,4},{6,7},{7,6},{8,9},{9,8},{10,11... | collective-permute-start | bytes 307208 | tf_op jit(solution)/shard_map/ppermute | solution.py:45
  54.3 7.8 %collective-permute-start.6 = (f32[232,128]{1,0:T(8,128)S(1)}, f32[232,128]{1,0:T(8,128)S(1)}, u32[]{:S(2)}, u32[]{:S(2)}) collective-permute-start(f32[232,128]{1,0:T(8,128)S(1)} %get-tuple-element.70), channel_id=1, source_target_pairs={{0,496},{16,32},{32,16},{48,64},{64,48},{80,96},{96,80},{112,128},... | collective-permute-start | bytes 356360 | tf_op jit(solution)/shard_map/ppermute | solution.py:45

commit v8 on v7

--- a/solution.py
+++ b/solution.py
@@ -21,11 +21,14 @@
 PAIRS = WIDE * WIDE // 2
 ROWS = PAIRS * 2 * CHANNELS
 GROUP = 8
-EARLY = 9
+EARLY = 8
 STORE = SLOTS + GROUP
 
 Y_CONC, Y_POT, Y_EPS, Y_NUM, Y_END = 8, 14, 30, 46, 47
-X_CONC, X_POT, X_EPS, X_NUM, X_END = 8, 14, 46, 78, 79
+X_AT = [0] + [sum(EXT - 2 * d for d in range(1, n + 1)) for n in range(W + 1)]
+X_CONC, X_NUM, X_POT = 64, 112, 120
+X_EPS = X_POT + X_AT[W + 1]
+X_END = X_EPS + X_AT[W + 1]
 DY_FORCE, DY_END = WIDE * W, WIDE * W + 56
 DX_AT = [sum(EXT - 2 - 2 * d for d in range(n)) for n in range(W + 1)]
 DX_FORCE, DX_END = DX_AT[W], DX_AT[W] + 3 * BY
@@ -95,11 +98,11 @@
     return jnp.max(tile).astype(jnp.int32)
 
 
-def append(total, buf, number_tile, way, nodes, rec, cells):
+def append(total, buf, number, way, nodes, rec, cells):
     for k in range(MOVERS):
-        rec[total + k] = buf[k // 2, (k % 2) * 4 : (k % 2) * 4 + 4]
+        rec[total + k] = buf[record(buf, k)]
         cells[total + k] = nodes[0, way, k : k + 1]
-    return total + number_in(buf[number_tile])
+    return total + number_in(number)
 
 
 def way_of(axis, odd):
@@ -108,16 +111,19 @@
     return up, (1 if axis == "gx" else 3) - up
 
 
-def pack_records(out, rec, slots, number, way, number_tile):
-    out[number_tile] = jnp.full((8, NZ), number.astype(F32))
+def pack_records(out, rec, slots, number, way):
     for k in range(MOVERS):
         row = rec[slots[0, way, k]]
-        out[k // 2, (k % 2) * 4 : (k % 2) * 4 + 4] = jnp.where(k < number, row, 0.0)
+        out[record(out, k)] = jnp.where(k < number, row, 0.0)
+
+
+def record(buf, k):
+    return (k // 2, pl.ds((k % 2) * 4, 4)) if len(buf.shape) == 3 else (pl.ds(4 * k, 4),)
 
 
 def first_kernel(
     conc_h, pot_h, eps_h, rec_h, nodes_h, arrive_h, slots_h, counts_h, count,
-    s1, s0, conc, pot, eps, arrive, xr, rows, cells, state,
+    s1, s0, conc, pot, eps, arrive, xr, rows, cells, state, acc,
     rec, nodes, slots, counts, gone, sems,
 ):
     copies = [(slots_h, slots), (counts_h, counts), (rec_h, rec), (nodes_h, nodes), (conc_h, conc)]
@@ -129,6 +135,7 @@
     copies = [pltpu.make_async_copy(a, b, sems.at[n]) for n, (a, b) in enumerate(copies)]
     for copy in copies:
         copy.start()
+    acc[...] = jnp.zeros_like(acc)
 
     def clear(c, _):
         gone[c] = 0
@@ -145,7 +152,7 @@
 
         lax.fori_loop(0, counts[0, way], mark, 0)
     live = count[0]
-    for copy in copies[2:]:
+    for copy in copies[2:4]:
         copy.wait()
 
     def gather(c, found):
@@ -156,21 +163,28 @@
 
     found = lax.fori_loop(0, SLOTS, gather, 0, unroll=16)
     state[...] = jnp.full((8, NZ), found.astype(F32))
+    copies[4].wait()
     for odd in range(2):
         up, way = way_of("gx", odd)
-        pack_records(xr.at[odd], rec, slots, counts[0, way], way, X_POT)
-        xr[odd, X_CONC:X_POT] = conc[:, up * (BX - 1)].reshape(6, 8, NZ)
+        number = counts[0, way]
+        pack_records(xr.at[odd], rec, slots, number, way)
+        xr[odd, X_CONC:X_NUM] = conc[:, up * (BX - 1)].reshape(X_NUM - X_CONC, NZ)
+        xr[odd, X_NUM:X_POT] = jnp.full((8, NZ), number.astype(F32))
     for odd, out in enumerate((s0, s1)):
         up, way = way_of("gy", odd)
-        pack_records(out, rec, slots, counts[0, way], way, Y_NUM)
+        number = counts[0, way]
+        pack_records(out, rec, slots, number, way)
+        out[Y_NUM] = jnp.full((8, NZ), number.astype(F32))
         for s in range(3):
             face = jnp.where(up == 1, conc[s, :, BY - 1], conc[s, :, 0])
             out[Y_CONC + 2 * s : Y_CONC + 2 * s + 2] = face.reshape(2, 8, NZ)
-
-
-def kept_kernel(rows, cells, state, state_out, acc):
+    for copy in copies[5:]:
+        copy.wait()
+
+
+def kept_kernel(acc_in, rows, cells, state, state_out, acc):
+    del acc_in
     state_out[...] = state[...]
-    acc[...] = jnp.zeros_like(acc)
     spread_groups(0, jnp.minimum(EARLY, number_in(state[...]) // GROUP), rows, cells, acc)
 
 
@@ -178,17 +192,17 @@
     del state
     px, py = parity("gx"), parity("gy")
     for n, (out, up) in enumerate(((s0, 1 - px), (s1, px))):
-        out[0:X_POT] = xr[n, 0:X_POT]
-        out[X_NUM] = xr[n, X_POT]
+        out[0:X_POT] = xr[n]
         for first, own, tile in ((X_POT, pot, Y_POT), (X_EPS, eps, Y_EPS)):
-            own = own[pl.ds(up * W, W)]
-            a, b = y0[pl.ds(tile + up * W, W)], y1[pl.ds(tile + up * W, W)]
-            low, high = jnp.where(py == 1, a, b), jnp.where(py == 1, b, a)
-            for x in range(W):
-                out[first + 4 * x] = low[x]
-                out[first + 4 * x + 1] = own[x, 0:8]
-                out[first + 4 * x + 2] = own[x, 8:16]
-                out[first + 4 * x + 3] = high[x]
+            for d in range(1, W + 1):
+                x = jnp.where(up == 1, BX - d, d - 1)
+                a, b = y0[tile + x], y1[tile + x]
+                low, high = jnp.where(py == 1, a, b), jnp.where(py == 1, b, a)
+                at = first + X_AT[d]
+                if d < W:
+                    out[at : at + W - d] = low[d:]
+                    out[at + W - d + BY : at + 2 * (W - d) + BY] = high[: W - d]
+                out[at + W - d : at + W - d + BY] = own[x]
 
 
 def arrive_y_kernel(acc_in, rows_in, cells_in, state, y0, y1, nodes, rows, cells, state_out, acc, rec, cell):
@@ -197,8 +211,8 @@
     rec[0:STORE] = rows_in[...]
     cell[0:STORE] = cells_in[...]
     found = number_in(state[...])
-    total = append(found, y0, Y_NUM, 3 - py, nodes, rec, cell)
-    total = append(total, y1, Y_NUM, 2 + py, nodes, rec, cell)
+    total = append(found, y0, y0[Y_NUM], 3 - py, nodes, rec, cell)
+    total = append(total, y1, y1[Y_NUM], 2 + py, nodes, rec, cell)
     done = total // GROUP
     spread_groups(jnp.minimum(EARLY, found // GROUP), done, rec, cell, acc)
     for g in range(GROUP):
@@ -223,8 +237,8 @@
     del acc_in
     rec[0:GROUP] = rows[...]
     cell[0:GROUP] = cells[...]
-    total = append(number_in(state[...]), x0, X_NUM, 1 - px, nodes, rec, cell)
-    total = append(total, x1, X_NUM, px, nodes, rec, cell)
+    total = append(number_in(state[...]), x0, x0[X_NUM:X_POT], 1 - px, nodes, rec, cell)
+    total = append(total, x1, x1[X_NUM:X_POT], px, nodes, rec, cell)
     for g in range(GROUP):
         rec[total + g] = jnp.zeros((CHANNELS, NODES), F32)
         cell[total + g] = jnp.zeros((1, NODES), jnp.int32)
@@ -233,14 +247,13 @@
     for f in range(4):
         wide[f, 1 : BX + 1, 8 : 8 + BY] = conc[f] if f < 3 else pot[...]
         if f < 3:
-            xa, xb = (x[X_CONC + 2 * f : X_CONC + 2 * f + 2].reshape(BY, NZ) for x in (x0, x1))
+            xa, xb = (x[X_CONC + BY * f : X_CONC + BY * f + BY] for x in (x0, x1))
             x_low, x_high = jnp.where(x_low_first, xa, xb), jnp.where(x_low_first, xb, xa)
             ya, yb = (y[Y_CONC + 2 * f : Y_CONC + 2 * f + 2].reshape(BX, NZ) for y in (y0, y1))
             y_low, y_high = jnp.where(y_low_first, ya, yb), jnp.where(y_low_first, yb, ya)
         else:
-            last, first = X_POT + 4 * (W - 1) + 1, X_POT + 1
-            x_low = jnp.where(x_low_first, x0[last : last + 2], x1[last : last + 2]).reshape(BY, NZ)
-            x_high = jnp.where(x_low_first, x1[first : first + 2], x0[first : first + 2]).reshape(BY, NZ)
+            xa, xb = (x[X_POT + W - 1 : X_POT + W - 1 + BY] for x in (x0, x1))
+            x_low, x_high = jnp.where(x_low_first, xa, xb), jnp.where(x_low_first, xb, xa)
             y_low = jnp.where(y_low_first, y0[Y_POT:Y_EPS, 7], y1[Y_POT:Y_EPS, 7])
             y_high = jnp.where(y_low_first, y1[Y_POT:Y_EPS, 0], y0[Y_POT:Y_EPS, 0])
         wide[f, 0, 8 : 8 + BY] = x_low
@@ -302,10 +315,12 @@
             buf[W + n, 0:W] = jnp.where(y_low_first, a, b)
             buf[W + n, W : W + BY] = own[x]
             buf[W + n, W + BY : EXT] = jnp.where(y_low_first, b, a)
-        for n in range(W):
-            at = pl.ds(x_tile + 4 * mirrored(px, n, W - 1 - n), 4)
-            buf[n] = x1[at].reshape(EXT, NZ)
-            buf[W + BX + n] = x0[at].reshape(EXT, NZ)
+        for n in (*range(W), *range(W + BX, EXT)):
+            buf[n] = jnp.ones((EXT, NZ), F32)
+        for d in range(1, W + 1):
+            at = slice(x_tile + X_AT[d], x_tile + X_AT[d + 1])
+            buf[W - d, d : EXT - d] = x1[at]
+            buf[W + BX - 1 + d, d : EXT - d] = x0[at]
     for x in range(1, EXT - 1):
         e = ew[x]
         up, down = e + ew[x + 1], e + ew[x - 1]
@@ -467,22 +482,22 @@
     more = [pltpu.with_memory_space_constraint(x, pltpu.HBM) for x in (own_nodes, arrive_nodes)]
     small = [pltpu.SMEM((1, 4, MOVERS), jnp.int32), pltpu.SMEM((1, 4), jnp.int32)]
     rec = pltpu.VMEM((SLOTS, CHANNELS, NODES), F32)
-    a1, a0, conc_v, pot_v, eps_v, arrive_v, xr, rows, cells, state = call(
+    a1, a0, conc_v, pot_v, eps_v, arrive_v, xr, rows, cells, state, acc = call(
         first_kernel,
         "first",
         [HBM] * 8 + [SMEM],
         [
             shape(Y_END, 8, NZ), shape(Y_END, 8, NZ), shape(3, BX, BY, NZ), core, core,
             jax.ShapeDtypeStruct((1, 4, MOVERS, NODES), jnp.int32),
-            shape(2, X_POT + 1, 8, NZ), *store(STORE, jax.ShapeDtypeStruct), shape(8, NZ),
+            shape(2, X_POT, NZ), *store(STORE, jax.ShapeDtypeStruct), shape(8, NZ), sums,
         ],
         [rec, pltpu.VMEM((SLOTS, NODES), jnp.int32), *small, pltpu.SMEM((SLOTS,), jnp.int32), pltpu.SemaphoreType.DMA((12,))],
     )(*ins, *more, *lists, count)
     y0, y1 = swap(a0, "gy", 0), swap(a1, "gy", 1)
-    late, acc = call(kept_kernel, "spread_kept", [VMEM] * 3, [shape(8, NZ), sums], flops=row_flops * EARLY * GROUP)(
-        rows, cells, state
-    )
-    b1, b0 = call(pack_x_kernel, "pack_x", [VMEM] * 6, [shape(X_END, 8, NZ)] * 2)(xr, pot_v, eps_v, y1, y0, late)
+    late, acc = call(
+        kept_kernel, "spread_kept", [VMEM] * 4, [shape(8, NZ), sums], flops=row_flops * EARLY * GROUP, aliases={0: 1}
+    )(acc, rows, cells, state)
+    b1, b0 = call(pack_x_kernel, "pack_x", [VMEM] * 6, [shape(X_END, NZ)] * 2)(xr, pot_v, eps_v, y1, y0, late)
     x1, x0 = swap(b1, "gx", 1), swap(b0, "gx", 0)
     rows, cells, state, acc = call(
         arrive_y_kernel,

time: 64.2 us -> 63.7 us (level)
  Pallas kernels: 17.6 us -> 15.5 us
  waiting for transfers between devices: 3.73 us -> 5.6 us
  blocking collectives: 4.68 us -> 3.89 us
    pallas_call x2, Pallas kernels: 4.98 us -> 2.69 us  [the longest x1 2.63 us: body(): call(kept_kernel, 'spread_kept', [VMEM] * 4, [shape(8, NZ), sums], flops=...]
    ppermute x7, waiting for transfers between devices: 3.73 us -> 5.6 us  [swap(): return lax.ppermute(block, axis, route)]
    pallas_call x1, Pallas kernels: 1.75 us -> 2.64 us  [body(): call(arrive_y_kernel, 'spread_y', [VMEM] * 7, [*store(GROUP, jax.ShapeDty...]
    all_gather x1, blocking collectives: 4.68 us -> 3.89 us  [chip_pair(): return lax.all_gather(block, 'gx', axis_index_groups=pairs)]
  transfers between devices with their start and end apart: 7 -> 7, of which waited for: 2 -> 2; matrix products, arithmetic and copies ran while one was open for 0% -> 0% of each run, Pallas kernels for 16% -> 13%
where the time goes in v8:
time: 63.7 us; the launch traced here: 63.3 us
  starting transfers between devices  36.8 us (58%)
  Pallas kernels  15.5 us (24%)
  waiting for transfers between devices  5.6 us (9%)
  blocking collectives  3.89 us (6%)
  between operations  1.42 us (2%)
    ppermute x7, starting transfers between devices, swap(): return lax.ppermute(block, axis, route)  36.8 us
    ppermute x7, waiting for transfers between devices, swap(): return lax.ppermute(block, axis, route)  5.6 us
    all_gather x1, blocking collectives, chip_pair(): return lax.all_gather(block, 'gx', axis_index_groups=pairs)  3.89 us
    pallas_call x1, Pallas kernels, body(): call(arrive_x_kernel, 'spread_x', [VMEM] * 11, [shape(3, BX, BY, NZ), sum...  3.39 us
    pallas_call x1, Pallas kernels, body(): call(arrive_y_kernel, 'spread_y', [VMEM] * 7, [*store(GROUP, jax.ShapeDty...  2.64 us
    pallas_call x1, Pallas kernels, body(): call(kept_kernel, 'spread_kept', [VMEM] * 4, [shape(8, NZ), sums], flops=...  2.63 us
    pallas_call x1, Pallas kernels, body(): call(coefficient_kernel, 'coefficients', [VMEM] * 8, [shape(3, BX, BY, NZ...  2.08 us
    pallas_call x1, Pallas kernels, body(): call(first_kernel, 'first', [HBM] * 8 + [SMEM], [shape(Y_END, 8, NZ), sha...  1.82 us
  transfers between devices with their start and end apart: 7, of which 2 were waited for; matrix products, arithmetic and copies ran while one was open for 0% of the time, Pallas kernels for 13%

profile of v8, /device:TPU:1, one launch (start us, length us, event | category | flops | bytes accessed | tf_op | source)
XLA Modules:
  0.0 63.3 jit_solution(10841568029217921290)
XLA Ops:
  1.3 1.8 %first.1 = (f32[47,8,128]{2,1,0:T(8,128)S(1)}, f32[47,8,128]{2,1,0:T(8,128)S(1)}, f32[3,16,16,128]{3,2,1,0:T(8,128)S(1)}, f32[16,16,128]{2,1,0:T(8,128)S(1)}, f3...) custom-call(f32[3,16,16,128]{3,2,1,0:T(8,128)} %conc_h.1, ...), custom_call_target="tpu_custom_call" | custom-call | bytes 2875392 | tf_op jit(solution)/shard_map/first/pallas_call | solution.py:485
  3.1 5.5 %collective-permute-start = (f32[47,8,128]{2,1,0:T(8,128)S(1)}, f32[47,8,128]{2,1,0:T(8,128)S(1)}, u32[]{:S(2)}, u32[]{:S(2)}) collective-permute-start(f32[47,8,128]{2,1,0:T(8,128)S(1)} %get-tuple-element.50), channel_id=1, source_target_pairs={{0,1},{1,0},{2,3},{3,2},{4,5},{5,4},{6,7},{7,6},{8,9},{9,8},{10,11... | collective-permute-start | bytes 577544 | tf_op jit(solution)/shard_map/ppermute | solution.py:48
  8.6 5.0 %collective-permute-start.1 = (f32[47,8,128]{2,1,0:T(8,128)S(1)}, f32[47,8,128]{2,1,0:T(8,128)S(1)}, u32[]{:S(2)}, u32[]{:S(2)}) collective-permute-start(f32[47,8,128]{2,1,0:T(8,128)S(1)} %get-tuple-element.51), channel_id=1, source_target_pairs={{0,15},{1,2},{2,1},{3,4},{4,3},{5,6},{6,5},{7,8},{8,7},{9,10},{10,... | collective-permute-start | bytes 577544 | tf_op jit(solution)/shard_map/ppermute | solution.py:48
  13.6 2.6 %spread_kept.1 = (f32[8,128]{1,0:T(8,128)S(1)}, f32[2,1296,128]{2,1,0:T(8,128)S(1)}) custom-call(f32[2,1296,128]{2,1,0:T(8,128)S(1)} %get-tuple-element.45.acc_in, f32[136,4,128]{2,1,0:T(4,128)S(1)} %get-tuple-element.46.rows.rows_in, s32[136,1,128]{2,1,0:T(1,128)S(1)} %get-tuple-element.47.cells.cells_in, ...), custom_call_target="tpu_custom_call", output_to_operand_aliasing={{1}: (0, {})} | custom-call | flops 5435817984 | bytes 1331200 | tf_op jit(solution)/shard_map/spread_kept/pallas_call | solution.py:497
  16.2 0.0 collective-permute-done.y0
  16.2 2.5 %collective-permute-done.1.y1 = f32[47,8,128]{2,1,0:T(8,128)S(1)} collective-permute-done((f32[47,8,128]{2,1,0:T(8,128)S(1)}, f32[47,8,128]{2,1,0:T(8,128)S(1)}, u32[]{:S(2)}, u32[]{:S(2)}) %collective-permute-start.1) | collective-permute-done | bytes 192544 | tf_op jit(solution)/shard_map/ppermute | solution.py:48
  18.7 0.1 pack_x.1
  18.7 6.5 %collective-permute-start.2 = (f32[488,128]{1,0:T(8,128)S(1)}, f32[488,128]{1,0:T(8,128)S(1)}, u32[]{:S(2)}, u32[]{:S(2)}) collective-permute-start(f32[488,128]{1,0:T(8,128)S(1)} %get-tuple-element.61), channel_id=1, source_target_pairs={{0,496},{16,32},{32,16},{48,64},{64,48},{80,96},{96,80},{112,128},... | collective-permute-start | bytes 749576 | tf_op jit(solution)/shard_map/ppermute | solution.py:48
  25.2 7.3 %collective-permute-start.3 = (f32[488,128]{1,0:T(8,128)S(1)}, f32[488,128]{1,0:T(8,128)S(1)}, u32[]{:S(2)}, u32[]{:S(2)}) collective-permute-start(f32[488,128]{1,0:T(8,128)S(1)} %get-tuple-element.62), channel_id=1, source_target_pairs={{0,16},{16,0},{32,48},{48,32},{64,80},{80,64},{96,112},{112,96},{1... | collective-permute-start | bytes 749576 | tf_op jit(solution)/shard_map/ppermute | solution.py:48
  32.5 2.6 %spread_y.1 = (f32[8,4,128]{2,1,0:T(4,128)S(1)}, s32[8,1,128]{2,1,0:T(1,128)S(1)}, f32[8,128]{1,0:T(8,128)S(1)}, f32[2,1296,128]{2,1,0:T(8,128)S(1)}) custom-call(f32[2,1296,128]{2,1,0:T(8,128)S(1)} %get-tuple-element.49.acc_in, f32[136,4,128]{2,1,0:T(4,128)S(1)} %get-tuple-element.46.rows.rows_in, ...), custom_call_target="tpu_custom_call", output_to_operand_aliasing={{3}: (0, {})} | custom-call | flops 4076863488 | bytes 1351680 | tf_op jit(solution)/shard_map/spread_y/pallas_call | solution.py:502
  35.2 0.0 collective-permute-done.2.x1
  35.2 0.0 collective-permute-done.3.x0
  35.2 3.4 %spread_x.1 = (f32[3,16,16,128]{3,2,1,0:T(8,128)S(1)}, f32[2,1296,128]{2,1,0:T(8,128)S(1)}, f32[18,32,128]{2,1,0:T(8,128)S(1)}, f32[200,128]{1,0:T(8,128)S(1)}, f32[200,128]{1,0:T(8,128)S(1)}) custom-call(f32[2,1296,128]{2,1,0:T(8,128)S(1)} %get-tuple-element.53.acc_in, f32[8,4,128]{2,1,0:T(4,128)S(1)} %get-tuple-element.54.rows, ...), custom_call_target="tpu_custom_call", output_to_operand_aliasing={{1}: (0, {})} | custom-call | flops 2717908992 | bytes 2220032 | tf_op jit(solution)/shard_map/spread_x/pallas_call | solution.py:511
  38.6 8.8 %collective-permute-start.4 = (f32[200,128]{1,0:T(8,128)S(1)}, f32[200,128]{1,0:T(8,128)S(1)}, u32[]{:S(2)}, u32[]{:S(2)}) collective-permute-start(f32[200,128]{1,0:T(8,128)S(1)} %get-tuple-element.69), channel_id=1, source_target_pairs={{0,15},{1,2},{2,1},{3,4},{4,3},{5,6},{6,5},{7,8},{8,7},{9,10},{10,... | collective-permute-start | bytes 307208 | tf_op jit(solution)/shard_map/ppermute | solution.py:48
  47.4 1.9 %collective-permute-start.5 = (f32[200,128]{1,0:T(8,128)S(1)}, f32[200,128]{1,0:T(8,128)S(1)}, u32[]{:S(2)}, u32[]{:S(2)}) collective-permute-start(f32[200,128]{1,0:T(8,128)S(1)} %get-tuple-element.70), channel_id=1, source_target_pairs={{0,1},{1,0},{2,3},{3,2},{4,5},{5,4},{6,7},{7,6},{8,9},{9,8},{10,11... | collective-permute-start | bytes 307208 | tf_op jit(solution)/shard_map/ppermute | solution.py:48
  49.3 2.1 %coefficients.1 = (f32[3,16,16,128]{3,2,1,0:T(8,128)}, f32[3,18,16,128]{3,2,1,0:T(8,128)S(1)}, f32[32,32,128]{2,1,0:T(8,128)S(1)}, f32[32,32,128]{2,1,0:T(8,128)...) custom-call(f32[2,1296,128]{2,1,0:T(8,128)S(1)} %get-tuple-element.6, ...), custom_call_target="tpu_custom_call" | custom-call | flops 679477248 | bytes 5029888 | tf_op jit(solution)/shard_map/coefficients/pallas_call | solution.py:521
  51.4 0.0 collective-permute-done.4.r1
  51.4 3.1 %collective-permute-done.5.r0 = f32[200,128]{1,0:T(8,128)S(1)} collective-permute-done((f32[200,128]{1,0:T(8,128)S(1)}, f32[200,128]{1,0:T(8,128)S(1)}, u32[]{:S(2)}, u32[]{:S(2)}) %collective-permute-start.5) | collective-permute-done | bytes 102432 | tf_op jit(solution)/shard_map/ppermute | solution.py:48
  54.5 0.2 join_y.1
  54.7 1.9 %collective-permute-start.6 = (f32[232,128]{1,0:T(8,128)S(1)}, f32[232,128]{1,0:T(8,128)S(1)}, u32[]{:S(2)}, u32[]{:S(2)}) collective-permute-start(f32[232,128]{1,0:T(8,128)S(1)} %get-tuple-element.72), channel_id=1, source_target_pairs={{0,496},{16,32},{32,16},{48,64},{64,48},{80,96},{96,80},{112,128},... | collective-permute-start | bytes 356360 | tf_op jit(solution)/shard_map/ppermute | solution.py:48
  56.6 3.9 %all-gather = f32[464,128]{1,0:T(8,128)S(1)} all-gather(f32[232,128]{1,0:T(8,128)S(1)} %get-tuple-element.73), channel_id=2, replica_groups={{0,16},{32,48},{64,80},{96,112},{128,144},{160,176},{192,208},{224,240}..., dimensions={0}, use_global_device_ids=true | all-gather | bytes 356352 | tf_op jit(solution)/shard_map/all_gather | solution.py:53
  60.5 1.1 %sweeps_near.1 = (f32[8,16,128]{2,1,0:T(8,128)S(1)}, f32[14,32,128]{2,1,0:T(8,128)S(1)}) custom-call(f32[32,32,128]{2,1,0:T(8,128)S(1)} %get-tuple-element.71.dext, f32[2,232,128]{2,1,0:T(8,128)S(1)} %bitcast.1, f32[32,32,128]{2,1,0:T(8,128)S(1)} %get-tuple-element.75.base, f32[32,32,128]{2,1,0:T(8,128)S(1)} %get-tuple-element.76.xp, ...), custom_call_target="tpu_custom_call" | custom-call | flops 12582912 | bytes 294912 | tf_op jit(solution)/shard_map/sweeps_near/pallas_call | solution.py:535
  61.7 0.0 collective-permute-done.6.r1
  61.7 1.6 %sweeps_far.1 = (f32[16,16,128]{2,1,0:T(8,128)}, f32[3,16,16,128]{3,2,1,0:T(8,128)}) custom-call(f32[32,32,128]{2,1,0:T(8,128)S(1)} %get-tuple-element.71.dext, f32[232,128]{1,0:T(8,128)S(1)} %collective-permute-done.6.r1, f32[2,232,128]{2,1,0:T(8,128)S(1)} %bitcast.2, f32[3,18,16,128]{3,2,1,0:T(8,128)S(1)} %get-tuple-element.74.fcore, ...), custom_call_target="tpu_custom_call" | custom-call | flops 8388608 | bytes 524288 | tf_op jit(solution)/shard_map/sweeps_far/pallas_call | solution.py:543
Async XLA Ops:
  3.1 13.1 %collective-permute-start = (f32[47,8,128]{2,1,0:T(8,128)S(1)}, f32[47,8,128]{2,1,0:T(8,128)S(1)}, u32[]{:S(2)}, u32[]{:S(2)}) collective-permute-start(f32[47,8,128]{2,1,0:T(8,128)S(1)} %get-tuple-element.50), channel_id=1, source_target_pairs={{0,1},{1,0},{2,3},{3,2},{4,5},{5,4},{6,7},{7,6},{8,9},{9,8},{10,11... | collective-permute-start | bytes 577544 | tf_op jit(solution)/shard_map/ppermute | solution.py:48
  8.6 10.1 %collective-permute-start.1 = (f32[47,8,128]{2,1,0:T(8,128)S(1)}, f32[47,8,128]{2,1,0:T(8,128)S(1)}, u32[]{:S(2)}, u32[]{:S(2)}) collective-permute-start(f32[47,8,128]{2,1,0:T(8,128)S(1)} %get-tuple-element.51), channel_id=1, source_target_pairs={{0,15},{1,2},{2,1},{3,4},{4,3},{5,6},{6,5},{7,8},{8,7},{9,10},{10,... | collective-permute-start | bytes 577544 | tf_op jit(solution)/shard_map/ppermute | solution.py:48
  18.7 16.4 %collective-permute-start.2 = (f32[488,128]{1,0:T(8,128)S(1)}, f32[488,128]{1,0:T(8,128)S(1)}, u32[]{:S(2)}, u32[]{:S(2)}) collective-permute-start(f32[488,128]{1,0:T(8,128)S(1)} %get-tuple-element.61), channel_id=1, source_target_pairs={{0,496},{16,32},{32,16},{48,64},{64,48},{80,96},{96,80},{112,128},... | collective-permute-start | bytes 749576 | tf_op jit(solution)/shard_map/ppermute | solution.py:48
  25.2 10.0 %collective-permute-start.3 = (f32[488,128]{1,0:T(8,128)S(1)}, f32[488,128]{1,0:T(8,128)S(1)}, u32[]{:S(2)}, u32[]{:S(2)}) collective-permute-start(f32[488,128]{1,0:T(8,128)S(1)} %get-tuple-element.62), channel_id=1, source_target_pairs={{0,16},{16,0},{32,48},{48,32},{64,80},{80,64},{96,112},{112,96},{1... | collective-permute-start | bytes 749576 | tf_op jit(solution)/shard_map/ppermute | solution.py:48
  38.6 12.8 %collective-permute-start.4 = (f32[200,128]{1,0:T(8,128)S(1)}, f32[200,128]{1,0:T(8,128)S(1)}, u32[]{:S(2)}, u32[]{:S(2)}) collective-permute-start(f32[200,128]{1,0:T(8,128)S(1)} %get-tuple-element.69), channel_id=1, source_target_pairs={{0,15},{1,2},{2,1},{3,4},{4,3},{5,6},{6,5},{7,8},{8,7},{9,10},{10,... | collective-permute-start | bytes 307208 | tf_op jit(solution)/shard_map/ppermute | solution.py:48
  47.4 7.2 %collective-permute-start.5 = (f32[200,128]{1,0:T(8,128)S(1)}, f32[200,128]{1,0:T(8,128)S(1)}, u32[]{:S(2)}, u32[]{:S(2)}) collective-permute-start(f32[200,128]{1,0:T(8,128)S(1)} %get-tuple-element.70), channel_id=1, source_target_pairs={{0,1},{1,0},{2,3},{3,2},{4,5},{5,4},{6,7},{7,6},{8,9},{9,8},{10,11... | collective-permute-start | bytes 307208 | tf_op jit(solution)/shard_map/ppermute | solution.py:48
  54.7 7.0 %collective-permute-start.6 = (f32[232,128]{1,0:T(8,128)S(1)}, f32[232,128]{1,0:T(8,128)S(1)}, u32[]{:S(2)}, u32[]{:S(2)}) collective-permute-start(f32[232,128]{1,0:T(8,128)S(1)} %get-tuple-element.72), channel_id=1, source_target_pairs={{0,496},{16,32},{32,16},{48,64},{64,48},{80,96},{96,80},{112,128},... | collective-permute-start | bytes 356360 | tf_op jit(solution)/shard_map/ppermute | solution.py:48

commit v9 on v8

--- a/solution.py
+++ b/solution.py
@@ -22,7 +22,7 @@
 ROWS = PAIRS * 2 * CHANNELS
 GROUP = 8
 EARLY = 8
-STORE = SLOTS + GROUP
+STORE = SLOTS + 4 * MOVERS + 2 * GROUP
 
 Y_CONC, Y_POT, Y_EPS, Y_NUM, Y_END = 8, 14, 30, 46, 47
 X_AT = [0] + [sum(EXT - 2 * d for d in range(1, n + 1)) for n in range(W + 1)]
@@ -86,7 +86,8 @@
         return group
 
     count = stop - start
-    first = lax.fori_loop(0, count // 2, groups(2 * GROUP), start * GROUP)
+    first = lax.fori_loop(0, count // 4, groups(4 * GROUP), start * GROUP)
+    first = lax.fori_loop(0, lax.rem(count, 4) // 2, groups(2 * GROUP), first)
     lax.fori_loop(0, lax.rem(count, 2), groups(GROUP), first)
 
 
@@ -145,12 +146,9 @@
     for copy in copies[:2]:
         copy.wait()
     for way in range(4):
-
-        def mark(k, _, way=way):
-            gone[slots[0, way, k]] = 1
-            return 0
-
-        lax.fori_loop(0, counts[0, way], mark, 0)
+        number = counts[0, way]
+        for k in range(MOVERS):
+            gone[jnp.where(k < number, slots[0, way, k], SLOTS)] = 1
     live = count[0]
     for copy in copies[2:4]:
         copy.wait()
@@ -205,20 +203,14 @@
                 out[at + W - d : at + W - d + BY] = own[x]
 
 
-def arrive_y_kernel(acc_in, rows_in, cells_in, state, y0, y1, nodes, rows, cells, state_out, acc, rec, cell):
+def arrive_y_kernel(acc_in, rows_in, cells_in, state, y0, y1, nodes, rows, cells, state_out, acc):
+    del acc_in, rows_in, cells_in
     py = parity("gy")
-    del acc_in
-    rec[0:STORE] = rows_in[...]
-    cell[0:STORE] = cells_in[...]
     found = number_in(state[...])
-    total = append(found, y0, y0[Y_NUM], 3 - py, nodes, rec, cell)
-    total = append(total, y1, y1[Y_NUM], 2 + py, nodes, rec, cell)
-    done = total // GROUP
-    spread_groups(jnp.minimum(EARLY, found // GROUP), done, rec, cell, acc)
-    for g in range(GROUP):
-        rows[g] = rec[done * GROUP + g]
-        cells[g] = cell[done * GROUP + g]
-    state_out[...] = jnp.full((8, NZ), (total - done * GROUP).astype(F32))
+    total = append(found, y0, y0[Y_NUM], 3 - py, nodes, rows, cells)
+    total = append(total, y1, y1[Y_NUM], 2 + py, nodes, rows, cells)
+    spread_groups(jnp.minimum(EARLY, found // GROUP), total // GROUP, rows, cells, acc)
+    state_out[...] = jnp.full((8, NZ), total.astype(F32))
 
 
 def spread_rows(acc, channel, ex, first, number):
@@ -228,21 +220,20 @@
 
 
 def arrive_x_kernel(
-    acc_in, rows, cells, state, x1, x0, y0, y1, nodes, conc, pot,
-    conc_next, acc, dens, s1, s0,
-    rec, cell, wide,
+    acc_in, rows_in, cells_in, state, x1, x0, y0, y1, nodes, conc, pot,
+    conc_next, acc, dens, s1, s0, rows, cells,
+    wide,
 ):
+    del acc_in, rows_in, cells_in
     px, py = parity("gx"), parity("gy")
     x_low_first, y_low_first = px == 1, py == 1
-    del acc_in
-    rec[0:GROUP] = rows[...]
-    cell[0:GROUP] = cells[...]
-    total = append(number_in(state[...]), x0, x0[X_NUM:X_POT], 1 - px, nodes, rec, cell)
-    total = append(total, x1, x1[X_NUM:X_POT], px, nodes, rec, cell)
+    before = number_in(state[...])
+    total = append(before, x0, x0[X_NUM:X_POT], 1 - px, nodes, rows, cells)
+    total = append(total, x1, x1[X_NUM:X_POT], px, nodes, rows, cells)
     for g in range(GROUP):
-        rec[total + g] = jnp.zeros((CHANNELS, NODES), F32)
-        cell[total + g] = jnp.zeros((1, NODES), jnp.int32)
-    spread_groups(0, (total + GROUP - 1) // GROUP, rec, cell, acc)
+        rows[total + g] = jnp.zeros((CHANNELS, NODES), F32)
+        cells[total + g] = jnp.zeros((1, NODES), jnp.int32)
+    spread_groups(before // GROUP, (total + GROUP - 1) // GROUP, rows, cells, acc)
 
     for f in range(4):
         wide[f, 1 : BX + 1, 8 : 8 + BY] = conc[f] if f < 3 else pot[...]
@@ -491,7 +482,7 @@
             jax.ShapeDtypeStruct((1, 4, MOVERS, NODES), jnp.int32),
             shape(2, X_POT, NZ), *store(STORE, jax.ShapeDtypeStruct), shape(8, NZ), sums,
         ],
-        [rec, pltpu.VMEM((SLOTS, NODES), jnp.int32), *small, pltpu.SMEM((SLOTS,), jnp.int32), pltpu.SemaphoreType.DMA((12,))],
+        [rec, pltpu.VMEM((SLOTS, NODES), jnp.int32), *small, pltpu.SMEM((SLOTS + 1,), jnp.int32), pltpu.SemaphoreType.DMA((12,))],
     )(*ins, *more, *lists, count)
     y0, y1 = swap(a0, "gy", 0), swap(a1, "gy", 1)
     late, acc = call(
@@ -503,19 +494,18 @@
         arrive_y_kernel,
         "spread_y",
         [VMEM] * 7,
-        [*store(GROUP, jax.ShapeDtypeStruct), shape(8, NZ), sums],
-        store(STORE + 2 * MOVERS + GROUP),
+        [*store(STORE, jax.ShapeDtypeStruct), shape(8, NZ), sums],
         flops=row_flops * 48,
-        aliases={0: 3},
+        aliases={0: 3, 1: 0, 2: 1},
     )(acc, rows, cells, state, y0, y1, arrive_v)
-    conc_near, acc, dens, c1, c0 = call(
+    conc_near, acc, dens, c1, c0, _, _ = call(
         arrive_x_kernel,
         "spread_x",
         [VMEM] * 11,
-        [shape(3, BX, BY, NZ), sums, shape(WIDE, EXT, NZ), shape(DY_END, NZ), shape(DY_END, NZ)],
-        store(2 * MOVERS + 2 * GROUP) + [pltpu.VMEM((4, WIDE, 32, NZ), F32)],
+        [shape(3, BX, BY, NZ), sums, shape(WIDE, EXT, NZ), shape(DY_END, NZ), shape(DY_END, NZ), *store(STORE, jax.ShapeDtypeStruct)],
+        [pltpu.VMEM((4, WIDE, 32, NZ), F32)],
         flops=row_flops * 2 * MOVERS,
-        aliases={0: 1},
+        aliases={0: 1, 1: 5, 2: 6},
     )(acc, rows, cells, state, x1, x0, y0, y1, arrive_v, conc_v, pot_v)
     r0, r1 = swap(c0, "gy", 0), swap(c1, "gy", 1)
     conc_next, force, base, *weights = call(

time: 63.7 us -> 63.2 us (level)
  Pallas kernels: 15.5 us -> 18.8 us
  waiting for transfers between devices: 5.6 us -> 3.37 us
  starting transfers between devices: 36.8 us -> 35.1 us
    ppermute x7, waiting for transfers between devices: 5.6 us -> 3.37 us  [swap(): return lax.ppermute(block, axis, route)]
    pallas_call x1, Pallas kernels: 2.63 us -> 4.76 us  [body(): call(kept_kernel, 'spread_kept', [VMEM] * 4, [shape(8, NZ), sums], flops=...]
    ppermute x7, starting transfers between devices: 36.8 us -> 35.1 us  [swap(): return lax.ppermute(block, axis, route)]
    pallas_call x1, Pallas kernels: 3.39 us -> 4.13 us  [body(): call(arrive_x_kernel, 'spread_x', [VMEM] * 11, [shape(3, BX, BY, NZ), sum...]
  transfers between devices with their start and end apart: 7 -> 7, of which waited for: 2 -> 2; matrix products, arithmetic and copies ran while one was open for 0% -> 0% of each run, Pallas kernels for 13% -> 18%
where the time goes in v9:
time: 63.2 us; the launch traced here: 62.9 us
  starting transfers between devices  35.1 us (56%)
  Pallas kernels  18.8 us (30%)
  blocking collectives  3.98 us (6%)
  waiting for transfers between devices  3.37 us (5%)
  between operations  1.59 us (3%)
    ppermute x7, starting transfers between devices, swap(): return lax.ppermute(block, axis, route)  35.1 us
    pallas_call x1, Pallas kernels, body(): call(kept_kernel, 'spread_kept', [VMEM] * 4, [shape(8, NZ), sums], flops=...  4.76 us
    pallas_call x1, Pallas kernels, body(): call(arrive_x_kernel, 'spread_x', [VMEM] * 11, [shape(3, BX, BY, NZ), sum...  4.13 us
    all_gather x1, blocking collectives, chip_pair(): return lax.all_gather(block, 'gx', axis_index_groups=pairs)  3.98 us
    ppermute x7, waiting for transfers between devices, swap(): return lax.ppermute(block, axis, route)  3.37 us
    pallas_call x1, Pallas kernels, body(): call(arrive_y_kernel, 'spread_y', [VMEM] * 7, [*store(STORE, jax.ShapeDty...  3.17 us
    pallas_call x1, Pallas kernels, body(): call(coefficient_kernel, 'coefficients', [VMEM] * 8, [shape(3, BX, BY, NZ...  2.08 us
    pallas_call x1, Pallas kernels, body(): call(first_kernel, 'first', [HBM] * 8 + [SMEM], [shape(Y_END, 8, NZ), sha...  1.7 us
  transfers between devices with their start and end apart: 7, of which 2 were waited for; matrix products, arithmetic and copies ran while one was open for 0% of the time, Pallas kernels for 18%

profile of v9, /device:TPU:1, one launch (start us, length us, event | category | flops | bytes accessed | tf_op | source)
XLA Modules:
  0.0 62.9 jit_solution(7520856141436974386)
XLA Ops:
  1.3 1.7 %first.1 = (f32[47,8,128]{2,1,0:T(8,128)S(1)}, f32[47,8,128]{2,1,0:T(8,128)S(1)}, f32[3,16,16,128]{3,2,1,0:T(8,128)S(1)}, f32[16,16,128]{2,1,0:T(8,128)S(1)}, f3...) custom-call(f32[3,16,16,128]{3,2,1,0:T(8,128)} %conc_h.1, ...), custom_call_target="tpu_custom_call" | custom-call | bytes 3059712 | tf_op jit(solution)/shard_map/first/pallas_call | solution.py:476
  3.0 5.5 %collective-permute-start = (f32[47,8,128]{2,1,0:T(8,128)S(1)}, f32[47,8,128]{2,1,0:T(8,128)S(1)}, u32[]{:S(2)}, u32[]{:S(2)}) collective-permute-start(f32[47,8,128]{2,1,0:T(8,128)S(1)} %get-tuple-element.50), channel_id=1, source_target_pairs={{0,1},{1,0},{2,3},{3,2},{4,5},{5,4},{6,7},{7,6},{8,9},{9,8},{10,11... | collective-permute-start | bytes 577544 | tf_op jit(solution)/shard_map/ppermute | solution.py:48
  8.5 5.0 %collective-permute-start.1 = (f32[47,8,128]{2,1,0:T(8,128)S(1)}, f32[47,8,128]{2,1,0:T(8,128)S(1)}, u32[]{:S(2)}, u32[]{:S(2)}) collective-permute-start(f32[47,8,128]{2,1,0:T(8,128)S(1)} %get-tuple-element.51), channel_id=1, source_target_pairs={{0,15},{1,2},{2,1},{3,4},{4,3},{5,6},{6,5},{7,8},{8,7},{9,10},{10,... | collective-permute-start | bytes 577544 | tf_op jit(solution)/shard_map/ppermute | solution.py:48
  13.5 4.8 %spread_kept.1 = (f32[8,128]{1,0:T(8,128)S(1)}, f32[2,1296,128]{2,1,0:T(8,128)S(1)}) custom-call(f32[2,1296,128]{2,1,0:T(8,128)S(1)} %get-tuple-element.45.acc_in, f32[208,4,128]{2,1,0:T(4,128)S(1)} %get-tuple-element.46.rows.rows_in, s32[208,1,128]{2,1,0:T(1,128)S(1)} %get-tuple-element.47.cells.cells_in, ...), custom_call_target="tpu_custom_call", output_to_operand_aliasing={{1}: (0, {})} | custom-call | flops 5435817984 | bytes 1331200 | tf_op jit(solution)/shard_map/spread_kept/pallas_call | solution.py:488
  18.3 0.0 collective-permute-done.y0
  18.3 0.3 collective-permute-done.1.y1
  18.6 0.1 pack_x.1
  18.6 6.5 %collective-permute-start.2 = (f32[488,128]{1,0:T(8,128)S(1)}, f32[488,128]{1,0:T(8,128)S(1)}, u32[]{:S(2)}, u32[]{:S(2)}) collective-permute-start(f32[488,128]{1,0:T(8,128)S(1)} %get-tuple-element.61), channel_id=1, source_target_pairs={{0,496},{16,32},{32,16},{48,64},{64,48},{80,96},{96,80},{112,128},... | collective-permute-start | bytes 749576 | tf_op jit(solution)/shard_map/ppermute | solution.py:48
  25.2 7.3 %collective-permute-start.3 = (f32[488,128]{1,0:T(8,128)S(1)}, f32[488,128]{1,0:T(8,128)S(1)}, u32[]{:S(2)}, u32[]{:S(2)}) collective-permute-start(f32[488,128]{1,0:T(8,128)S(1)} %get-tuple-element.62), channel_id=1, source_target_pairs={{0,16},{16,0},{32,48},{48,32},{64,80},{80,64},{96,112},{112,96},{1... | collective-permute-start | bytes 749576 | tf_op jit(solution)/shard_map/ppermute | solution.py:48
  32.4 3.2 %spread_y.1 = (f32[208,4,128]{2,1,0:T(4,128)S(1)}, s32[208,1,128]{2,1,0:T(1,128)S(1)}, f32[8,128]{1,0:T(8,128)S(1)}, f32[2,1296,128]{2,1,0:T(8,128)S(1)}) custom-call(f32[2,1296,128]{2,1,0:T(8,128)S(1)} %get-tuple-element.49.acc_in, f32[208,4,128]{2,1,0:T(4,128)S(1)} %get-tuple-element.46.rows.rows_in, ...), custom_call_target="tpu_custom_call", output_to_operand_aliasing={{3}: (0, {}), {0}: (1, {}), {1}: (2, {})} | custom-call | flops 4076863488 | bytes 1863680 | tf_op jit(solution)/shard_map/spread_y/pallas_call | solution.py:493
  35.6 0.0 collective-permute-done.2.x1
  35.6 0.0 collective-permute-done.3.x0
  35.6 4.1 %spread_x.1 = (f32[3,16,16,128]{3,2,1,0:T(8,128)S(1)}, f32[2,1296,128]{2,1,0:T(8,128)S(1)}, f32[18,32,128]{2,1,0:T(8,128)S(1)}, f32[200,128]{1,0:T(8,128)S(1)}, ...) custom-call(f32[2,1296,128]{2,1,0:T(8,128)S(1)} %get-tuple-element.5, ...), custom_call_target="tpu_custom_call", output_to_operand_aliasing={{1}: (0, {}), {5}: (1, {}), {6}: (2, {})} | custom-call | flops 2717908992 | bytes 2752512 | tf_op jit(solution)/shard_map/spread_x/pallas_call | solution.py:501
  39.8 7.0 %collective-permute-start.4 = (f32[200,128]{1,0:T(8,128)S(1)}, f32[200,128]{1,0:T(8,128)S(1)}, u32[]{:S(2)}, u32[]{:S(2)}) collective-permute-start(f32[200,128]{1,0:T(8,128)S(1)} %get-tuple-element.69), channel_id=1, source_target_pairs={{0,15},{1,2},{2,1},{3,4},{4,3},{5,6},{6,5},{7,8},{8,7},{9,10},{10,... | collective-permute-start | bytes 307208 | tf_op jit(solution)/shard_map/ppermute | solution.py:48
  46.7 1.9 %collective-permute-start.5 = (f32[200,128]{1,0:T(8,128)S(1)}, f32[200,128]{1,0:T(8,128)S(1)}, u32[]{:S(2)}, u32[]{:S(2)}) collective-permute-start(f32[200,128]{1,0:T(8,128)S(1)} %get-tuple-element.70), channel_id=1, source_target_pairs={{0,1},{1,0},{2,3},{3,2},{4,5},{5,4},{6,7},{7,6},{8,9},{9,8},{10,11... | collective-permute-start | bytes 307208 | tf_op jit(solution)/shard_map/ppermute | solution.py:48
  48.7 2.1 %coefficients.1 = (f32[3,16,16,128]{3,2,1,0:T(8,128)}, f32[3,18,16,128]{3,2,1,0:T(8,128)S(1)}, f32[32,32,128]{2,1,0:T(8,128)S(1)}, f32[32,32,128]{2,1,0:T(8,128)...) custom-call(f32[2,1296,128]{2,1,0:T(8,128)S(1)} %get-tuple-element.6, ...), custom_call_target="tpu_custom_call" | custom-call | flops 679477248 | bytes 5029888 | tf_op jit(solution)/shard_map/coefficients/pallas_call | solution.py:511
  50.7 0.0 collective-permute-done.4.r1
  50.8 3.1 %collective-permute-done.5.r0 = f32[200,128]{1,0:T(8,128)S(1)} collective-permute-done((f32[200,128]{1,0:T(8,128)S(1)}, f32[200,128]{1,0:T(8,128)S(1)}, u32[]{:S(2)}, u32[]{:S(2)}) %collective-permute-start.5) | collective-permute-done | bytes 102432 | tf_op jit(solution)/shard_map/ppermute | solution.py:48
  53.8 0.2 join_y.1
  54.0 1.9 %collective-permute-start.6 = (f32[232,128]{1,0:T(8,128)S(1)}, f32[232,128]{1,0:T(8,128)S(1)}, u32[]{:S(2)}, u32[]{:S(2)}) collective-permute-start(f32[232,128]{1,0:T(8,128)S(1)} %get-tuple-element.72), channel_id=1, source_target_pairs={{0,496},{16,32},{32,16},{48,64},{64,48},{80,96},{96,80},{112,128},... | collective-permute-start | bytes 356360 | tf_op jit(solution)/shard_map/ppermute | solution.py:48
  56.0 4.0 %all-gather = f32[464,128]{1,0:T(8,128)S(1)} all-gather(f32[232,128]{1,0:T(8,128)S(1)} %get-tuple-element.73), channel_id=2, replica_groups={{0,16},{32,48},{64,80},{96,112},{128,144},{160,176},{192,208},{224,240}..., dimensions={0}, use_global_device_ids=true | all-gather | bytes 356352 | tf_op jit(solution)/shard_map/all_gather | solution.py:53
  59.9 1.1 %sweeps_near.1 = (f32[8,16,128]{2,1,0:T(8,128)S(1)}, f32[14,32,128]{2,1,0:T(8,128)S(1)}) custom-call(f32[32,32,128]{2,1,0:T(8,128)S(1)} %get-tuple-element.71.dext, f32[2,232,128]{2,1,0:T(8,128)S(1)} %bitcast.1, f32[32,32,128]{2,1,0:T(8,128)S(1)} %get-tuple-element.75.base, f32[32,32,128]{2,1,0:T(8,128)S(1)} %get-tuple-element.76.xp, ...), custom_call_target="tpu_custom_call" | custom-call | flops 12582912 | bytes 294912 | tf_op jit(solution)/shard_map/sweeps_near/pallas_call | solution.py:525
  61.1 0.0 collective-permute-done.6.r1
  61.1 1.6 %sweeps_far.1 = (f32[16,16,128]{2,1,0:T(8,128)}, f32[3,16,16,128]{3,2,1,0:T(8,128)}) custom-call(f32[32,32,128]{2,1,0:T(8,128)S(1)} %get-tuple-element.71.dext, f32[232,128]{1,0:T(8,128)S(1)} %collective-permute-done.6.r1, f32[2,232,128]{2,1,0:T(8,128)S(1)} %bitcast.2, f32[3,18,16,128]{3,2,1,0:T(8,128)S(1)} %get-tuple-element.74.fcore, ...), custom_call_target="tpu_custom_call" | custom-call | flops 8388608 | bytes 524288 | tf_op jit(solution)/shard_map/sweeps_far/pallas_call | solution.py:533
Async XLA Ops:
  3.0 15.3 %collective-permute-start = (f32[47,8,128]{2,1,0:T(8,128)S(1)}, f32[47,8,128]{2,1,0:T(8,128)S(1)}, u32[]{:S(2)}, u32[]{:S(2)}) collective-permute-start(f32[47,8,128]{2,1,0:T(8,128)S(1)} %get-tuple-element.50), channel_id=1, source_target_pairs={{0,1},{1,0},{2,3},{3,2},{4,5},{5,4},{6,7},{7,6},{8,9},{9,8},{10,11... | collective-permute-start | bytes 577544 | tf_op jit(solution)/shard_map/ppermute | solution.py:48
  8.5 10.1 %collective-permute-start.1 = (f32[47,8,128]{2,1,0:T(8,128)S(1)}, f32[47,8,128]{2,1,0:T(8,128)S(1)}, u32[]{:S(2)}, u32[]{:S(2)}) collective-permute-start(f32[47,8,128]{2,1,0:T(8,128)S(1)} %get-tuple-element.51), channel_id=1, source_target_pairs={{0,15},{1,2},{2,1},{3,4},{4,3},{5,6},{6,5},{7,8},{8,7},{9,10},{10,... | collective-permute-start | bytes 577544 | tf_op jit(solution)/shard_map/ppermute | solution.py:48
  18.6 17.0 %collective-permute-start.2 = (f32[488,128]{1,0:T(8,128)S(1)}, f32[488,128]{1,0:T(8,128)S(1)}, u32[]{:S(2)}, u32[]{:S(2)}) collective-permute-start(f32[488,128]{1,0:T(8,128)S(1)} %get-tuple-element.61), channel_id=1, source_target_pairs={{0,496},{16,32},{32,16},{48,64},{64,48},{80,96},{96,80},{112,128},... | collective-permute-start | bytes 749576 | tf_op jit(solution)/shard_map/ppermute | solution.py:48
  25.2 10.4 %collective-permute-start.3 = (f32[488,128]{1,0:T(8,128)S(1)}, f32[488,128]{1,0:T(8,128)S(1)}, u32[]{:S(2)}, u32[]{:S(2)}) collective-permute-start(f32[488,128]{1,0:T(8,128)S(1)} %get-tuple-element.62), channel_id=1, source_target_pairs={{0,16},{16,0},{32,48},{48,32},{64,80},{80,64},{96,112},{112,96},{1... | collective-permute-start | bytes 749576 | tf_op jit(solution)/shard_map/ppermute | solution.py:48
  39.8 11.0 %collective-permute-start.4 = (f32[200,128]{1,0:T(8,128)S(1)}, f32[200,128]{1,0:T(8,128)S(1)}, u32[]{:S(2)}, u32[]{:S(2)}) collective-permute-start(f32[200,128]{1,0:T(8,128)S(1)} %get-tuple-element.69), channel_id=1, source_target_pairs={{0,15},{1,2},{2,1},{3,4},{4,3},{5,6},{6,5},{7,8},{8,7},{9,10},{10,... | collective-permute-start | bytes 307208 | tf_op jit(solution)/shard_map/ppermute | solution.py:48
  46.7 7.1 %collective-permute-start.5 = (f32[200,128]{1,0:T(8,128)S(1)}, f32[200,128]{1,0:T(8,128)S(1)}, u32[]{:S(2)}, u32[]{:S(2)}) collective-permute-start(f32[200,128]{1,0:T(8,128)S(1)} %get-tuple-element.70), channel_id=1, source_target_pairs={{0,1},{1,0},{2,3},{3,2},{4,5},{5,4},{6,7},{7,6},{8,9},{9,8},{10,11... | collective-permute-start | bytes 307208 | tf_op jit(solution)/shard_map/ppermute | solution.py:48
  54.0 7.1 %collective-permute-start.6 = (f32[232,128]{1,0:T(8,128)S(1)}, f32[232,128]{1,0:T(8,128)S(1)}, u32[]{:S(2)}, u32[]{:S(2)}) collective-permute-start(f32[232,128]{1,0:T(8,128)S(1)} %get-tuple-element.72), channel_id=1, source_target_pairs={{0,496},{16,32},{32,16},{48,64},{64,48},{80,96},{96,80},{112,128},... | collective-permute-start | bytes 356360 | tf_op jit(solution)/shard_map/ppermute | solution.py:48
